TPU v7x, 32 devices: a whole 2x2x4 slice. The times are simulated.
32 devices in a mesh: dp: 4 (over y, core), ctx: 8 (over z, x).
Axes of the slice: x: 2, y: 2, z: 4, core: 2. Of those that a mesh axis runs over, the one named last changes fastest.
Arguments:
- tokens: bfloat16 [4, 1024, 1024], P('dp', 'ctx'), may hold values from -6 to 6
- out_cotangent: bfloat16 [4, 1024, 1024], P('dp', 'ctx'), may hold values from -6 to 6
- input_gain: bfloat16 [1024], P(('dp', 'ctx')), may hold values from 0.5 to 1.5
- mamba_gate_weight: bfloat16 [1024, 1536], P(('dp', 'ctx')), may hold values from -0.1875 to 0.1875
- mamba_mix_weight: bfloat16 [1024, 1792], P(('dp', 'ctx')), may hold values from -0.1875 to 0.1875
- mamba_step_weight: bfloat16 [1024, 24], P(('dp', 'ctx')), may hold values from -0.1875 to 0.1875
- conv_kernel: bfloat16 [4, 1792], P(None, ('dp', 'ctx')), may hold values from -3 to 3
- conv_offset: bfloat16 [1792], P(('dp', 'ctx')), may hold values from -3 to 3
- step_offset: float32 [24], replicated, may hold values from -5 to -3
- decay_log: float32 [24], replicated, may hold values from -6 to 0
- skip_scale: float32 [24], replicated, may hold values from 0.5 to 1.5
- mamba_norm_gain: bfloat16 [1536], P(('dp', 'ctx')), may hold values from 0.5 to 1.5
- mamba_out_weight: bfloat16 [1536, 1024], P(None, ('dp', 'ctx')), may hold values from -0.15625 to 0.15625
- query_weight: bfloat16 [1024, 512], P(('dp', 'ctx')), may hold values from -0.1875 to 0.1875
- key_weight: bfloat16 [1024, 128], P(('dp', 'ctx')), may hold values from -0.1875 to 0.1875
- value_weight: bfloat16 [1024, 128], P(('dp', 'ctx')), may hold values from -0.1875 to 0.1875
- attention_out_weight: bfloat16 [512, 1024], P(None, ('dp', 'ctx')), may hold values from -6 to 6
- ffn_gain: bfloat16 [1024], P(('dp', 'ctx')), may hold values from 0.5 to 1.5
- feed_gate_weight: bfloat16 [1024, 2048], P(('dp', 'ctx')), may hold values from -0.1875 to 0.1875
- feed_up_weight: bfloat16 [1024, 2048], P(('dp', 'ctx')), may hold values from -0.1875 to 0.1875
- feed_down_weight: bfloat16 [2048, 1024], P(None, ('dp', 'ctx')), may hold values from -0.125 to 0.125
Outputs:
- layer_out: bfloat16 [4, 1024, 1024], P('dp', 'ctx')
- input_gradient: float32 [4, 1024, 1024], P('dp', 'ctx')
- input_gain_gradient: float32 [1024], P(('dp', 'ctx'))
- mamba_gate_gradient: float32 [1024, 1536], P(('dp', 'ctx'))
- mamba_mix_gradient: float32 [1024, 1792], P(('dp', 'ctx'))
- mamba_step_gradient: float32 [1024, 24], P(('dp', 'ctx'))
- conv_kernel_gradient: float32 [4, 1792], P(None, ('dp', 'ctx'))
- conv_offset_gradient: float32 [1792], P(('dp', 'ctx'))
- step_offset_gradient: float32 [24], replicated
- decay_log_gradient: float32 [24], replicated
- skip_scale_gradient: float32 [24], replicated
- mamba_norm_gain_gradient: float32 [1536], P(('dp', 'ctx'))
- mamba_out_gradient: float32 [1536, 1024], P(None, ('dp', 'ctx'))
- query_gradient: float32 [1024, 512], P(('dp', 'ctx'))
- key_gradient: float32 [1024, 128], P(('dp', 'ctx'))
- value_gradient: float32 [1024, 128], P(('dp', 'ctx'))
- attention_out_gradient: float32 [512, 1024], P(None, ('dp', 'ctx'))
- ffn_gain_gradient: float32 [1024], P(('dp', 'ctx'))
- feed_gate_gradient: float32 [1024, 2048], P(('dp', 'ctx'))
- feed_up_gradient: float32 [1024, 2048], P(('dp', 'ctx'))
- feed_down_gradient: float32 [2048, 1024], P(None, ('dp', 'ctx'))
All inputs are finite; a program needn't handle non-finite values.
Results may differ from a plain program's by a relative error of at most 0.015.
Values may be sent and summed in bfloat16 or wider, within the bound.
No kernel may reach another device: no remote copies, remote signals or barrier semaphores. Data moves between devices by JAX's collectives and lax.ppermute only.
A program may use at most 256 MiB of HBM per device.

v0:
```python
import math

import jax
import jax.numpy as jnp
from jax import lax
from jax.sharding import PartitionSpec as P

DSSM = 1536
MP = 64
NS = 128
KW = 4
AH = 8
KVH = 2
HD = 64


EPSILON = 1e-05
ROPE_BASE = 100000000000.0
HIGHEST = lax.Precision.HIGHEST
NEGATIVE = -1e30


def shifted(shard, axis, by):
    devices = lax.axis_size(axis)
    pairs = [(i, i + by) for i in range(devices) if 0 <= i + by < devices]
    return lax.ppermute(shard, axis, pairs)


def carried_in(shard, axis, combine, identity):
    devices, index = (lax.axis_size(axis), lax.axis_index(axis))
    everything = jax.tree.map(
        lambda part, kind: lax.all_gather(part.astype(kind), axis),
        shard,
        (jnp.bfloat16, jnp.bfloat16),
    )
    start = jax.tree.map(
        lambda part, zero: jnp.broadcast_to(jnp.asarray(zero, part.dtype), part.shape),
        shard,
        identity,
    )

    def step(k, before):
        reached = k < index
        new = combine(
            before, jax.tree.map(lambda part, own: part[k].astype(own.dtype), everything, shard)
        )
        return jax.tree.map(lambda a, b: jnp.where(reached, a, b), new, before)

    return lax.fori_loop(0, devices, step, start)


def entering(shard, axis, combine, identity):
    devices, index = (lax.axis_size(axis), lax.axis_index(axis))
    everything = jax.tree.map(
        lambda part, kind: lax.all_gather(part.astype(kind), axis),
        shard,
        jax.tree.map(lambda a: jnp.bfloat16 if a.dtype == jnp.float32 else a.dtype, shard),
    )
    start = jax.tree.map(
        lambda part, zero: jnp.broadcast_to(jnp.asarray(zero, part.dtype), part.shape),
        shard,
        identity,
    )

    def step(k, before):
        at = devices - 1 - k
        reached = at > index
        new = combine(
            before, jax.tree.map(lambda part, own: part[at].astype(own.dtype), everything, shard)
        )
        return jax.tree.map(lambda a, b: jnp.where(reached, a, b), new, before)

    return lax.fori_loop(0, devices, step, start)


def forward_product(left, right):
    return jnp.dot(left, right, preferred_element_type=jnp.float32)


def weight_product(left, right):
    return lax.dot_general(
        left, right, (((0,), (0,)), ((), ())), preferred_element_type=jnp.float32
    )


def input_product(upstream, weight):
    return lax.dot_general(
        upstream, weight, (((1,), (1,)), ((), ())), preferred_element_type=jnp.float32
    )


def rms_forward(values, gain):
    scale = lax.rsqrt(jnp.mean(values * values, -1, keepdims=True) + EPSILON)
    return (values * scale * gain, scale)


def rms_backward(values, scale, gain, upstream):
    weighted = upstream * gain
    gain_part = jnp.sum(upstream * values * scale, 0)
    result = scale * weighted - values * scale**3 * jnp.mean(weighted * values, -1, keepdims=True)
    return (result, gain_part)


def rope_tables(positions):
    ladder = jnp.arange(HD // 2, dtype=jnp.float32)
    rates = ROPE_BASE ** (-2.0 * ladder / HD)
    angles = positions.astype(jnp.float32)[:, None] * rates[None, :]
    return (jnp.cos(angles), jnp.sin(angles))


def rotate(values, cosine, sine):
    half = values.shape[-1] // 2
    first = values[..., :half]
    second = values[..., half:]
    cosine = cosine[:, None, :]
    sine = sine[:, None, :]
    return jnp.concatenate([first * cosine - second * sine, second * cosine + first * sine], -1)


def mamba_prep(extended, step_rows, kernel, offset, step_offset, decay_log):
    rows = step_rows.shape[0]
    conv = offset[None, :] + kernel[0][None, :] * extended[0:rows]
    for tap in range(1, kernel.shape[0]):
        conv = conv + kernel[tap][None, :] * extended[tap : tap + rows]
    steps = jax.nn.softplus(step_rows + step_offset[None, :])
    curve = jnp.cumsum(-jnp.exp(decay_log)[None, :] * steps, axis=0)
    return (jax.nn.silu(conv), steps, curve)


def mamba_state(conv, steps, curve):
    rows, heads = steps.shape
    signal = conv[:, :DSSM].reshape(rows, heads, MP)
    entry = conv[:, DSSM : DSSM + NS]
    weights = jnp.exp(curve[-1][None, :] - curve) * steps
    state = jnp.einsum("th,thp,tn->hpn", weights, signal, entry, precision=HIGHEST)
    return (jnp.exp(curve[-1]), state)


def mamba_out(conv, steps, curve, gate_rows, skip_scale, norm_gain, state_in):
    rows, heads = steps.shape
    signal = conv[:, :DSSM].reshape(rows, heads, MP)
    entry = conv[:, DSSM : DSSM + NS]
    readout = conv[:, DSSM + NS :]
    causal = jnp.arange(rows)[:, None] >= jnp.arange(rows)[None, :]
    spread = curve.T[:, :, None] - curve.T[:, None, :]
    mixing = jnp.where(causal[None], jnp.exp(jnp.where(causal[None], spread, 0.0)), 0.0)
    intersection = jnp.dot(readout, entry.T, precision=HIGHEST)
    mixing = mixing * intersection[None] * steps.T[:, None, :]
    local_part = jnp.einsum("hts,shp->thp", mixing, signal, precision=HIGHEST)
    carried = (
        jnp.einsum("tn,hpn->thp", readout, state_in, precision=HIGHEST) * jnp.exp(curve)[:, :, None]
    )
    mixed = (local_part + carried + skip_scale[None, :, None] * signal).reshape(rows, DSSM)
    gated = mixed * jax.nn.silu(gate_rows)
    return gated * lax.rsqrt(jnp.mean(gated * gated, -1, keepdims=True) + EPSILON) * norm_gain


def combine_states(earlier, later):
    return (earlier[0] * later[0], later[0][:, None, None] * earlier[1] + later[1])


def widen_mixer(mixer):
    (
        gain,
        gate,
        mix,
        step,
        kernel,
        offset,
        mamba_gain,
        mamba_out_w,
        query_w,
        key_w,
        value_w,
        attention_w,
    ) = mixer
    return (
        gain.astype(jnp.float32),
        gate,
        mix,
        step,
        kernel.astype(jnp.float32),
        offset.astype(jnp.float32),
        mamba_gain.astype(jnp.float32),
        mamba_out_w,
        query_w,
        key_w,
        value_w,
        attention_w,
    )


def widen_feed(feed):
    return (feed[0].astype(jnp.float32), feed[1], feed[2], feed[3])


def flash_forward(grouped, query_index, gathered):
    heads, count, width = grouped.shape
    length = gathered.shape[0]
    block = math.gcd(length, 512)
    blocks = gathered.reshape(length // block, block, 2, heads, width)
    starts = jnp.arange(length // block, dtype=jnp.int32) * block
    scale = width ** (-0.5)

    def one_block(carry, inputs):
        peak, total, summed = carry
        piece, start = inputs
        key_index = start + jnp.arange(block, dtype=jnp.int32)
        visible = key_index[None, None, :] <= query_index[None, :, None]
        scores = (
            jnp.einsum("gqd,kgd->gqk", grouped, piece[:, 0], preferred_element_type=jnp.float32)
            * scale
        )
        new_peak = jnp.maximum(peak, jnp.max(jnp.where(visible, scores, NEGATIVE), -1))
        weights = jnp.where(visible, jnp.exp(scores - new_peak[:, :, None]), 0.0)
        factor = jnp.exp(peak - new_peak)
        total = total * factor + jnp.sum(weights, -1)
        summed = summed * factor[:, :, None] + jnp.einsum(
            "gqk,kgd->gqd",
            weights.astype(jnp.bfloat16),
            piece[:, 1],
            preferred_element_type=jnp.float32,
        )
        return ((new_peak, total, summed), None)

    start_carry = (
        jnp.full((heads, count), NEGATIVE, jnp.float32),
        jnp.zeros((heads, count), jnp.float32),
        jnp.zeros((heads, count, width), jnp.float32),
    )
    (peak, total, summed), unused = lax.scan(one_block, start_carry, (blocks, starts))
    return (summed / total[:, :, None], peak + jnp.log(total))


def flash_backward(grouped, query_index, gathered, grouped_back, log_total, delta):
    heads, count, width = grouped.shape
    length = gathered.shape[0]
    block = math.gcd(length, 512)
    blocks = gathered.reshape(length // block, block, 2, heads, width)
    starts = jnp.arange(length // block, dtype=jnp.int32) * block
    scale = width ** (-0.5)

    def one_block(back_query, inputs):
        piece, start = inputs
        key_index = start + jnp.arange(block, dtype=jnp.int32)
        visible = key_index[None, None, :] <= query_index[None, :, None]
        scores = (
            jnp.einsum("gqd,kgd->gqk", grouped, piece[:, 0], preferred_element_type=jnp.float32)
            * scale
        )
        chance = jnp.where(visible, jnp.exp(scores - log_total[:, :, None]), 0.0)
        back_values = jnp.einsum(
            "gqk,gqd->kgd",
            chance.astype(jnp.bfloat16),
            grouped_back,
            preferred_element_type=jnp.float32,
        )
        back_chance = jnp.einsum(
            "gqd,kgd->gqk", grouped_back, piece[:, 1], preferred_element_type=jnp.float32
        )
        back_scores = (chance * (back_chance - delta[:, :, None]) * scale).astype(jnp.bfloat16)
        back_query = back_query + jnp.einsum(
            "gqk,kgd->gqd", back_scores, piece[:, 0], preferred_element_type=jnp.float32
        )
        back_keys = jnp.einsum(
            "gqk,gqd->kgd", back_scores, grouped, preferred_element_type=jnp.float32
        )
        return (
            back_query,
            jnp.concatenate(
                [
                    back_keys.reshape(block, heads * width),
                    back_values.reshape(block, heads * width),
                ],
                1,
            ),
        )

    back_query, pieces = lax.scan(
        one_block, jnp.zeros((heads, count, width), jnp.float32), (blocks, starts)
    )
    return (back_query, pieces.reshape(length, 2 * heads * width))


def local(
    tokens,
    out_cotangent,
    input_gain,
    mamba_gate_weight,
    mamba_mix_weight,
    mamba_step_weight,
    conv_kernel,
    conv_offset,
    step_offset,
    decay_log,
    skip_scale,
    mamba_norm_gain,
    mamba_out_weight,
    query_weight,
    key_weight,
    value_weight,
    attention_out_weight,
    ffn_gain,
    feed_gate_weight,
    feed_up_weight,
    feed_down_weight,
):
    rows = tokens.shape[1]
    group = AH // KVH
    hidden_in = tokens[0].astype(jnp.float32)
    mixer = (
        lax.all_gather(input_gain, ("dp", "ctx"), axis=0, tiled=True),
        lax.all_gather(mamba_gate_weight, ("dp", "ctx"), axis=0, tiled=True),
        lax.all_gather(mamba_mix_weight, ("dp", "ctx"), axis=0, tiled=True),
        lax.all_gather(mamba_step_weight, ("dp", "ctx"), axis=0, tiled=True),
        lax.all_gather(conv_kernel, ("dp", "ctx"), axis=1, tiled=True),
        lax.all_gather(conv_offset, ("dp", "ctx"), axis=0, tiled=True),
        lax.all_gather(mamba_norm_gain, ("dp", "ctx"), axis=0, tiled=True),
        lax.all_gather(mamba_out_weight, ("dp", "ctx"), axis=1, tiled=True),
        lax.all_gather(query_weight, ("dp", "ctx"), axis=0, tiled=True),
        lax.all_gather(key_weight, ("dp", "ctx"), axis=0, tiled=True),
        lax.all_gather(value_weight, ("dp", "ctx"), axis=0, tiled=True),
        lax.all_gather(attention_out_weight, ("dp", "ctx"), axis=1, tiled=True),
    )
    (
        full_gain,
        full_gate,
        full_mix,
        full_step,
        full_kernel,
        full_offset,
        full_mamba_gain,
        full_mamba_out,
        full_query,
        full_key,
        full_value,
        full_attention_out,
    ) = widen_mixer(mixer)
    normed, scale_one = rms_forward(hidden_in, full_gain)
    low_normed = normed.astype(jnp.bfloat16)
    gate_rows = forward_product(low_normed, full_gate)
    mix_rows = forward_product(low_normed, full_mix).astype(jnp.bfloat16)
    step_rows = forward_product(low_normed, full_step)
    rim = shifted(mix_rows[rows - (KW - 1) :], "ctx", 1)
    extended = lax.optimization_barrier(jnp.concatenate([rim, mix_rows], 0)).astype(jnp.float32)
    (conv, steps, curve), prep_pull = jax.vjp(
        mamba_prep, extended, step_rows, full_kernel, full_offset, step_offset, decay_log
    )
    (total, local_state), state_pull = jax.vjp(mamba_state, conv, steps, curve)
    carried, state_in = carried_in(
        (total, local_state),
        "ctx",
        combine_states,
        (jnp.ones_like(total), jnp.zeros_like(local_state)),
    )
    mamba_result, out_pull = jax.vjp(
        mamba_out, conv, steps, curve, gate_rows, skip_scale, full_mamba_gain, state_in
    )
    mamba_rows = mamba_result.astype(jnp.bfloat16)
    mamba_branch = forward_product(mamba_rows, full_mamba_out)
    positions = lax.axis_index("ctx") * rows + jnp.arange(rows, dtype=jnp.int32)
    cosine, sine = rope_tables(positions)
    query = rotate(
        forward_product(low_normed, full_query).reshape(rows, AH, HD), cosine, sine
    ).astype(jnp.bfloat16)
    keys = rotate(forward_product(low_normed, full_key).reshape(rows, KVH, HD), cosine, sine)
    values = forward_product(low_normed, full_value)
    key_value = jnp.concatenate([keys.reshape(rows, KVH * HD), values], 1).astype(jnp.bfloat16)
    gathered = lax.all_gather(key_value, "ctx", axis=0, tiled=True)
    grouped = (
        query.reshape(rows, KVH, group, HD).transpose(1, 2, 0, 3).reshape(KVH, group * rows, HD)
    )
    query_index = jnp.tile(positions, group)
    attention_rows, log_total = flash_forward(grouped, query_index, gathered)
    attended = (
        attention_rows.reshape(KVH, group, rows, HD)
        .transpose(2, 0, 1, 3)
        .reshape(rows, AH * HD)
        .astype(jnp.bfloat16)
    )
    attention_branch = forward_product(attended, full_attention_out)
    middle = hidden_in + mamba_branch + attention_branch
    feed = (
        lax.all_gather(ffn_gain, ("dp", "ctx"), axis=0, tiled=True),
        lax.all_gather(feed_gate_weight, ("dp", "ctx"), axis=0, tiled=True),
        lax.all_gather(feed_up_weight, ("dp", "ctx"), axis=0, tiled=True),
        lax.all_gather(feed_down_weight, ("dp", "ctx"), axis=1, tiled=True),
    )
    full_gain_two, full_feed_gate, full_feed_up, full_feed_down = widen_feed(feed)
    normed_two, scale_two = rms_forward(middle, full_gain_two)
    low_two = normed_two.astype(jnp.bfloat16)
    gate_pre = forward_product(low_two, full_feed_gate)
    up_pre = forward_product(low_two, full_feed_up)
    activation = (jax.nn.silu(gate_pre) * up_pre).astype(jnp.bfloat16)
    layer_out = (middle + forward_product(activation, full_feed_down)).astype(jnp.bfloat16)
    upstream = out_cotangent[0]
    feed = (
        lax.all_gather(ffn_gain, ("dp", "ctx"), axis=0, tiled=True),
        lax.all_gather(feed_gate_weight, ("dp", "ctx"), axis=0, tiled=True),
        lax.all_gather(feed_up_weight, ("dp", "ctx"), axis=0, tiled=True),
        lax.all_gather(feed_down_weight, ("dp", "ctx"), axis=1, tiled=True),
    )
    full_gain_two, full_feed_gate, full_feed_up, full_feed_down = widen_feed(feed)
    gradient_down = weight_product(activation, upstream)
    back_activation = input_product(upstream, full_feed_down)
    sigmoid = jax.nn.sigmoid(gate_pre)
    back_gate = (back_activation * up_pre * sigmoid * (1.0 + gate_pre * (1.0 - sigmoid))).astype(
        jnp.bfloat16
    )
    back_up = (back_activation * jax.nn.silu(gate_pre)).astype(jnp.bfloat16)
    gradient_feed_gate = weight_product(low_two, back_gate)
    gradient_feed_up = weight_product(low_two, back_up)
    back_normed_two = input_product(back_gate, full_feed_gate) + input_product(
        back_up, full_feed_up
    )
    back_middle, gradient_gain_two = rms_backward(middle, scale_two, full_gain_two, back_normed_two)
    back_middle = back_middle + upstream.astype(jnp.float32)
    feed_grads = (
        lax.psum_scatter(gradient_gain_two, ("dp", "ctx"), scatter_dimension=0, tiled=True),
        lax.psum_scatter(gradient_feed_gate, ("dp", "ctx"), scatter_dimension=0, tiled=True),
        lax.psum_scatter(gradient_feed_up, ("dp", "ctx"), scatter_dimension=0, tiled=True),
        lax.psum_scatter(gradient_down, ("dp", "ctx"), scatter_dimension=1, tiled=True),
    )
    mixer = (
        lax.all_gather(input_gain, ("dp", "ctx"), axis=0, tiled=True),
        lax.all_gather(mamba_gate_weight, ("dp", "ctx"), axis=0, tiled=True),
        lax.all_gather(mamba_mix_weight, ("dp", "ctx"), axis=0, tiled=True),
        lax.all_gather(mamba_step_weight, ("dp", "ctx"), axis=0, tiled=True),
        lax.all_gather(conv_kernel, ("dp", "ctx"), axis=1, tiled=True),
        lax.all_gather(conv_offset, ("dp", "ctx"), axis=0, tiled=True),
        lax.all_gather(mamba_norm_gain, ("dp", "ctx"), axis=0, tiled=True),
        lax.all_gather(mamba_out_weight, ("dp", "ctx"), axis=1, tiled=True),
        lax.all_gather(query_weight, ("dp", "ctx"), axis=0, tiled=True),
        lax.all_gather(key_weight, ("dp", "ctx"), axis=0, tiled=True),
        lax.all_gather(value_weight, ("dp", "ctx"), axis=0, tiled=True),
        lax.all_gather(attention_out_weight, ("dp", "ctx"), axis=1, tiled=True),
    )
    (
        full_gain,
        full_gate,
        full_mix,
        full_step,
        full_kernel,
        full_offset,
        full_mamba_gain,
        full_mamba_out,
        full_query,
        full_key,
        full_value,
        full_attention_out,
    ) = widen_mixer(mixer)
    low_middle = back_middle.astype(jnp.bfloat16)
    gradient_mamba_out = weight_product(mamba_rows, low_middle)
    back_mamba_rows = input_product(low_middle, full_mamba_out)
    gradient_attention_out = weight_product(attended, low_middle)
    back_attended = input_product(low_middle, full_attention_out).astype(jnp.bfloat16)
    grouped_back = (
        back_attended.reshape(rows, KVH, group, HD)
        .transpose(1, 2, 0, 3)
        .reshape(KVH, group * rows, HD)
    )
    grouped_out = (
        attended.reshape(rows, KVH, group, HD).transpose(1, 2, 0, 3).reshape(KVH, group * rows, HD)
    )
    delta = jnp.einsum("gqd,gqd->gq", grouped_back, grouped_out, preferred_element_type=jnp.float32)
    back_grouped, back_key_value_full = flash_backward(
        grouped, query_index, gathered, grouped_back, log_total, delta
    )
    back_key_value = lax.psum_scatter(
        back_key_value_full.astype(jnp.bfloat16), "ctx", scatter_dimension=0, tiled=True
    ).astype(jnp.float32)
    back_query = back_grouped.reshape(KVH, group, rows, HD).transpose(2, 0, 1, 3)
    back_query = (
        rotate(back_query.reshape(rows, AH, HD), cosine, -sine)
        .reshape(rows, AH * HD)
        .astype(jnp.bfloat16)
    )
    back_keys = (
        rotate(back_key_value[:, : KVH * HD].reshape(rows, KVH, HD), cosine, -sine)
        .reshape(rows, KVH * HD)
        .astype(jnp.bfloat16)
    )
    back_values = back_key_value[:, KVH * HD :].astype(jnp.bfloat16)
    out_grads = out_pull(back_mamba_rows)
    unused, next_back = entering(
        (total, out_grads[6]),
        "ctx",
        combine_states,
        (jnp.ones_like(total), jnp.zeros_like(local_state)),
    )
    total_back = jnp.sum(next_back * state_in, axis=(1, 2))
    state_grads = state_pull((total_back, next_back))
    prep_grads = prep_pull(
        (
            out_grads[0] + state_grads[0],
            out_grads[1] + state_grads[1],
            out_grads[2] + state_grads[2],
        )
    )
    back_extended = prep_grads[0]
    returned = shifted(back_extended[: KW - 1], "ctx", -1)
    back_mix = back_extended[KW - 1 :]
    back_mix = jnp.concatenate(
        [back_mix[: rows - (KW - 1)], back_mix[rows - (KW - 1) :] + returned], 0
    )
    low_mix = back_mix.astype(jnp.bfloat16)
    low_step = prep_grads[1].astype(jnp.bfloat16)
    low_gate = out_grads[3].astype(jnp.bfloat16)
    back_normed = (
        input_product(low_gate, full_gate)
        + input_product(low_mix, full_mix)
        + input_product(low_step, full_step)
    )
    back_normed = (
        back_normed
        + input_product(back_query, full_query)
        + input_product(back_keys, full_key)
        + input_product(back_values, full_value)
    )
    back_hidden, gradient_gain_one = rms_backward(hidden_in, scale_one, full_gain, back_normed)
    input_gradient = back_hidden + back_middle
    mixer_grads = (
        lax.psum_scatter(gradient_gain_one, ("dp", "ctx"), scatter_dimension=0, tiled=True),
        lax.psum_scatter(
            weight_product(low_normed, low_gate), ("dp", "ctx"), scatter_dimension=0, tiled=True
        ),
        lax.psum_scatter(
            weight_product(low_normed, low_mix), ("dp", "ctx"), scatter_dimension=0, tiled=True
        ),
        lax.psum_scatter(
            weight_product(low_normed, low_step), ("dp", "ctx"), scatter_dimension=0, tiled=True
        ),
        lax.psum_scatter(prep_grads[2], ("dp", "ctx"), scatter_dimension=1, tiled=True),
        lax.psum_scatter(prep_grads[3], ("dp", "ctx"), scatter_dimension=0, tiled=True),
        lax.psum_scatter(out_grads[5], ("dp", "ctx"), scatter_dimension=0, tiled=True),
        lax.psum_scatter(gradient_mamba_out, ("dp", "ctx"), scatter_dimension=1, tiled=True),
        lax.psum_scatter(
            weight_product(low_normed, back_query), ("dp", "ctx"), scatter_dimension=0, tiled=True
        ),
        lax.psum_scatter(
            weight_product(low_normed, back_keys), ("dp", "ctx"), scatter_dimension=0, tiled=True
        ),
        lax.psum_scatter(
            weight_product(low_normed, back_values), ("dp", "ctx"), scatter_dimension=0, tiled=True
        ),
        lax.psum_scatter(gradient_attention_out, ("dp", "ctx"), scatter_dimension=1, tiled=True),
    )
    head_grads = lax.psum((prep_grads[4], prep_grads[5], out_grads[4]), ("dp", "ctx"))
    return (
        layer_out[None],
        input_gradient[None],
        mixer_grads[0],
        mixer_grads[1],
        mixer_grads[2],
        mixer_grads[3],
        mixer_grads[4],
        mixer_grads[5],
        head_grads[0],
        head_grads[1],
        head_grads[2],
        mixer_grads[6],
        mixer_grads[7],
        mixer_grads[8],
        mixer_grads[9],
        mixer_grads[10],
        mixer_grads[11],
        feed_grads[0],
        feed_grads[1],
        feed_grads[2],
        feed_grads[3],
    )


def solution(mesh):
    return jax.shard_map(
        local,
        mesh=mesh,
        in_specs=(
            P("dp", "ctx", None),
            P("dp", "ctx", None),
            P(("dp", "ctx")),
            P(("dp", "ctx"), None),
            P(("dp", "ctx"), None),
            P(("dp", "ctx"), None),
            P(None, ("dp", "ctx")),
            P(("dp", "ctx")),
            P(),
            P(),
            P(),
            P(("dp", "ctx")),
            P(None, ("dp", "ctx")),
            P(("dp", "ctx"), None),
            P(("dp", "ctx"), None),
            P(("dp", "ctx"), None),
            P(None, ("dp", "ctx")),
            P(("dp", "ctx")),
            P(("dp", "ctx"), None),
            P(("dp", "ctx"), None),
            P(None, ("dp", "ctx")),
        ),
        out_specs=(
            P("dp", "ctx", None),
            P("dp", "ctx", None),
            P(("dp", "ctx")),
            P(("dp", "ctx"), None),
            P(("dp", "ctx"), None),
            P(("dp", "ctx"), None),
            P(None, ("dp", "ctx")),
            P(("dp", "ctx")),
            P(),
            P(),
            P(),
            P(("dp", "ctx")),
            P(None, ("dp", "ctx")),
            P(("dp", "ctx"), None),
            P(("dp", "ctx"), None),
            P(("dp", "ctx"), None),
            P(None, ("dp", "ctx")),
            P(("dp", "ctx")),
            P(("dp", "ctx"), None),
            P(("dp", "ctx"), None),
            P(None, ("dp", "ctx")),
        ),
        check_vma=False,
    )
```

profile of v0, /device:TPU:0, one launch (start us, length us, event | category | flops | bytes accessed | tf_op | source)
XLA Modules:
  0.0 2457.6 jit_solution(12458854291203329776)
XLA Ops:
  12.1 42.2 %all-reduce.25 = (bf16[1024]{0:T(1024)(128)(2,1)S(1)}, bf16[1792]{0:T(1024)(128)(2,1)S(1)}, bf16[1536]{0:T(1024)(128)(2,1)}, bf16[1024]{0:T(1024)(128)(2,1)}) all-reduce(bf16[1024]{0:T(1024)(128)(2,1)S(1)} %dynamic-update-slice.1, bf16[1792]{0:T(1024)(128)(2,1)S(1)} %dynamic-update-slice, ...), channel_id=1, replica_groups=mesh['dp'=4,'ctx'=8] {'dp','ctx'}, use_global_device_ids=true, to_apply=%add.16 | all-reduce | flops 5376 | bytes 21504
  55.9 67.9 %all-gather.3 = bf16[32,32,24]{1,2,0:T(8,128)(2,1)S(1)} all-gather(bf16[1,32,24]{1,2,0:T(8,128)(2,1)} %bitcast.423), channel_id=1, replica_groups=mesh['dp'=4,'ctx'=8] {'dp','ctx'}, dimensions={0}, use_global_device_ids=true | all-gather | bytes 50688 | tf_op jit(solution)/shard_map/all_gather | solution.py:315
  126.4 63.4 %all-gather.2 = bf16[32,56,4]{1,2,0:T(4,128)(2,1)S(1)} all-gather(bf16[1,56,4]{1,2,0:T(4,128)(2,1)S(1)} %bitcast.428), channel_id=1, replica_groups=mesh['dp'=4,'ctx'=8] {'dp','ctx'}, dimensions={0}, use_global_device_ids=true | all-gather | bytes 14784 | tf_op jit(solution)/shard_map/all_gather | solution.py:316
  193.0 4.2 collective-permute-start
  211.0 68.5 %all_gather.93 = bf16[1024,128]{1,0:T(8,128)(2,1)S(1)} all-gather(bf16[32,128]{1,0:T(8,128)(2,1)S(1)} %copy-done.94), channel_id=1, replica_groups=mesh['dp'=4,'ctx'=8] {'dp','ctx'}, dimensions={0}, use_global_device_ids=true | all-gather | bytes 270336 | tf_op jit(solution)/shard_map/all_gather | solution.py:321
  280.0 65.4 %all_gather.94 = bf16[1024,128]{1,0:T(8,128)(2,1)S(1)} all-gather(bf16[32,128]{1,0:T(8,128)(2,1)S(1)} %copy-done.95), channel_id=1, replica_groups=mesh['dp'=4,'ctx'=8] {'dp','ctx'}, dimensions={0}, use_global_device_ids=true | all-gather | bytes 270336 | tf_op jit(solution)/shard_map/all_gather | solution.py:322
  346.1 28.7 %all_gather.95 = bf16[1024,256]{0,1:T(8,128)(2,1)S(1)} all-gather(bf16[128,256]{0,1:T(8,128)(2,1)S(1)} %pad_maximum_fusion.4), channel_id=1, replica_groups=mesh['dp'=4,'ctx'=8] {'ctx'}, dimensions={0}, use_global_device_ids=true | all-gather | bytes 589824 | tf_op jit(solution)/shard_map/all_gather | solution.py:369
  376.0 16.8 all-gather.4
  395.7 17.1 while.59
  415.7 18.6 while.58
  436.4 4.3 fusion.43
  442.1 3.8 multiply_reduce_fusion.12
  446.0 3.3 convolution_add_fusion.6
  451.9 56.7 %all-gather.26.cloned.1.call-done = bf16[1024,2048]{1,0:T(8,128)(2,1)} async-done(((bf16[32,2048]{1,0:T(8,128)(2,1)}), bf16[1024,2048]{1,0:T(8,128)(2,1)}) %all-gather.26.cloned.1.call-update) | async-done | bytes 4194320 | tf_op jit(solution)/shard_map/all_gather | solution.py:385
  508.6 2.9 fusion.181
  511.5 60.7 %all-gather.28.cloned.1.call-done = bf16[1024,2048]{1,0:T(8,128)(2,1)} async-done(((bf16[32,2048]{1,0:T(8,128)(2,1)}), bf16[1024,2048]{1,0:T(8,128)(2,1)}) %all-gather.28.cloned.1.call-update) | async-done | bytes 4194320 | tf_op jit(solution)/shard_map/all_gather | solution.py:386
  572.2 4.0 fusion.182
  576.2 59.7 %all-gather.30.cloned.1.call-done = bf16[2048,1024]{0,1:T(8,128)(2,1)} async-done(((bf16[2048,32]{0,1:T(8,128)(2,1)}), bf16[2048,1024]{0,1:T(8,128)(2,1)}) %all-gather.30.cloned.1.call-update) | async-done | bytes 4194320 | tf_op jit(solution)/shard_map/all_gather | solution.py:387
  635.9 4.7 multiply_convert_fusion
  648.6 18.3 while.61
  667.1 3.6 multiply_reduce_fusion.7
  678.6 5.5 fusion.55
  684.1 43.5 %reduce-scatter.16.cloned.1.call-done = bf16[128,256]{1,0:T(8,128)(2,1)} async-done(((bf16[1024,256]{1,0:T(8,128)(2,1)}), bf16[128,256]{1,0:T(8,128)(2,1)}) %reduce-scatter.16.cloned.1.call-update) | async-done | bytes 65552 | tf_op jit(solution)/shard_map/reduce_scatter | solution.py:469
  728.5 61.0 %all-gather.34.cloned.1.call-done = bf16[192,64,128]{2,1,0:T(8,128)(2,1)} async-done(((bf16[24,64,128]{2,1,0:T(8,128)(2,1)}), bf16[192,64,128]{2,1,0:T(8,128)(2,1)}) %all-gather.34.cloned.1.call-update) | async-done | bytes 3145744 | tf_op jit(solution)/shard_map/all_gather | solution.py:55
  789.5 15.2 while.60
  804.8 2.9 multiply_reduce_fusion.6
  819.2 4.8 fusion.158
  825.0 3.7 fusion.166
  829.6 5.6 fusion.187
  835.3 5.6 fusion.188
  841.8 5.6 fusion.100
  848.3 4.2 fusion.37
  867.8 4.0 collective-permute-done.1
  871.9 4.1 fusion.98
  876.9 3.0 fusion.184
  880.0 4.6 fusion.49
  887.6 41.1 %all-reduce.24 = (f32[1024]{0:T(1024)S(1)}, f32[4,1792]{1,0:T(4,128)S(1)}, f32[1792]{0:T(1024)S(1)}, f32[24]{0:T(128)}, f32[24]{0:T(128)}, /*index=5*/f32[24]{0:T(128)}, f32[1536]{0:T(1024)S(1)}, f32[1024]{0:T(1024)S(1)}) all-reduce(f32[1024]{0:T(1024)S(1)} %get-tuple-element.574, ...), channel_id=5, replica_groups=mesh['dp'=4,'ctx'=8] {'dp','ctx'}, use_global_device_ids=true, to_apply=%region_27.28.clone | all-reduce | flops 12616 | bytes 100928
  932.8 12.0 reduce-scatter.38.cloned.1.call-done
  946.1 131.9 %reduce-scatter.26.cloned.1.call-done = f32[32,128]{1,0:T(8,128)} async-done(((f32[1024,128]{1,0:T(8,128)}), f32[32,128]{1,0:T(8,128)}) %reduce-scatter.26.cloned.1.call-update) | async-done | bytes 16400 | tf_op jit(solution)/shard_map/reduce_scatter | solution.py:540
  1078.0 132.8 %reduce-scatter.28.cloned.1.call-done = f32[32,128]{1,0:T(8,128)} async-done(((f32[1024,128]{1,0:T(8,128)}), f32[32,128]{1,0:T(8,128)}) %reduce-scatter.28.cloned.1.call-update) | async-done | bytes 16400 | tf_op jit(solution)/shard_map/reduce_scatter | solution.py:543
  1210.8 136.6 %reduce-scatter.24.cloned.1.call-done = f32[32,512]{1,0:T(8,128)} async-done(((f32[1024,512]{1,0:T(8,128)}), f32[32,512]{1,0:T(8,128)}) %reduce-scatter.24.cloned.1.call-update) | async-done | bytes 65552 | tf_op jit(solution)/shard_map/reduce_scatter | solution.py:537
  1347.4 137.0 %reduce-scatter.30.cloned.1.call-done = f32[512,32]{0,1:T(8,128)} async-done(((f32[512,1024]{0,1:T(8,128)}), f32[512,32]{0,1:T(8,128)}) %reduce-scatter.30.cloned.1.call-update) | async-done | bytes 65552 | tf_op jit(solution)/shard_map/reduce_scatter | solution.py:546
  1484.4 117.8 %reduce-scatter.22.cloned.1.call-done = f32[1536,32]{0,1:T(8,128)} async-done(((f32[1536,1024]{0,1:T(8,128)}), f32[1536,32]{0,1:T(8,128)}) %reduce-scatter.22.cloned.1.call-update) | async-done | bytes 196624 | tf_op jit(solution)/shard_map/reduce_scatter | solution.py:536
  1602.2 121.0 %reduce-scatter.18.cloned.1.call-done = f32[32,1536]{1,0:T(8,128)} async-done(((f32[1024,1536]{1,0:T(8,128)}), f32[32,1536]{1,0:T(8,128)}) %reduce-scatter.18.cloned.1.call-update) | async-done | bytes 196624 | tf_op jit(solution)/shard_map/reduce_scatter | solution.py:524
  1723.1 187.0 %reduce-scatter.32.cloned.1.call-done = f32[32,2048]{1,0:T(8,128)} async-done(((f32[1024,2048]{1,0:T(8,128)}), f32[32,2048]{1,0:T(8,128)}) %reduce-scatter.32.cloned.1.call-update) | async-done | bytes 262160 | tf_op jit(solution)/shard_map/reduce_scatter | solution.py:420
  1910.1 187.2 %reduce-scatter.34.cloned.1.call-done = f32[32,2048]{1,0:T(8,128)} async-done(((f32[1024,2048]{1,0:T(8,128)}), f32[32,2048]{1,0:T(8,128)}) %reduce-scatter.34.cloned.1.call-update) | async-done | bytes 262160 | tf_op jit(solution)/shard_map/reduce_scatter | solution.py:421
  2097.3 186.7 %reduce-scatter.36.cloned.1.call-done = f32[2048,32]{0,1:T(8,128)} async-done(((f32[2048,1024]{0,1:T(8,128)}), f32[2048,32]{0,1:T(8,128)}) %reduce-scatter.36.cloned.1.call-update) | async-done | bytes 262160 | tf_op jit(solution)/shard_map/reduce_scatter | solution.py:422
  2284.0 166.6 %reduce-scatter.20.cloned.1.call-done = f32[32,1792]{1,0:T(8,128)} async-done(((f32[1024,1792]{1,0:T(8,128)}), f32[32,1792]{1,0:T(8,128)}) %reduce-scatter.20.cloned.1.call-update) | async-done | bytes 229392 | tf_op jit(solution)/shard_map/reduce_scatter | solution.py:527
  (508 shorter events, 163.6 us)
Async XLA Ops:
  7.2 183.0 %copy-start.1 = (bf16[1,128,1024]{2,1,0:T(8,128)(2,1)S(1)}, bf16[1,128,1024]{2,1,0:T(8,128)(2,1)}, u32[]{:S(2)}) copy-start(bf16[1,128,1024]{2,1,0:T(8,128)(2,1)} %param.29) | copy-start | bytes 786436
  7.2 119.2 %copy-start.100 = (bf16[4,56]{1,0:T(4,128)(2,1)S(1)}, bf16[4,56]{1,0:T(4,128)(2,1)}, u32[]{:S(2)}) copy-start(bf16[4,56]{1,0:T(4,128)(2,1)} %param.35) | copy-start | bytes 1348
  7.2 183.0 %all-gather.16.cloned.1.call-start = ((), (), s32[]{:S(2)}) async-start(), calls=%async_computation.12 | async-start | bytes 3784704 | tf_op jit(solution)/shard_map/all_gather | solution.py:314
  7.9 385.0 %all-gather.22.cloned.1.call-start = ((), (), s32[]{:S(2)}) async-start(), calls=%async_computation.15 | async-start | bytes 1081344 | tf_op jit(solution)/shard_map/all_gather | solution.py:320
  8.7 407.0 %all-gather.32.cloned.1.call-start = ((), (), s32[]{:S(2)}) async-start(), calls=%async_computation.31 | async-start | bytes 3538944 | tf_op jit(solution)/shard_map/all_gather | solution.py:32
  55.9 386.2 %copy-start.69 = (f32[128]{0:T(128)}, f32[128]{0:T(128)S(1)}, u32[]{:S(2)}) copy-start(f32[128]{0:T(128)S(1)} %get-tuple-element.688) | copy-start | bytes 1540
  124.1 68.9 %copy-start.54 = (bf16[1024,24]{0,1:T(8,128)(2,1)}, bf16[1024,24]{0,1:T(8,128)(2,1)S(1)}, u32[]{:S(2)}) copy-start(bf16[1024,24]{0,1:T(8,128)(2,1)S(1)} %reshape.548) | copy-start | bytes 147460
  124.8 68.2 %copy-start.101 = (f32[24]{0:T(128)}, f32[24]{0:T(128)S(1)}, u32[]{:S(2)}) copy-start(f32[24]{0:T(128)S(1)} %exponential_negate_fusion) | copy-start | bytes 292
  190.2 484.3 %copy-start.59 = (f32[128,24]{0,1:T(8,128)}, f32[128,24]{0,1:T(8,128)S(1)}, u32[]{:S(2)}) copy-start(f32[128,24]{0,1:T(8,128)S(1)} %get-tuple-element.682) | copy-start | bytes 36868
  193.0 5.6 collective-permute-start
  202.9 142.9 %copy-start.11 = (f32[128,1536]{0,1:T(8,128)}, f32[128,1536]{0,1:T(8,128)S(1)}, u32[]{:S(2)}) copy-start(f32[128,1536]{0,1:T(8,128)S(1)} %copy.220) | copy-start | bytes 2359300
  202.9 77.1 %copy-start.95 = (bf16[32,128]{1,0:T(8,128)(2,1)S(1)}, bf16[32,128]{1,0:T(8,128)(2,1)}, u32[]{:S(2)}) copy-start(bf16[32,128]{1,0:T(8,128)(2,1)} %param.44) | copy-start | bytes 24580
  204.5 237.7 %all-gather.18.cloned.1.call-start = ((), (), s32[]{:S(2)}) async-start(), calls=%async_computation.13 | async-start | bytes 3244032 | tf_op jit(solution)/shard_map/all_gather | solution.py:313
  205.0 241.0 %all-gather.20.cloned.1.call-start = ((), (), s32[]{:S(2)}) async-start(), calls=%async_computation.14 | async-start | bytes 3244032 | tf_op jit(solution)/shard_map/all_gather | solution.py:319
  205.6 243.7 %all-gather.24.cloned.1.call-start = ((), (), s32[]{:S(2)}) async-start(), calls=%async_computation.16 | async-start | bytes 1081344 | tf_op jit(solution)/shard_map/all_gather | solution.py:323
  206.2 302.3 %all-gather.26.cloned.1.call-start = ((), (), s32[]{:S(2)}) async-start(), calls=%async_computation.17 | async-start | bytes 4325376 | tf_op jit(solution)/shard_map/all_gather | solution.py:385
  207.0 365.3 %all-gather.28.cloned.1.call-start = ((), (), s32[]{:S(2)}) async-start(), calls=%async_computation.18 | async-start | bytes 4325376 | tf_op jit(solution)/shard_map/all_gather | solution.py:386
  207.7 428.2 %all-gather.30.cloned.1.call-start = ((), (), s32[]{:S(2)}) async-start(), calls=%async_computation.19 | async-start | bytes 4325376 | tf_op jit(solution)/shard_map/all_gather | solution.py:387
  208.4 519.2 %reduce-scatter.16.cloned.1.call-start = ((), (), s32[]{:S(2)}) async-start(), calls=%async_computation.20 | async-start | bytes 589824 | tf_op jit(solution)/shard_map/reduce_scatter | solution.py:469
  279.5 96.5 %copy-start.33 = (bf16[1024,128]{1,0:T(8,128)(2,1)}, bf16[1024,128]{1,0:T(8,128)(2,1)S(1)}, u32[]{:S(2)}) copy-start(bf16[1024,128]{1,0:T(8,128)(2,1)S(1)} %all_gather.93) | copy-start | bytes 786436
  280.0 112.9 %copy-start.96 = (bf16[1536]{0:T(1024)(128)(2,1)S(1)}, bf16[1536]{0:T(1024)(128)(2,1)}, u32[]{:S(2)}) copy-start(bf16[1536]{0:T(1024)(128)(2,1)} %get-tuple-element.646) | copy-start | bytes 9220
  280.0 112.9 %copy-start.99 = (bf16[1024]{0:T(1024)(128)(2,1)S(1)}, bf16[1024]{0:T(1024)(128)(2,1)}, u32[]{:S(2)}) copy-start(bf16[1024]{0:T(1024)(128)(2,1)} %get-tuple-element.647) | copy-start | bytes 6148
  345.9 382.6 %copy-start.58 = (f32[128,32]{0,1:T(8,128)}, f32[128,32]{0,1:T(8,128)S(1)}, u32[]{:S(2)}) copy-start(f32[128,32]{0,1:T(8,128)S(1)} %get-tuple-element.684) | copy-start | bytes 49156
  392.9 43.5 %copy-start.88 = (f32[24,128]{1,0:T(8,128)}, f32[24,128]{1,0:T(8,128)S(1)}, u32[]{:S(2)}) copy-start(f32[24,128]{1,0:T(8,128)S(1)} %copy.223) | copy-start | bytes 36868
  392.9 249.2 %copy-start.74 = (f32[1024]{0:T(1024)}, f32[1024]{0:T(1024)S(1)}, u32[]{:S(2)}) copy-start(f32[1024]{0:T(1024)S(1)} %convert_element_type.233) | copy-start | bytes 12292
  413.9 35.5 %copy-start.38 = (bf16[128,2,4,64]{0,3,2,1:T(8,128)(2,1)}, bf16[128,2,4,64]{0,3,2,1:T(8,128)(2,1)S(1)}, u32[]{:S(2)}) copy-start(bf16[128,2,4,64]{0,3,2,1:T(8,128)(2,1)S(1)} %copy.233) | copy-start | bytes 393220
  415.7 20.7 copy-start.71
  415.7 20.7 copy-start.12
  415.7 20.7 copy-start.79
  415.7 20.7 copy-start.91
  451.2 194.1 %copy-start.9 = (f32[128,1024]{1,0:T(8,128)}, f32[128,1024]{1,0:T(8,128)S(1)}, u32[]{:S(2)}) copy-start(f32[128,1024]{1,0:T(8,128)S(1)} %get-tuple-element.695) | copy-start | bytes 1572868
  451.9 120.4 %copy-start.19 = (bf16[128,1024]{1,0:T(8,128)(2,1)}, bf16[128,1024]{1,0:T(8,128)(2,1)S(1)}, u32[]{:S(2)}) copy-start(bf16[128,1024]{1,0:T(8,128)(2,1)S(1)} %multiply_convert_fusion.4) | copy-start | bytes 786436
  511.5 124.5 %copy-start.42 = (bf16[1,128,1024]{2,1,0:T(8,128)(2,1)S(1)}, bf16[1,128,1024]{2,1,0:T(8,128)(2,1)}, u32[]{:S(2)}) copy-start(bf16[1,128,1024]{2,1,0:T(8,128)(2,1)} %param.30) | copy-start | bytes 786436
  667.0 122.5 %all-gather.34.cloned.1.call-start = ((), (), s32[]{:S(2)}) async-start(), calls=%async_computation.32 | async-start | bytes 3538944 | tf_op jit(solution)/shard_map/all_gather | solution.py:55
  676.9 267.8 %reduce-scatter.38.cloned.1.call-start = ((), (), s32[]{:S(2)}) async-start(), calls=%async_computation.33 | async-start | bytes 540672
  811.7 266.3 %reduce-scatter.26.cloned.1.call-start = ((), (), s32[]{:S(2)}) async-start(), calls=%async_computation.25 | async-start | bytes 540672 | tf_op jit(solution)/shard_map/reduce_scatter | solution.py:540
  812.9 397.9 %reduce-scatter.28.cloned.1.call-start = ((), (), s32[]{:S(2)}) async-start(), calls=%async_computation.26 | async-start | bytes 540672 | tf_op jit(solution)/shard_map/reduce_scatter | solution.py:543
  814.1 533.3 %reduce-scatter.24.cloned.1.call-start = ((), (), s32[]{:S(2)}) async-start(), calls=%async_computation.24 | async-start | bytes 2162688 | tf_op jit(solution)/shard_map/reduce_scatter | solution.py:537
  817.2 667.2 %reduce-scatter.30.cloned.1.call-start = ((), (), s32[]{:S(2)}) async-start(), calls=%async_computation.27 | async-start | bytes 2162688 | tf_op jit(solution)/shard_map/reduce_scatter | solution.py:546
  819.1 783.1 %reduce-scatter.22.cloned.1.call-start = ((), (), s32[]{:S(2)}) async-start(), calls=%async_computation.23 | async-start | bytes 6488064 | tf_op jit(solution)/shard_map/reduce_scatter | solution.py:536
  824.0 899.1 %reduce-scatter.18.cloned.1.call-start = ((), (), s32[]{:S(2)}) async-start(), calls=%async_computation.21 | async-start | bytes 6488064 | tf_op jit(solution)/shard_map/reduce_scatter | solution.py:524
  828.7 1081.4 %reduce-scatter.32.cloned.1.call-start = ((), (), s32[]{:S(2)}) async-start(), calls=%async_computation.28 | async-start | bytes 8650752 | tf_op jit(solution)/shard_map/reduce_scatter | solution.py:420
  835.2 1262.1 %reduce-scatter.34.cloned.1.call-start = ((), (), s32[]{:S(2)}) async-start(), calls=%async_computation.29 | async-start | bytes 8650752 | tf_op jit(solution)/shard_map/reduce_scatter | solution.py:421
  840.9 1443.1 %reduce-scatter.36.cloned.1.call-start = ((), (), s32[]{:S(2)}) async-start(), calls=%async_computation.30 | async-start | bytes 8650752 | tf_op jit(solution)/shard_map/reduce_scatter | solution.py:422
  847.5 1603.1 %reduce-scatter.20.cloned.1.call-start = ((), (), s32[]{:S(2)}) async-start(), calls=%async_computation.22 | async-start | bytes 7569408 | tf_op jit(solution)/shard_map/reduce_scatter | solution.py:527
  866.1 5.8 collective-permute-start.1
  886.9 44.8 %copy-start.36 = (f32[128,1024]{1,0:T(8,128)S(1)}, f32[128,1024]{1,0:T(8,128)}, u32[]{:S(2)}) copy-start(f32[128,1024]{1,0:T(8,128)} %get-tuple-element.656) | copy-start | bytes 1572868
  887.0 44.8 %copy-start.105 = (f32[128]{0:T(128)S(1)}, f32[128]{0:T(128)}, u32[]{:S(2)}) copy-start(f32[128]{0:T(128)} %get-tuple-element.687) | copy-start | bytes 1540
  (93 other events, 331.1 us)
Sparse Core Ops, SparseCore 0:
  10.9 63.6 all-gather.15
  77.6 52.6 all-gather.21
  204.6 60.7 all-gather.31
  268.2 58.4 all-gather.17
  329.5 59.4 all-gather.19
  391.8 52.5 all-gather.23
  447.5 61.0 all-gather.25
  511.5 60.6 all-gather.27
  575.2 60.6 all-gather.29
  667.1 60.4 reduce-scatter.15
  730.0 59.4 all-gather.33
  811.8 132.9 reduce-scatter.37
  947.6 130.3 reduce-scatter.25
  1080.8 130.0 reduce-scatter.27
  1213.5 133.8 reduce-scatter.23
  1350.2 134.1 reduce-scatter.29
  1490.4 111.6 reduce-scatter.21
  1609.2 113.9 reduce-scatter.17
  1726.0 184.0 reduce-scatter.31
  1912.8 184.4 reduce-scatter.33
  2100.2 183.7 reduce-scatter.35
  2286.9 163.6 reduce-scatter.19
where the time goes:
time: 2470 us; the launch traced here: 2460 us
  waiting for transfers between devices  1810 us (73%)
  blocking collectives  394 us (16%)
  matrix products  123 us (5%)
  other arithmetic  64.5 us (3%)
  local copies, waits for them, and re-layouts  42.9 us (2%)
    reduce_scatter x1, waiting for transfers between devices, local(): lax.psum_scatter(gradient_feed_up, ('dp', 'ctx'), scatter_dimension=0, ti...  187 us
    reduce_scatter x1, waiting for transfers between devices, local(): lax.psum_scatter(gradient_feed_gate, ('dp', 'ctx'), scatter_dimension=0,...  187 us
    reduce_scatter x1, waiting for transfers between devices, local(): lax.psum_scatter(gradient_down, ('dp', 'ctx'), scatter_dimension=1, tiled...  187 us
    reduce_scatter x1, waiting for transfers between devices, local(): lax.psum_scatter(weight_product(low_normed, low_mix), ('dp', 'ctx'), scat...  167 us
    reduce_scatter x1, waiting for transfers between devices, local(): lax.psum_scatter(gradient_attention_out, ('dp', 'ctx'), scatter_dimension...  137 us
    reduce_scatter x1, waiting for transfers between devices, local(): lax.psum_scatter(weight_product(low_normed, back_query), ('dp', 'ctx'), s...  137 us
    reduce_scatter x1, waiting for transfers between devices, local(): lax.psum_scatter(weight_product(low_normed, back_values), ('dp', 'ctx'),...  133 us
    reduce_scatter x1, waiting for transfers between devices, local(): lax.psum_scatter(weight_product(low_normed, back_keys), ('dp', 'ctx'), sc...  132 us
  transfers between devices with their start and end apart: 24, of which 18 were waited for; matrix products, arithmetic and copies ran while one was open for 7% of the time, Pallas kernels for 0%

commit v1 on v0

v1 whole, which is shorter than its diff:
```python
import jax
import jax.numpy as jnp
from jax import lax
from jax.sharding import PartitionSpec as P

D = 1024
DSSM = 1536
MH = 24
MP = 64
NS = 128
KW = 4
AH = 8
KVH = 2
HD = 64
FF = 2048
CONV = DSSM + 2 * NS

TP = 4
SW = DSSM // TP
SH = MH // TP
QW = AH * HD // TP
FW = FF // TP
MIXW = SW + 2 * NS
STEP_AT = SW + MIXW + QW + 2 * HD
VEC = 16
WIDE = 1408

EPSILON = 1e-05
ROPE_BASE = 100000000000.0
HIGHEST = lax.Precision.HIGHEST
NEGATIVE = -1e30
BOTH = ("dp", "ctx")
bf16 = jnp.bfloat16
f32 = jnp.float32


def forward_product(left, right):
    return jnp.dot(left, right, preferred_element_type=f32)


def weight_product(left, right):
    return lax.dot_general(
        left, right, (((0,), (0,)), ((), ())), preferred_element_type=f32
    ).astype(bf16)


def input_product(upstream, weight):
    return lax.dot_general(
        upstream, weight, (((1,), (1,)), ((), ())), preferred_element_type=f32
    )


def swap_core(value):
    pairs = [(i, i ^ 1) for i in range(lax.axis_size("dp"))]
    return lax.ppermute(value, "dp", pairs)


def swap_side(value):
    pairs = [(i, i ^ 1) for i in range(lax.axis_size("ctx"))]
    return lax.ppermute(value, "ctx", pairs)


def swap_both(value):
    blocks = lax.axis_size("ctx")
    count = lax.axis_size("dp") * blocks
    pairs = [(i, ((i // blocks) ^ 1) * blocks + ((i % blocks) ^ 1)) for i in range(count)]
    return lax.ppermute(value, BOTH, pairs)


def move_spans(value, by):
    blocks = lax.axis_size("ctx")
    pairs = [(i, i + 2 * by) for i in range(blocks) if 0 <= i + 2 * by < blocks]
    return lax.ppermute(value, "ctx", pairs)


def group_gather(value, side):
    other = swap_side(value)
    first = side == 0
    mine = jnp.concatenate([jnp.where(first, value, other), jnp.where(first, other, value)], 0)
    return jnp.concatenate([mine, swap_core(mine)], 0)


def group_scatter(partial, side):
    span = partial.shape[0] // 2
    rows = span // 2
    mine = partial[:span] + swap_core(partial[span:])
    first = side == 0
    keep = jnp.where(first, mine[:rows], mine[rows:])
    send = jnp.where(first, mine[rows:], mine[:rows]).astype(bf16)
    return keep + swap_side(send).astype(f32)


def group_sum(value):
    span = value.shape[0] // 2
    other = swap_core(value)
    value = value + jnp.concatenate([other[span:], other[:span]], 0)
    return value + swap_side(value)


def group_swap(parts, rank):
    def at(index):
        return lax.dynamic_index_in_dim(parts, index, 0, keepdims=True)

    pieces = (
        (rank, at(rank)),
        (rank ^ 1, swap_side(at(rank ^ 1))),
        (rank ^ 2, swap_core(at(rank ^ 2))),
        (rank ^ 3, swap_both(at(rank ^ 3))),
    )
    result = jnp.zeros_like(parts)
    for index, piece in pieces:
        result = lax.dynamic_update_slice_in_dim(result, piece, index, 0)
    return result


def rope_tables(positions):
    ladder = jnp.arange(HD // 2, dtype=f32)
    rates = ROPE_BASE ** (-2.0 * ladder / HD)
    angles = positions.astype(f32)[:, None] * rates[None, :]
    return (jnp.cos(angles), jnp.sin(angles))


def rotate(values, cosine, sine):
    half = values.shape[-1] // 2
    first = values[..., :half]
    second = values[..., half:]
    cosine = cosine[:, None, :]
    sine = sine[:, None, :]
    return jnp.concatenate([first * cosine - second * sine, second * cosine + first * sine], -1)


def mamba_prep(extended, step_rows, kernel, offset, step_offset, decay_log):
    rows = step_rows.shape[1]
    conv = offset + kernel[0] * extended[:, 0:rows]
    for tap in range(1, KW):
        conv = conv + kernel[tap] * extended[:, tap : tap + rows]
    steps = jax.nn.softplus(step_rows + step_offset)
    rate = -jnp.exp(decay_log) * steps
    lower = jnp.tril(jnp.ones((rows, rows), f32))
    curve = jnp.einsum("ts,bsh->bth", lower, rate, precision=HIGHEST)
    return (jax.nn.silu(conv), steps, curve)


def mamba_state(conv, steps, curve):
    batch, rows, heads = steps.shape
    signal = conv[..., :SW].reshape(batch, rows, heads, MP)
    entry = conv[..., SW : SW + NS]
    weights = jnp.exp(curve[:, -1:] - curve) * steps
    scaled = weights[..., None] * signal
    state = jnp.einsum("bthp,btn->bhpn", scaled, entry, precision=HIGHEST)
    return (curve[:, -1], state)


def mamba_out(conv, steps, curve, skip_scale, state_in):
    batch, rows, heads = steps.shape
    signal = conv[..., :SW].reshape(batch, rows, heads, MP)
    entry = conv[..., SW : SW + NS]
    readout = conv[..., SW + NS :]
    causal = jnp.tril(jnp.ones((rows, rows), jnp.bool_))
    turned = curve.transpose(0, 2, 1)
    spread = turned[:, :, :, None] - turned[:, :, None, :]
    mixing = jnp.where(causal, jnp.exp(jnp.where(causal, spread, 0.0)), 0.0)
    intersection = jnp.einsum("btn,bsn->bts", readout, entry, precision=HIGHEST)
    mixing = mixing * intersection[:, None] * steps.transpose(0, 2, 1)[:, :, None, :]
    local_part = jnp.einsum("bhts,bshp->bthp", mixing, signal, precision=HIGHEST)
    carried = (
        jnp.einsum("btn,bhpn->bthp", readout, state_in, precision=HIGHEST)
        * jnp.exp(curve)[..., None]
    )
    mixed = local_part + carried + skip_scale[:, None] * signal
    return mixed.reshape(batch * rows, heads * MP)


def visible_keys(span, spans, heads, at):
    query = jnp.arange(heads * span, dtype=jnp.int32)[:, None] % span
    key = jnp.arange(spans * span, dtype=jnp.int32)[None, :]
    back = key // span
    return jnp.where(back == 0, key <= query, back <= at)


def attend(query, keys, values, visible):
    scores = jnp.einsum("bqd,bkd->bqk", query, keys, preferred_element_type=f32) * HD ** (-0.5)
    scores = jnp.where(visible, scores, NEGATIVE)
    peak = jnp.max(scores, -1, keepdims=True)
    weights = jnp.exp(scores - peak)
    total = jnp.sum(weights, -1, keepdims=True)
    summed = jnp.einsum("bqk,bkd->bqd", weights.astype(bf16), values, preferred_element_type=f32)
    return (summed / total, peak + jnp.log(total))


def attend_back(query, keys, values, visible, back, log_total, delta):
    scale = HD ** (-0.5)
    scores = jnp.einsum("bqd,bkd->bqk", query, keys, preferred_element_type=f32) * scale
    chance = jnp.where(visible, jnp.exp(scores - log_total), 0.0)
    back_values = jnp.einsum(
        "bqk,bqd->bkd", chance.astype(bf16), back, preferred_element_type=f32
    )
    back_chance = jnp.einsum("bqd,bkd->bqk", back, values, preferred_element_type=f32)
    back_scores = (chance * (back_chance - delta) * scale).astype(bf16)
    back_query = jnp.einsum("bqk,bkd->bqd", back_scores, keys, preferred_element_type=f32)
    back_keys = jnp.einsum("bqk,bqd->bkd", back_scores, query, preferred_element_type=f32)
    return (back_query, jnp.concatenate([back_keys, back_values], -1))


def local(
    tokens,
    out_cotangent,
    input_gain,
    mamba_gate_weight,
    mamba_mix_weight,
    mamba_step_weight,
    conv_kernel,
    conv_offset,
    step_offset,
    decay_log,
    skip_scale,
    mamba_norm_gain,
    mamba_out_weight,
    query_weight,
    key_weight,
    value_weight,
    attention_out_weight,
    ffn_gain,
    feed_gate_weight,
    feed_up_weight,
    feed_down_weight,
):
    rows = tokens.shape[1]
    span = 2 * rows
    count = 2 * span
    pairs, spans = lax.axis_size("dp") // 2, lax.axis_size("ctx") // 2
    devices = 4 * pairs * spans
    dp_at, ctx_at = lax.axis_index("dp"), lax.axis_index("ctx")
    side, span_at = ctx_at % 2, ctx_at // 2
    rank = (dp_at % 2) * 2 + side
    part = D // devices
    conv_part = CONV // devices
    gain_part = DSSM // devices
    groups = [
        [(y * 2 + c) * 2 * spans + z * 2 + x for y in range(pairs) for z in range(spans)]
        for c in range(2)
        for x in range(2)
    ]

    def order(value):
        lead = value.shape[:-1]
        value = value.reshape(*lead, pairs, 2, spans, 2 * part)
        return jnp.swapaxes(value, -3, -2).reshape(*lead, D)

    def disorder(value):
        lead = value.shape[:-1]
        value = value.reshape(*lead, pairs, spans, 2, 2 * part)
        return jnp.swapaxes(value, -3, -2).reshape(*lead, D)

    def gather(value):
        return lax.all_gather(value, BOTH, axis=0, tiled=True, axis_index_groups=groups)

    def scatter(value):
        return lax.psum_scatter(
            value, BOTH, scatter_dimension=0, tiled=True, axis_index_groups=groups
        )

    vector = jnp.concatenate(
        [
            input_gain,
            ffn_gain,
            conv_kernel.reshape(-1),
            conv_offset,
            mamba_norm_gain,
        ]
    )
    vector = jnp.pad(vector, (0, part * VEC - vector.shape[0])).reshape(part, VEC)

    def mixer_part(s):
        kv = s // 2
        return jnp.concatenate(
            [
                mamba_gate_weight[:, SW * s : SW * (s + 1)],
                mamba_mix_weight[:, SW * s : SW * (s + 1)],
                mamba_mix_weight[:, DSSM:],
                query_weight[:, QW * s : QW * (s + 1)],
                key_weight[:, HD * kv : HD * (kv + 1)],
                value_weight[:, HD * kv : HD * (kv + 1)],
                mamba_step_weight[:, SH * s : SH * (s + 1)],
                vector,
                jnp.zeros((part, WIDE - STEP_AT - SH - VEC), bf16),
            ],
            1,
        )

    mamba_out_turned = mamba_out_weight.T
    attention_out_turned = attention_out_weight.T
    feed_down_turned = feed_down_weight.T

    def feed_part(s):
        return jnp.concatenate(
            [
                mamba_out_turned[:, SW * s : SW * (s + 1)],
                attention_out_turned[:, QW * s : QW * (s + 1)],
                feed_gate_weight[:, FW * s : FW * (s + 1)],
                feed_up_weight[:, FW * s : FW * (s + 1)],
                feed_down_turned[:, FW * s : FW * (s + 1)],
            ],
            1,
        )

    mixer_own = group_swap(jnp.stack([mixer_part(s) for s in range(TP)]), rank)
    mixer = gather(mixer_own.reshape(TP * part, WIDE))
    feed_own = group_swap(jnp.stack([feed_part(s) for s in range(TP)]), rank)
    feed_own, mixer = lax.optimization_barrier((feed_own, mixer))
    feed = gather(feed_own.reshape(TP * part, feed_own.shape[-1]))
    full_out = feed[:, : SW + QW]
    full_gate_up = feed[:, SW + QW : SW + QW + 2 * FW]
    full_down = feed[:, SW + QW + 2 * FW :]

    vectors = mixer[:, STEP_AT + SH : STEP_AT + SH + VEC].reshape(devices, part * VEC)
    full_gain = vectors[:, :part].reshape(D).astype(f32)
    full_gain_two = vectors[:, part : 2 * part].reshape(D).astype(f32)
    natural = vectors.reshape(pairs, spans, 2, 2, part * VEC)
    natural = natural.transpose(0, 2, 1, 3, 4).reshape(devices, part * VEC)
    at = 2 * part
    all_kernel = natural[:, at : at + KW * conv_part].reshape(devices, KW, conv_part)
    all_kernel = all_kernel.transpose(1, 0, 2).reshape(KW, CONV)
    at += KW * conv_part
    all_offset = natural[:, at : at + conv_part].reshape(1, CONV)
    at += conv_part
    all_mamba_gain = natural[:, at : at + gain_part].reshape(DSSM)
    taps = jnp.concatenate([all_kernel, all_offset], 0)
    taps = jnp.concatenate(
        [lax.dynamic_slice_in_dim(taps, rank * SW, SW, 1), taps[:, DSSM:]], 1
    ).astype(f32)
    kernel, offset = taps[:KW], taps[KW]
    mamba_gain = lax.dynamic_slice_in_dim(all_mamba_gain, rank * SW, SW, 0).astype(f32)
    own_step_offset = lax.dynamic_slice_in_dim(step_offset, rank * SH, SH, 0)
    own_decay_log = lax.dynamic_slice_in_dim(decay_log, rank * SH, SH, 0)
    own_skip = lax.dynamic_slice_in_dim(skip_scale, rank * SH, SH, 0)

    own_low = order(tokens[0])
    own_hidden = own_low.astype(f32)
    own_scale_one = lax.rsqrt(jnp.mean(own_hidden * own_hidden, -1, keepdims=True) + EPSILON)
    hidden = group_gather(own_low, side).astype(f32)
    own_cotangent = order(out_cotangent[0])
    upstream = group_gather(own_cotangent, side)
    scale_one = lax.rsqrt(jnp.mean(hidden * hidden, -1, keepdims=True) + EPSILON)
    low_normed = (hidden * scale_one * full_gain).astype(bf16)

    projected = forward_product(low_normed, mixer)
    gate_rows = projected[:, :SW]
    mix_rows = projected[:, SW : SW + MIXW].astype(bf16).reshape(2, span, MIXW)
    at = SW + MIXW
    query_rows = projected[:, at : at + QW]
    key_rows = projected[:, at + QW : at + QW + HD]
    value_rows = projected[:, at + QW + HD : STEP_AT]
    step_rows = projected[:, STEP_AT : STEP_AT + SH].reshape(2, span, SH)

    positions = span_at * span + jnp.arange(span, dtype=jnp.int32)
    cosine, sine = rope_tables(positions)
    heads = QW // HD
    query = rotate(query_rows.reshape(2, span, heads, HD), cosine, sine).astype(bf16)
    query = query.transpose(0, 2, 1, 3).reshape(2, heads * span, HD)
    keys = rotate(key_rows.reshape(2, span, 1, HD), cosine, sine).reshape(2, span, HD)
    key_value = jnp.concatenate([keys, value_rows.reshape(2, span, HD)], -1).astype(bf16)
    reached = [key_value] + [move_spans(key_value, s) for s in range(1, spans)]
    key_values = jnp.concatenate(reached, 1)
    all_keys, all_values = key_values[..., :HD], key_values[..., HD:]
    visible = visible_keys(span, spans, heads, span_at)

    rim = move_spans(mix_rows[:, span - (KW - 1) :], 1)
    extended = jnp.concatenate([rim, mix_rows], 1).astype(f32)
    (conv, steps, curve), prep_pull = jax.vjp(
        mamba_prep, extended, step_rows, kernel, offset, own_step_offset, own_decay_log
    )
    (log_decay, local_state), state_pull = jax.vjp(mamba_state, conv, steps, curve)
    low_state = local_state.astype(bf16)
    states = [move_spans(low_state, s) for s in range(1, spans)]
    decays = [move_spans(log_decay, s) for s in range(1, spans)]
    factors = []
    between = jnp.zeros_like(log_decay)
    for s in range(1, spans):
        factors.append(jnp.exp(between)[:, :, None, None])
        between = between + decays[s - 1]
    state_in = sum(factor * state.astype(f32) for factor, state in zip(factors, states))

    attended_rows, log_total = attend(query, all_keys, all_values, visible)

    def join(value):
        return value.reshape(2, heads, span, HD).transpose(0, 2, 1, 3).reshape(count, QW)

    def split(value):
        return value.reshape(2, span, heads, HD).transpose(0, 2, 1, 3).reshape(2, heads * span, HD)

    attended = join(attended_rows).astype(bf16)

    mixed, out_pull = jax.vjp(mamba_out, conv, steps, curve, own_skip, state_in)
    gate_sigmoid = jax.nn.sigmoid(gate_rows)
    gate_silu = gate_rows * gate_sigmoid
    gated = mixed * gate_silu
    square = group_sum(jnp.sum(gated * gated, -1))
    mamba_scale = lax.rsqrt(square / DSSM + EPSILON)[:, None]
    mamba_rows = (gated * mamba_scale * mamba_gain).astype(bf16)
    branches = jnp.concatenate([mamba_rows, attended], 1)
    middle = own_hidden + group_scatter(input_product(branches, full_out), side)

    scale_two = lax.rsqrt(jnp.mean(middle * middle, -1, keepdims=True) + EPSILON)
    low_two = group_gather((middle * scale_two * full_gain_two).astype(bf16), side)
    pre = forward_product(low_two, full_gate_up)
    gate_pre, up_pre = pre[:, :FW], pre[:, FW:]
    sigmoid = jax.nn.sigmoid(gate_pre)
    silu = gate_pre * sigmoid
    activation = (silu * up_pre).astype(bf16)

    back_activation = forward_product(upstream, full_down)
    back_gate = (back_activation * up_pre * sigmoid * (1.0 + gate_pre * (1.0 - sigmoid))).astype(
        bf16
    )
    back_up = (back_activation * silu).astype(bf16)
    back_feed = jnp.concatenate([back_gate, back_up], 1)
    back_normed_two = group_scatter(input_product(back_feed, full_gate_up), side)
    weighted = back_normed_two * full_gain_two
    gradient_gain_two = jnp.sum(back_normed_two * middle * scale_two, 0)
    back_middle = (
        own_cotangent.astype(f32)
        + scale_two * weighted
        - middle * scale_two**3 * jnp.mean(weighted * middle, -1, keepdims=True)
    )
    low_middle = group_gather(back_middle.astype(bf16), side)

    gradient_feed = scatter(
        jnp.concatenate(
            [
                weight_product(low_middle, branches),
                weight_product(low_two, back_feed),
                weight_product(upstream, activation),
            ],
            1,
        )
    )
    layer_out = middle + group_scatter(input_product(activation, full_down), side)

    back_branches = forward_product(low_middle, full_out)
    back_attended = back_branches[:, SW:].astype(bf16)
    back_rows = back_branches[:, :SW]
    wide_back = back_attended.astype(f32) * attended.astype(f32)
    delta = jnp.sum(split(wide_back), -1, keepdims=True)
    back_turned, back_key_values = attend_back(
        query, all_keys, all_values, visible, split(back_attended), log_total, delta
    )
    low_key_values = back_key_values.astype(bf16).reshape(2, spans, span, 2 * HD)
    back_key_value = back_key_values[:, :span]
    for s in range(1, spans):
        back_key_value = back_key_value + move_spans(low_key_values[:, s], -s).astype(f32)
    back_query = rotate(join(back_turned).reshape(2, span, heads, HD), cosine, -sine)
    back_keys = rotate(back_key_value[..., :HD].reshape(2, span, 1, HD), cosine, -sine)

    weighted = back_rows * mamba_gain
    gradient_mamba_gain = jnp.sum(back_rows * gated * mamba_scale, 0)
    product = group_sum(jnp.sum(weighted * gated, -1))[:, None] / DSSM
    back_gated = mamba_scale * weighted - gated * mamba_scale**3 * product
    back_mixed = back_gated * gate_silu
    low_gate = (
        back_gated * mixed * gate_sigmoid * (1.0 + gate_rows * (1.0 - gate_sigmoid))
    ).astype(bf16)
    out_grads = out_pull(back_mixed)
    next_back = jnp.zeros_like(local_state)
    for s in range(1, spans):
        sent = (factors[s - 1] * out_grads[4]).astype(bf16)
        next_back = next_back + move_spans(sent, -s).astype(f32)
    decay_back = jnp.sum(next_back * state_in, axis=(2, 3)) * jnp.exp(log_decay)
    state_grads = state_pull((decay_back, next_back))
    prep_grads = prep_pull(
        (
            out_grads[0] + state_grads[0],
            out_grads[1] + state_grads[1],
            out_grads[2] + state_grads[2],
        )
    )
    back_extended = prep_grads[0]
    returned = move_spans(back_extended[:, : KW - 1], -1)
    back_mix = back_extended[:, KW - 1 :]
    back_mix = jnp.concatenate(
        [back_mix[:, : span - (KW - 1)], back_mix[:, span - (KW - 1) :] + returned], 1
    )
    back_all = jnp.concatenate(
        [
            low_gate,
            back_mix.reshape(count, MIXW).astype(bf16),
            back_query.reshape(count, QW).astype(bf16),
            back_keys.reshape(count, HD).astype(bf16),
            back_key_value[..., HD:].reshape(count, HD).astype(bf16),
            prep_grads[1].reshape(count, SH).astype(bf16),
            jnp.zeros((count, WIDE - STEP_AT - SH), bf16),
        ],
        1,
    )
    gradient_mixer = scatter(weight_product(low_normed, back_all))
    back_normed = group_scatter(input_product(back_all, mixer), side)
    weighted = back_normed * full_gain
    gradient_gain_one = jnp.sum(back_normed * own_hidden * own_scale_one, 0)
    input_gradient = (
        back_middle
        + own_scale_one * weighted
        - own_hidden * own_scale_one**3 * jnp.mean(weighted * own_hidden, -1, keepdims=True)
    )

    def placed(value, width):
        wide = jnp.zeros(value.shape[:-1] + (width,), f32)
        return lax.dynamic_update_slice_in_dim(
            wide, value, rank * value.shape[-1], value.ndim - 1
        )

    tap_grads = jnp.concatenate([prep_grads[2], prep_grads[3][None]], 0)
    tap_grads = jnp.concatenate([placed(tap_grads[:, :SW], DSSM), tap_grads[:, SW:]], 1)
    head_grads = jnp.stack([prep_grads[4], prep_grads[5], out_grads[3]])
    gain_grads, tap_grads, mamba_gain_grad, head_grads = lax.psum(
        (
            jnp.stack([gradient_gain_one, gradient_gain_two]),
            tap_grads,
            placed(gradient_mamba_gain, DSSM),
            placed(head_grads, MH),
        ),
        BOTH,
    )
    feature_at = ((dp_at // 2 * spans + span_at) * TP + rank) * part
    own_gains = lax.dynamic_slice_in_dim(gain_grads, feature_at, part, 1)
    device_at = dp_at * 2 * spans + ctx_at
    own_taps = lax.dynamic_slice_in_dim(tap_grads, device_at * conv_part, conv_part, 1)
    own_mamba_gain = lax.dynamic_slice_in_dim(
        mamba_gain_grad, device_at * gain_part, gain_part, 0
    )

    feed_parts = group_swap(gradient_feed.reshape(TP, part, -1), rank).astype(f32)
    mixer_parts = group_swap(gradient_mixer.reshape(TP, part, WIDE), rank).astype(f32)

    def columns(parts, start, width):
        piece = parts[:, :, start : start + width]
        return piece.transpose(1, 0, 2).reshape(part, TP * width)

    def shared(start):
        piece = mixer_parts[:, :, start : start + HD].reshape(KVH, TP // KVH, part, HD)
        return jnp.sum(piece, 1).transpose(1, 0, 2).reshape(part, KVH * HD)

    at = SW + MIXW
    mix_gradient = jnp.concatenate(
        [
            columns(mixer_parts, SW, SW),
            jnp.sum(mixer_parts[:, :, 2 * SW : SW + MIXW], 0),
        ],
        1,
    )
    return (
        disorder(layer_out.astype(bf16))[None],
        disorder(input_gradient)[None],
        own_gains[0],
        columns(mixer_parts, 0, SW),
        mix_gradient,
        columns(mixer_parts, STEP_AT, SH),
        own_taps[:KW],
        own_taps[KW],
        head_grads[0],
        head_grads[1],
        head_grads[2],
        own_mamba_gain,
        columns(feed_parts, 0, SW).T,
        columns(mixer_parts, at, QW),
        shared(at + QW),
        shared(at + QW + HD),
        columns(feed_parts, SW, QW).T,
        own_gains[1],
        columns(feed_parts, SW + QW, FW),
        columns(feed_parts, SW + QW + FW, FW),
        columns(feed_parts, SW + QW + 2 * FW, FW).T,
    )


def solution(mesh):
    both = BOTH
    tokens = P("dp", "ctx", None)
    first = P(both, None)
    second = P(None, both)
    vector = P(both)
    whole = P()
    weights = (
        vector,
        first,
        first,
        first,
        second,
        vector,
        whole,
        whole,
        whole,
        vector,
        second,
        first,
        first,
        first,
        second,
        vector,
        first,
        first,
        second,
    )
    return jax.shard_map(
        local,
        mesh=mesh,
        in_specs=(tokens, tokens) + weights,
        out_specs=(tokens, tokens) + weights,
        check_vma=False,
    )
```

time: 2470 us -> 569 us (0.23)
  waiting for transfers between devices: 1810 us -> 226 us
  blocking collectives: 394 us -> 43.3 us
  starting transfers between devices: 6.52 us -> 61.4 us
  matrix products: 123 us -> 71.2 us
  local copies, waits for them, and re-layouts: 42.9 us -> 91.8 us
    reduce_scatter x11 -> x2, waiting for transfers between devices: 1550 us -> 72.2 us  [scatter(): lax.psum_scatter(value, BOTH, scatter_dimension=0, tiled=True, axis_index...]
    all_gather x6 -> x0, blocking collectives: 311 us -> none  [the longest x1 68.5 us: local(): lax.all_gather(key_weight, ('dp', 'ctx'), axis=0, tiled=True)]
    all_gather x10 -> x2, waiting for transfers between devices: 238 us -> 42.1 us  [gather(): lax.all_gather(value, BOTH, axis=0, tiled=True, axis_index_groups=groups)]
    ppermute x2 -> x48, waiting for transfers between devices: 5.31 us -> 111 us  [the longest x14 51.7 us: swap_side(): return lax.ppermute(value, 'ctx', pairs)]
    unnamed x2 -> x0, blocking collectives: 83.3 us -> none
    ppermute x2 -> x48, starting transfers between devices: 5.47 us -> 61 us  [the longest x16 40.3 us: move_spans(): return lax.ppermute(value, 'ctx', pairs)]
    psum x0 -> x1, blocking collectives: none -> 43.3 us  [local(): lax.psum((jnp.stack([gradient_gain_one, gradient_gain_two]), tap_grads, p...]
    dot_general x10 -> x4, matrix products: 35.5 us -> 7.35 us  [weight_product(): lax.dot_general(left, right, (((0,), (0,)), ((), ())), preferred_element_...]
  transfers between devices with their start and end apart: 24 -> 52, of which waited for: 18 -> 31; matrix products, arithmetic and copies ran while one was open for 7% -> 25% of each run, Pallas kernels for 0% -> 0%
where the time goes in v1:
time: 569 us; the launch traced here: 559 us
  waiting for transfers between devices  226 us (40%)
  local copies, waits for them, and re-layouts  91.8 us (16%)
  matrix products  71.2 us (13%)
  starting transfers between devices  61.4 us (11%)
  other arithmetic  48.9 us (9%)
  blocking collectives  43.3 us (8%)
  between operations  17 us (3%)
    reduce_scatter x2, waiting for transfers between devices, scatter(): lax.psum_scatter(value, BOTH, scatter_dimension=0, tiled=True, axis_index...  72.2 us
    ppermute x14, waiting for transfers between devices, swap_side(): return lax.ppermute(value, 'ctx', pairs)  51.7 us
    psum x1, blocking collectives, local(): lax.psum((jnp.stack([gradient_gain_one, gradient_gain_two]), tap_grads, p...  43.3 us
    ppermute x16, waiting for transfers between devices, move_spans(): return lax.ppermute(value, 'ctx', pairs)  42.4 us
    all_gather x2, waiting for transfers between devices, gather(): lax.all_gather(value, BOTH, axis=0, tiled=True, axis_index_groups=groups)  42.1 us
    ppermute x16, starting transfers between devices, move_spans(): return lax.ppermute(value, 'ctx', pairs)  40.3 us
    unnamed x312, local copies, waits for them, and re-layouts  19.9 us
    ppermute x14, starting transfers between devices, swap_side(): return lax.ppermute(value, 'ctx', pairs)  17.4 us
  transfers between devices with their start and end apart: 52, of which 31 were waited for; matrix products, arithmetic and copies ran while one was open for 25% of the time, Pallas kernels for 0%

profile of v1, /device:TPU:0, one launch (start us, length us, event | category | flops | bytes accessed | tf_op | source)
XLA Modules:
  0.0 559.2 jit_solution(399645155197531994)
XLA Ops:
  12.1 2.8 concatenate.134
  16.8 3.0 collective-permute-start.3
  20.0 2.6 collective-permute-done.3
  33.2 6.4 %collective-permute-done.6 = bf16[128,1024]{1,0:T(8,128)(2,1)S(1)} collective-permute-done((bf16[128,1024]{1,0:T(8,128)(2,1)S(1)}, bf16[128,1024]{1,0:T(8,128)(2,1)S(1)}, u32[]{:S(2)}, u32[]{:S(2)}) %collective-permute-start.6) | collective-permute-done | bytes 262176 | tf_op jit(solution)/shard_map/ppermute | solution.py:60
  42.0 42.0 %all-gather.3.cloned.1.call-done = bf16[1024,1408]{1,0:T(8,128)(2,1)} async-done(((bf16[128,1408]{1,0:T(8,128)(2,1)}), bf16[1024,1408]{1,0:T(8,128)(2,1)}) %all-gather.3.cloned.1.call-update) | async-done | bytes 2883600 | tf_op jit(solution)/shard_map/all_gather | solution.py:256
  86.3 3.7 fusion.204
  92.9 4.5 collective-permute-start.18
  99.4 2.5 collective-permute-start.16
  110.2 4.4 collective-permute-done.10
  114.6 9.9 %collective-permute-start.8 = (bf16[2,3,640]{2,1,0:T(4,128)(2,1)S(1)}, bf16[2,3,640]{2,1,0:T(4,128)(2,1)S(1)}, u32[]{:S(2)}, u32[]{:S(2)}) collective-permute-start(bf16[2,3,640]{2,1,0:T(4,128)(2,1)S(1)} %slice.590), channel_id=1, source_target_pairs={{0,2},{1,3},{2,4},{3,5},{4,6},{5,7},{8,10},{9,11},{10,12},{11,13},... | collective-permute-start | bytes 23048 | tf_op jit(solution)/shard_map/ppermute | solution.py:73
  132.1 5.6 collective-permute-start.13
  139.6 2.7 collective-permute-start.9
  143.5 3.0 select_reduce_fusion
  147.1 8.4 %collective-permute-done.11 = bf16[2,6,64,128]{3,2,1,0:T(8,128)(2,1)S(1)} collective-permute-done((bf16[2,6,64,128]{3,2,1,0:T(8,128)(2,1)S(1)}, bf16[2,6,64,128]{3,2,1,0:T(8,128)(2,1)S(1)}, u32[]{:S(2)}, u32[]{:S(2)}) %collective-permute-start.11) | collective-permute-done | bytes 196640 | tf_op jit(solution)/shard_map/ppermute | solution.py:73
  155.5 7.8 %collective-permute-done.9 = bf16[2,6,64,128]{3,2,1,0:T(8,128)(2,1)S(1)} collective-permute-done((bf16[2,6,64,128]{3,2,1,0:T(8,128)(2,1)S(1)}, bf16[2,6,64,128]{3,2,1,0:T(8,128)(2,1)S(1)}, u32[]{:S(2)}, u32[]{:S(2)}) %collective-permute-start.9) | collective-permute-done | bytes 196640 | tf_op jit(solution)/shard_map/ppermute | solution.py:73
  164.3 3.8 multiply_add_fusion.1
  171.8 3.6 fusion
  187.9 2.5 collective-permute-done.19
  192.3 7.9 %collective-permute-done.20 = bf16[128,1024]{1,0:T(8,128)(2,1)} collective-permute-done((bf16[128,1024]{1,0:T(8,128)(2,1)S(1)}, bf16[128,1024]{1,0:T(8,128)(2,1)}, u32[]{:S(2)}, u32[]{:S(2)}) %collective-permute-start.20) | collective-permute-done | bytes 262176 | tf_op jit(solution)/shard_map/ppermute | solution.py:60
  207.6 4.5 collective-permute-done.21
  213.4 2.5 collective-permute-done.25
  225.9 6.8 %collective-permute-done.28 = bf16[128,1024]{1,0:T(8,128)(2,1)S(1)} collective-permute-done((bf16[128,1024]{1,0:T(8,128)(2,1)S(1)}, bf16[128,1024]{1,0:T(8,128)(2,1)S(1)}, u32[]{:S(2)}, u32[]{:S(2)}) %collective-permute-start.28) | collective-permute-done | bytes 262176 | tf_op jit(solution)/shard_map/ppermute | solution.py:60
  233.5 4.3 collective-permute-done.24
  239.4 7.3 %collective-permute-done.29 = bf16[128,1024]{1,0:T(8,128)(2,1)S(1)} collective-permute-done((bf16[128,1024]{1,0:T(8,128)(2,1)S(1)}, bf16[128,1024]{1,0:T(8,128)(2,1)S(1)}, u32[]{:S(2)}, u32[]{:S(2)}) %collective-permute-start.29) | collective-permute-done | bytes 262176 | tf_op jit(solution)/shard_map/ppermute | solution.py:60
  262.7 4.7 fusion.206
  288.1 4.1 fusion.66
  296.0 2.4 fusion.193
  298.5 5.5 fusion.47
  304.0 5.7 %fusion.25 = (f32[2,6,256]{2,1,0:T(8,128)}, f32[2,6,256]{2,1,0:T(8,128)}, f32[2,6,256]{2,1,0:T(8,128)}, f32[2,256,256]{2,1,0:T(8,128)S(1)}) fusion(f32[2,6,256]{2,1,0:T(8,128)S(1)} %copy-done.116, f32[2,256,256]{2,1,0:T(8,128)S(1)} %copy-done.73, f32[2,6,256]{2,1,0:T(8,128)S(1)} %copy-done.84, pred[256,256]{1,0:T(8,128)(4,1)S(1)} %copy-done.92, ...), kind=kOutput, calls=%fused_computation.36 | convolution fusion | flops 615635968 | bytes 2748416 | tf_op jit(solution)/shard_map/transpose(jvp(bhts,bshp->bthp))/dot_general | solution.py:165
  317.7 3.8 fusion.50
  328.0 11.5 %collective-permute-done.35 = bf16[2,6,64,128]{3,2,1,0:T(8,128)(2,1)} collective-permute-done((bf16[2,6,64,128]{3,2,1,0:T(8,128)(2,1)}, bf16[2,6,64,128]{3,2,1,0:T(8,128)(2,1)}, u32[]{:S(2)}, u32[]{:S(2)}) %collective-permute-start.35) | collective-permute-done | bytes 196640 | tf_op jit(solution)/shard_map/ppermute | solution.py:73
  339.5 7.5 %collective-permute-done.34 = bf16[2,6,64,128]{3,2,1,0:T(8,128)(2,1)} collective-permute-done((bf16[2,6,64,128]{3,2,1,0:T(8,128)(2,1)}, bf16[2,6,64,128]{3,2,1,0:T(8,128)(2,1)}, u32[]{:S(2)}, u32[]{:S(2)}) %collective-permute-start.34) | collective-permute-done | bytes 196640 | tf_op jit(solution)/shard_map/ppermute | solution.py:73
  347.0 2.9 multiply_reduce_fusion.8
  349.9 2.4 copy.418
  352.3 2.7 convolution_bitcast_fusion
  355.1 2.8 multiply_reduce_fusion.5
  369.0 2.4 concatenate.165
  371.4 3.5 convolution_convert_fusion
  376.3 2.3 convolution_convert_fusion.1
  380.8 2.3 pad_maximum_fusion
  383.1 6.7 %copy.459 = bf16[1024,2048]{1,0:T(8,128)(2,1)} copy(bf16[1024,2048]{0,1:T(8,128)(2,1)} %pad_maximum_fusion) | data formatting | bytes 8388608
  389.8 4.1 fusion.207
  401.3 6.7 %collective-permute-done.41 = bf16[128,1024]{1,0:T(8,128)(2,1)S(1)} collective-permute-done((bf16[128,1024]{1,0:T(8,128)(2,1)S(1)}, bf16[128,1024]{1,0:T(8,128)(2,1)S(1)}, u32[]{:S(2)}, u32[]{:S(2)}) %collective-permute-start.41) | collective-permute-done | bytes 262176 | tf_op jit(solution)/shard_map/ppermute | solution.py:60
  408.2 43.3 %all-reduce.16 = (f32[2,1024]{1,0:T(2,128)S(1)}, f32[5,1792]{1,0:T(8,128)S(1)}, f32[3,24]{1,0:T(4,128)S(1)}, f32[1536]{0:T(1024)S(1)}) all-reduce(f32[2,1024]{1,0:T(2,128)S(1)} %pad_maximum_fusion.30, f32[5,1792]{1,0:T(8,128)S(1)} %fusion.124, f32[3,24]{1,0:T(4,128)S(1)} %dynamic_update_slice.70, ...), channel_id=1, replica_groups=mesh['dp'=4,'ctx'=8] {'dp','ctx'}, use_global_device_ids=true, to_apply=%region_20.21 | all-reduce | flops 12616 | bytes 100928 | tf_op jit(solution)/shard_map/psum | solution.py:514
  454.1 2.4 collective-permute-start.42
  460.7 3.0 collective-permute-done.44
  467.4 72.2 %reduce-scatter.7.cloned.1.call-done = bf16[128,2048]{1,0:T(8,128)(2,1)} async-done(((bf16[1024,2048]{1,0:T(8,128)(2,1)}), bf16[128,2048]{1,0:T(8,128)(2,1)}) %reduce-scatter.7.cloned.1.call-update) | async-done | bytes 524304 | tf_op jit(solution)/shard_map/reduce_scatter | solution.py:259
  543.6 2.6 collective-permute-done.45
  (645 shorter events, 182.3 us)
Async XLA Ops:
  7.2 76.8 %all-gather.3.cloned.1.call-start = ((), (), s32[]{:S(2)}) async-start(), calls=%async_computation.2 | async-start | bytes 3244032 | tf_op jit(solution)/shard_map/all_gather | solution.py:256
  16.8 5.8 %collective-permute-start.3 = (bf16[1,32,1408]{2,1,0:T(8,128)(2,1)S(1)}, bf16[1,32,1408]{2,1,0:T(8,128)(2,1)S(1)}, u32[]{:S(2)}, u32[]{:S(2)}) collective-permute-start(bf16[1,32,1408]{2,1,0:T(8,128)(2,1)S(1)} %get-tuple-element.221), channel_id=1, source_target_pairs={{0,1},{1,0},{2,3},{3,2},{4,5},{5,4},{6,7},{7,6},{8,9},{9,8},{10,11... | collective-permute-start | bytes 270344 | tf_op jit(solution)/shard_map/ppermute | solution.py:60
  19.8 2.9 collective-permute-start.4
  19.8 4.3 collective-permute-start.5
  24.8 160.6 %all-gather.5.cloned.1.call-start = ((), (), s32[]{:S(2)}) async-start(), calls=%async_computation.3 | async-start | bytes 4718592 | tf_op jit(solution)/shard_map/all_gather | solution.py:256
  25.2 14.6 %collective-permute-start = (bf16[1,32,2048]{2,1,0:T(8,128)(2,1)S(1)}, bf16[1,32,2048]{2,1,0:T(8,128)(2,1)S(1)}, u32[]{:S(2)}, u32[]{:S(2)}) collective-permute-start(bf16[1,32,2048]{2,1,0:T(8,128)(2,1)S(1)} %get-tuple-element.210), channel_id=1, source_target_pairs={{0,1},{1,0},{2,3},{3,2},{4,5},{5,4},{6,7},{7,6},{8,9},{9,8},{10,11... | collective-permute-start | bytes 393224 | tf_op jit(solution)/shard_map/ppermute | solution.py:60
  26.4 13.4 %collective-permute-start.1 = (bf16[1,32,2048]{2,1,0:T(8,128)(2,1)S(1)}, bf16[1,32,2048]{2,1,0:T(8,128)(2,1)S(1)}, u32[]{:S(2)}, u32[]{:S(2)}) collective-permute-start(bf16[1,32,2048]{2,1,0:T(8,128)(2,1)S(1)} %get-tuple-element.209), channel_id=1, source_target_pairs={{0,8},{8,0},{16,24},{24,16},{1,9},{9,1},{17,25},{25,17},{2,10},{10... | collective-permute-start | bytes 393224 | tf_op jit(solution)/shard_map/ppermute | solution.py:55
  26.9 13.0 %collective-permute-start.2 = (bf16[1,32,2048]{2,1,0:T(8,128)(2,1)S(1)}, bf16[1,32,2048]{2,1,0:T(8,128)(2,1)S(1)}, u32[]{:S(2)}, u32[]{:S(2)}) collective-permute-start(bf16[1,32,2048]{2,1,0:T(8,128)(2,1)S(1)} %get-tuple-element.208), channel_id=1, source_target_pairs={{0,9},{1,8},{2,11},{3,10},{4,13},{5,12},{6,15},{7,14},{8,1},{9,0},... | collective-permute-start | bytes 393224 | tf_op jit(solution)/shard_map/ppermute | solution.py:67
  28.5 11.1 %collective-permute-start.6 = (bf16[128,1024]{1,0:T(8,128)(2,1)S(1)}, bf16[128,1024]{1,0:T(8,128)(2,1)S(1)}, u32[]{:S(2)}, u32[]{:S(2)}) collective-permute-start(bf16[128,1024]{1,0:T(8,128)(2,1)S(1)} %copy.379), channel_id=1, source_target_pairs={{0,1},{1,0},{2,3},{3,2},{4,5},{5,4},{6,7},{7,6},{8,9},{9,8},{10,11... | collective-permute-start | bytes 786440 | tf_op jit(solution)/shard_map/ppermute | solution.py:60
  84.1 368.9 %reduce-scatter.5.cloned.1.call-start = ((), (), s32[]{:S(2)}) async-start(), calls=%async_computation.4 | async-start | bytes 3244032 | tf_op jit(solution)/shard_map/reduce_scatter | solution.py:259
  92.9 46.6 %collective-permute-start.18 = (bf16[2,256,128]{1,2,0:T(8,128)(2,1)}, bf16[2,256,128]{1,2,0:T(8,128)(2,1)}, u32[]{:S(2)}, u32[]{:S(2)}) collective-permute-start(bf16[2,256,128]{1,2,0:T(8,128)(2,1)} %pad_maximum_fusion.27), channel_id=1, source_target_pairs={{0,6},{1,7},{8,14},{9,15},{16,22},{17,23},{24,30},{25,31}} | collective-permute-start | bytes 393224 | tf_op jit(solution)/shard_map/ppermute | solution.py:73
  97.4 44.8 %collective-permute-start.17 = (bf16[2,256,128]{1,2,0:T(8,128)(2,1)}, bf16[2,256,128]{1,2,0:T(8,128)(2,1)}, u32[]{:S(2)}, u32[]{:S(2)}) collective-permute-start(bf16[2,256,128]{1,2,0:T(8,128)(2,1)} %pad_maximum_fusion.27), channel_id=1, source_target_pairs={{0,4},{1,5},{2,6},{3,7},{8,12},{9,13},{10,14},{11,15},{16,20},{17,... | collective-permute-start | bytes 393224 | tf_op jit(solution)/shard_map/ppermute | solution.py:73
  99.4 42.9 %collective-permute-start.16 = (bf16[2,256,128]{1,2,0:T(8,128)(2,1)}, bf16[2,256,128]{1,2,0:T(8,128)(2,1)}, u32[]{:S(2)}, u32[]{:S(2)}) collective-permute-start(bf16[2,256,128]{1,2,0:T(8,128)(2,1)} %pad_maximum_fusion.27), channel_id=1, source_target_pairs={{0,2},{1,3},{2,4},{3,5},{4,6},{5,7},{8,10},{9,11},{10,12},{11,13},... | collective-permute-start | bytes 393224 | tf_op jit(solution)/shard_map/ppermute | solution.py:73
  104.0 10.6 %collective-permute-start.10 = (f32[2,6]{1,0:T(2,128)S(1)}, f32[2,6]{1,0:T(2,128)S(1)}, u32[]{:S(2)}, u32[]{:S(2)}) collective-permute-start(f32[2,6]{1,0:T(2,128)S(1)} %slice_reduce_fusion.1), channel_id=1, source_target_pairs={{0,2},{1,3},{2,4},{3,5},{4,6},{5,7},{8,10},{9,11},{10,12},{11,13},... | collective-permute-start | bytes 152 | tf_op jit(solution)/shard_map/ppermute | solution.py:73
  105.3 19.1 %collective-permute-start.12 = (f32[2,6]{1,0:T(2,128)S(1)}, f32[2,6]{1,0:T(2,128)S(1)}, u32[]{:S(2)}, u32[]{:S(2)}) collective-permute-start(f32[2,6]{1,0:T(2,128)S(1)} %slice_reduce_fusion.1), channel_id=1, source_target_pairs={{0,4},{1,5},{2,6},{3,7},{8,12},{9,13},{10,14},{11,15},{16,20},{17,... | collective-permute-start | bytes 152 | tf_op jit(solution)/shard_map/ppermute | solution.py:73
  114.6 11.2 %collective-permute-start.8 = (bf16[2,3,640]{2,1,0:T(4,128)(2,1)S(1)}, bf16[2,3,640]{2,1,0:T(4,128)(2,1)S(1)}, u32[]{:S(2)}, u32[]{:S(2)}) collective-permute-start(bf16[2,3,640]{2,1,0:T(4,128)(2,1)S(1)} %slice.590), channel_id=1, source_target_pairs={{0,2},{1,3},{2,4},{3,5},{4,6},{5,7},{8,10},{9,11},{10,12},{11,13},... | collective-permute-start | bytes 23048 | tf_op jit(solution)/shard_map/ppermute | solution.py:73
  132.1 15.0 %collective-permute-start.13 = (bf16[2,6,64,128]{3,2,1,0:T(8,128)(2,1)S(1)}, bf16[2,6,64,128]{3,2,1,0:T(8,128)(2,1)S(1)}, u32[]{:S(2)}, u32[]{:S(2)}) collective-permute-start(bf16[2,6,64,128]{3,2,1,0:T(8,128)(2,1)S(1)} %convolution_convert_fusion.4), channel_id=1, source_target_pairs={{0,6},{1,7},{8,14},{9,15},{16,22},{17,23},{24,30},{25,31}} | collective-permute-start | bytes 589832 | tf_op jit(solution)/shard_map/ppermute | solution.py:73
  137.6 17.9 %collective-permute-start.11 = (bf16[2,6,64,128]{3,2,1,0:T(8,128)(2,1)S(1)}, bf16[2,6,64,128]{3,2,1,0:T(8,128)(2,1)S(1)}, u32[]{:S(2)}, u32[]{:S(2)}) collective-permute-start(bf16[2,6,64,128]{3,2,1,0:T(8,128)(2,1)S(1)} %convolution_convert_fusion.4), channel_id=1, source_target_pairs={{0,4},{1,5},{2,6},{3,7},{8,12},{9,13},{10,14},{11,15},{16,20},{17,... | collective-permute-start | bytes 589832 | tf_op jit(solution)/shard_map/ppermute | solution.py:73
  139.6 23.8 %collective-permute-start.9 = (bf16[2,6,64,128]{3,2,1,0:T(8,128)(2,1)S(1)}, bf16[2,6,64,128]{3,2,1,0:T(8,128)(2,1)S(1)}, u32[]{:S(2)}, u32[]{:S(2)}) collective-permute-start(bf16[2,6,64,128]{3,2,1,0:T(8,128)(2,1)S(1)} %convolution_convert_fusion.4), channel_id=1, source_target_pairs={{0,2},{1,3},{2,4},{3,5},{4,6},{5,7},{8,10},{9,11},{10,12},{11,13},... | collective-permute-start | bytes 589832 | tf_op jit(solution)/shard_map/ppermute | solution.py:73
  171.7 3.7 collective-permute-start.14
  175.4 8.6 %collective-permute-start.15 = (f32[512]{0:T(512)S(1)}, f32[512]{0:T(512)S(1)}, u32[]{:S(2)}, u32[]{:S(2)}) collective-permute-start(f32[512]{0:T(512)S(1)} %maximum_add_fusion), channel_id=1, source_target_pairs={{0,1},{1,0},{2,3},{3,2},{4,5},{5,4},{6,7},{7,6},{8,9},{9,8},{10,11... | collective-permute-start | bytes 6152 | tf_op jit(solution)/shard_map/ppermute | solution.py:60
  187.7 2.7 collective-permute-start.19
  191.7 8.5 %collective-permute-start.20 = (bf16[128,1024]{1,0:T(8,128)(2,1)S(1)}, bf16[128,1024]{1,0:T(8,128)(2,1)}, u32[]{:S(2)}, u32[]{:S(2)}) collective-permute-start(bf16[128,1024]{1,0:T(8,128)(2,1)S(1)} %select_convert_fusion.3), channel_id=1, source_target_pairs={{0,1},{1,0},{2,3},{3,2},{4,5},{5,4},{6,7},{7,6},{8,9},{9,8},{10,11... | collective-permute-start | bytes 786440 | tf_op jit(solution)/shard_map/ppermute | solution.py:60
  202.6 9.6 %collective-permute-start.21 = (bf16[128,1024]{1,0:T(8,128)(2,1)}, bf16[128,1024]{1,0:T(8,128)(2,1)}, u32[]{:S(2)}, u32[]{:S(2)}) collective-permute-start(bf16[128,1024]{1,0:T(8,128)(2,1)} %multiply_convert_fusion.6), channel_id=1, source_target_pairs={{0,1},{1,0},{2,3},{3,2},{4,5},{5,4},{6,7},{7,6},{8,9},{9,8},{10,11... | collective-permute-start | bytes 786440 | tf_op jit(solution)/shard_map/ppermute | solution.py:60
  206.0 9.9 %collective-permute-start.25 = (bf16[128,1024]{1,0:T(8,128)(2,1)S(1)}, bf16[128,1024]{1,0:T(8,128)(2,1)S(1)}, u32[]{:S(2)}, u32[]{:S(2)}) collective-permute-start(bf16[128,1024]{1,0:T(8,128)(2,1)S(1)} %copy.404), channel_id=1, source_target_pairs={{0,1},{1,0},{2,3},{3,2},{4,5},{5,4},{6,7},{7,6},{8,9},{9,8},{10,11... | collective-permute-start | bytes 786440 | tf_op jit(solution)/shard_map/ppermute | solution.py:60
  213.3 2.8 collective-permute-start.22
  220.6 2.7 collective-permute-start.27
  221.8 3.0 collective-permute-start.23
  223.5 9.2 %collective-permute-start.28 = (bf16[128,1024]{1,0:T(8,128)(2,1)S(1)}, bf16[128,1024]{1,0:T(8,128)(2,1)S(1)}, u32[]{:S(2)}, u32[]{:S(2)}) collective-permute-start(bf16[128,1024]{1,0:T(8,128)(2,1)S(1)} %select_convert_fusion.1), channel_id=1, source_target_pairs={{0,1},{1,0},{2,3},{3,2},{4,5},{5,4},{6,7},{7,6},{8,9},{9,8},{10,11... | collective-permute-start | bytes 786440 | tf_op jit(solution)/shard_map/ppermute | solution.py:60
  225.0 12.8 %collective-permute-start.24 = (bf16[128,1024]{1,0:T(8,128)(2,1)S(1)}, bf16[128,1024]{1,0:T(8,128)(2,1)S(1)}, u32[]{:S(2)}, u32[]{:S(2)}) collective-permute-start(bf16[128,1024]{1,0:T(8,128)(2,1)S(1)} %select_convert_fusion.2), channel_id=1, source_target_pairs={{0,1},{1,0},{2,3},{3,2},{4,5},{5,4},{6,7},{7,6},{8,9},{9,8},{10,11... | collective-permute-start | bytes 786440 | tf_op jit(solution)/shard_map/ppermute | solution.py:60
  239.0 7.8 %collective-permute-start.29 = (bf16[128,1024]{1,0:T(8,128)(2,1)S(1)}, bf16[128,1024]{1,0:T(8,128)(2,1)S(1)}, u32[]{:S(2)}, u32[]{:S(2)}) collective-permute-start(bf16[128,1024]{1,0:T(8,128)(2,1)S(1)} %get-tuple-element.168), channel_id=1, source_target_pairs={{0,1},{1,0},{2,3},{3,2},{4,5},{5,4},{6,7},{7,6},{8,9},{9,8},{10,11... | collective-permute-start | bytes 786440 | tf_op jit(solution)/shard_map/ppermute | solution.py:60
  272.3 6.0 %collective-permute-start.31 = (f32[512]{0:T(512)}, f32[512]{0:T(512)}, u32[]{:S(2)}, u32[]{:S(2)}) collective-permute-start(f32[512]{0:T(512)} %get-tuple-element.139), channel_id=1, source_target_pairs={{0,8},{8,0},{16,24},{24,16},{1,9},{9,1},{17,25},{25,17},{2,10},{10... | collective-permute-start | bytes 6152 | tf_op jit(solution)/shard_map/ppermute | solution.py:55
  280.3 7.1 %collective-permute-start.32 = (f32[512]{0:T(512)}, f32[512]{0:T(512)}, u32[]{:S(2)}, u32[]{:S(2)}) collective-permute-start(f32[512]{0:T(512)} %maximum_add_fusion.1), channel_id=1, source_target_pairs={{0,1},{1,0},{2,3},{3,2},{4,5},{5,4},{6,7},{7,6},{8,9},{9,8},{10,11... | collective-permute-start | bytes 6152 | tf_op jit(solution)/shard_map/ppermute | solution.py:60
  283.3 39.0 %collective-permute-start.39 = (bf16[2,256,128]{1,2,0:T(8,128)(2,1)}, bf16[2,256,128]{1,2,0:T(8,128)(2,1)}, u32[]{:S(2)}, u32[]{:S(2)}) collective-permute-start(bf16[2,256,128]{1,2,0:T(8,128)(2,1)} %get-tuple-element.197), channel_id=1, source_target_pairs={{6,0},{7,1},{14,8},{15,9},{22,16},{23,17},{30,24},{31,25}} | collective-permute-start | bytes 393224 | tf_op jit(solution)/shard_map/ppermute | solution.py:73
  284.6 39.2 %collective-permute-start.38 = (bf16[2,256,128]{1,2,0:T(8,128)(2,1)}, bf16[2,256,128]{1,2,0:T(8,128)(2,1)}, u32[]{:S(2)}, u32[]{:S(2)}) collective-permute-start(bf16[2,256,128]{1,2,0:T(8,128)(2,1)} %get-tuple-element.198), channel_id=1, source_target_pairs={{4,0},{5,1},{6,2},{7,3},{12,8},{13,9},{14,10},{15,11},{20,16},{21,... | collective-permute-start | bytes 393224 | tf_op jit(solution)/shard_map/ppermute | solution.py:73
  285.9 37.9 %collective-permute-start.37 = (bf16[2,256,128]{1,2,0:T(8,128)(2,1)}, bf16[2,256,128]{1,2,0:T(8,128)(2,1)}, u32[]{:S(2)}, u32[]{:S(2)}) collective-permute-start(bf16[2,256,128]{1,2,0:T(8,128)(2,1)} %get-tuple-element.196), channel_id=1, source_target_pairs={{2,0},{3,1},{4,2},{5,3},{6,4},{7,5},{10,8},{11,9},{12,10},{13,11},... | collective-permute-start | bytes 393224 | tf_op jit(solution)/shard_map/ppermute | solution.py:73
  312.8 26.7 %collective-permute-start.35 = (bf16[2,6,64,128]{3,2,1,0:T(8,128)(2,1)}, bf16[2,6,64,128]{3,2,1,0:T(8,128)(2,1)}, u32[]{:S(2)}, u32[]{:S(2)}) collective-permute-start(bf16[2,6,64,128]{3,2,1,0:T(8,128)(2,1)} %get-tuple-element.213), channel_id=1, source_target_pairs={{6,0},{7,1},{14,8},{15,9},{22,16},{23,17},{30,24},{31,25}} | collective-permute-start | bytes 589832 | tf_op jit(solution)/shard_map/ppermute | solution.py:73
  314.1 32.9 %collective-permute-start.34 = (bf16[2,6,64,128]{3,2,1,0:T(8,128)(2,1)}, bf16[2,6,64,128]{3,2,1,0:T(8,128)(2,1)}, u32[]{:S(2)}, u32[]{:S(2)}) collective-permute-start(bf16[2,6,64,128]{3,2,1,0:T(8,128)(2,1)} %get-tuple-element.214), channel_id=1, source_target_pairs={{4,0},{5,1},{6,2},{7,3},{12,8},{13,9},{14,10},{15,11},{20,16},{21,... | collective-permute-start | bytes 589832 | tf_op jit(solution)/shard_map/ppermute | solution.py:73
  322.3 24.7 %collective-permute-start.33 = (bf16[2,6,64,128]{3,2,1,0:T(8,128)(2,1)}, bf16[2,6,64,128]{3,2,1,0:T(8,128)(2,1)}, u32[]{:S(2)}, u32[]{:S(2)}) collective-permute-start(bf16[2,6,64,128]{3,2,1,0:T(8,128)(2,1)} %get-tuple-element.212), channel_id=1, source_target_pairs={{2,0},{3,1},{4,2},{5,3},{6,4},{7,5},{10,8},{11,9},{12,10},{13,11},... | collective-permute-start | bytes 589832 | tf_op jit(solution)/shard_map/ppermute | solution.py:73
  359.7 8.2 %collective-permute-start.36 = (f32[2,3,640]{2,1,0:T(4,128)}, f32[2,3,640]{2,1,0:T(4,128)}, u32[]{:S(2)}, u32[]{:S(2)}) collective-permute-start(f32[2,3,640]{2,1,0:T(4,128)} %pad_add_fusion.1), channel_id=1, source_target_pairs={{2,0},{3,1},{4,2},{5,3},{6,4},{7,5},{10,8},{11,9},{12,10},{13,11},... | collective-permute-start | bytes 46088 | tf_op jit(solution)/shard_map/ppermute | solution.py:73
  375.0 164.6 %reduce-scatter.7.cloned.1.call-start = ((), (), s32[]{:S(2)}) async-start(), calls=%async_computation.5 | async-start | bytes 4718592 | tf_op jit(solution)/shard_map/reduce_scatter | solution.py:259
  395.1 3.0 collective-permute-start.40
  399.6 8.4 %collective-permute-start.41 = (bf16[128,1024]{1,0:T(8,128)(2,1)S(1)}, bf16[128,1024]{1,0:T(8,128)(2,1)S(1)}, u32[]{:S(2)}, u32[]{:S(2)}) collective-permute-start(bf16[128,1024]{1,0:T(8,128)(2,1)S(1)} %select_convert_fusion), channel_id=1, source_target_pairs={{0,1},{1,0},{2,3},{3,2},{4,5},{5,4},{6,7},{7,6},{8,9},{9,8},{10,11... | collective-permute-start | bytes 786440 | tf_op jit(solution)/shard_map/ppermute | solution.py:60
  454.1 5.4 collective-permute-start.42
  459.4 4.3 collective-permute-start.44
  540.8 5.5 collective-permute-start.45
  543.0 3.3 collective-permute-start.46
  543.0 5.5 collective-permute-start.47
  (149 other events, 1350.9 us)
Sparse Core Ops, SparseCore 0:
  24.9 59.0 all-gather.2
  86.7 90.1 all-gather.4
  375.1 73.6 reduce-scatter.4
  452.3 87.2 reduce-scatter.6

commit v2 on v1

v2 whole, which is shorter than its diff:
```python
import jax
import jax.numpy as jnp
from jax import lax
from jax.experimental import pallas as pl
from jax.experimental.pallas import tpu as pltpu
from jax.sharding import PartitionSpec as P

D = 1024
DSSM = 1536
MH = 24
MP = 64
NS = 128
KW = 4
AH = 8
KVH = 2
HD = 64
FF = 2048
CONV = DSSM + 2 * NS

TP = 4
SW = DSSM // TP
SH = MH // TP
QW = AH * HD // TP
FW = FF // TP
MIXW = SW + 2 * NS
STEP_AT = MIXW + QW + 2 * HD
VEC = 16
WIDE = 1024

EPSILON = 1e-05
ROPE_BASE = 100000000000.0
HIGHEST = lax.Precision.HIGHEST
NEGATIVE = -1e30
BOTH = ("dp", "ctx")
bf16 = jnp.bfloat16
f32 = jnp.float32


def forward_product(left, right):
    return jnp.dot(left, right, preferred_element_type=f32)


def input_product(upstream, weight):
    return lax.dot_general(
        upstream, weight, (((1,), (1,)), ((), ())), preferred_element_type=f32
    )


def swap_core(value):
    pairs = [(i, i ^ 1) for i in range(lax.axis_size("dp"))]
    return lax.ppermute(value, "dp", pairs)


def swap_side(value):
    pairs = [(i, i ^ 1) for i in range(lax.axis_size("ctx"))]
    return lax.ppermute(value, "ctx", pairs)


def swap_both(value):
    blocks = lax.axis_size("ctx")
    count = lax.axis_size("dp") * blocks
    pairs = [(i, ((i // blocks) ^ 1) * blocks + ((i % blocks) ^ 1)) for i in range(count)]
    return lax.ppermute(value, BOTH, pairs)


def move_spans(value, by):
    blocks = lax.axis_size("ctx")
    pairs = [(i, i + 2 * by) for i in range(blocks) if 0 <= i + 2 * by < blocks]
    return lax.ppermute(value, "ctx", pairs)


def group_gather(value, side):
    other = swap_side(value)
    first = side == 0
    mine = jnp.concatenate([jnp.where(first, value, other), jnp.where(first, other, value)], 0)
    return jnp.concatenate([mine, swap_core(mine)], 0)


def group_scatter(partial, side):
    span = partial.shape[0] // 2
    rows = span // 2
    mine = partial[:span] + swap_core(partial[span:])
    first = side == 0
    keep = jnp.where(first, mine[:rows], mine[rows:])
    send = jnp.where(first, mine[rows:], mine[:rows]).astype(bf16)
    return keep + swap_side(send).astype(f32)


def group_sum(value):
    span = value.shape[0] // 2
    other = swap_core(value)
    value = value + jnp.concatenate([other[span:], other[:span]], 0)
    return value + swap_side(value)


def group_swap(parts, rank):
    def at(index):
        return lax.dynamic_index_in_dim(parts, index, 0, keepdims=True)

    pieces = (
        (rank, at(rank)),
        (rank ^ 1, swap_side(at(rank ^ 1))),
        (rank ^ 2, swap_core(at(rank ^ 2))),
        (rank ^ 3, swap_both(at(rank ^ 3))),
    )
    result = jnp.zeros_like(parts)
    for index, piece in pieces:
        result = lax.dynamic_update_slice_in_dim(result, piece, index, 0)
    return result


def call(body, grid, in_specs, out_specs, out_shape, scratch=()):
    return pl.pallas_call(
        body,
        grid=grid,
        in_specs=in_specs,
        out_specs=out_specs,
        out_shape=out_shape,
        scratch_shapes=list(scratch),
        compiler_params=pltpu.CompilerParams(vmem_limit_bytes=48 * 1024 * 1024),
    )


def shape(*dims, dtype=f32):
    return jax.ShapeDtypeStruct(dims, dtype)


def row_block(rows, width):
    return pl.BlockSpec((rows, width), lambda b: (b, 0))


def seq_block(*dims):
    return pl.BlockSpec((1,) + dims, lambda b: (b,) + (0,) * len(dims))


def fixed(*dims):
    return pl.BlockSpec(dims, lambda b: (0,) * len(dims))


SCALAR = pl.BlockSpec(memory_space=pltpu.SMEM)


def product(left, right, left_dim=1, right_dim=0):
    return lax.dot_general(
        left, right, (((left_dim,), (right_dim,)), ((), ())), preferred_element_type=f32
    )


def halves(value):
    high = value.astype(bf16)
    return high, (value - high.astype(f32)).astype(bf16)


def fine_product(left, right, left_dim=1, right_dim=0):
    left_high, left_low = halves(left)
    right_high, right_low = halves(right)
    return (
        product(left_high, right_high, left_dim, right_dim)
        + product(left_high, right_low, left_dim, right_dim)
        + product(left_low, right_high, left_dim, right_dim)
    )


def head_mask():
    row = lax.broadcasted_iota(jnp.int32, (128, SW), 0)
    column = lax.broadcasted_iota(jnp.int32, (128, SW), 1)
    return jnp.where(column // MP == row, 1.0, 0.0).astype(bf16)


def spread_heads(value, mask):
    high, low = halves(value)
    return product(high, mask) + product(low, mask)


def sum_heads(value, mask):
    high, low = halves(value)
    return product(high, mask, 1, 1) + product(low, mask, 1, 1)


def rope_tables(positions):
    ladder = jnp.arange(HD // 2, dtype=f32)
    rates = ROPE_BASE ** (-2.0 * ladder / HD)
    angles = positions.astype(f32)[:, None] * rates[None, :]
    cosine, sine = jnp.cos(angles), jnp.sin(angles)
    return (
        jnp.concatenate([cosine] * 4, 1),
        jnp.concatenate([-sine, sine, -sine, sine], 1),
    )


def turn(value, cosine, sine):
    lane = lax.broadcasted_iota(jnp.int32, value.shape, 1)
    half = HD // 2
    other = jnp.where(
        lane % HD < half, pltpu.roll(value, 128 - half, 1), pltpu.roll(value, half, 1)
    )
    return value * cosine + other * sine


def turn_first(value, cosine, sine):
    lane = lax.broadcasted_iota(jnp.int32, value.shape, 1)
    return jnp.where(lane < HD, turn(value, cosine, sine), value)


def project_kernel(
    hidden, gain, weight, cosine, sine, normed_out, mix_out, query_out, key_value_out, step_out
):
    wide = hidden[...].astype(f32)
    scale = lax.rsqrt(jnp.mean(wide * wide, -1, keepdims=True) + EPSILON)
    normed = (wide * scale * gain[...]).astype(bf16)
    normed_out[...] = normed
    rows = product(normed, weight[...])
    mix_out[...] = rows[:, :MIXW].astype(bf16)
    at = MIXW
    query_out[...] = turn(rows[:, at : at + QW], cosine[...], sine[...]).astype(bf16)
    at += QW
    pair = turn_first(rows[:, at : at + 2 * HD], cosine[...], sine[...])
    key_value_out[...] = pair.astype(bf16)
    tail = rows[:, STEP_AT:]
    lane = lax.broadcasted_iota(jnp.int32, tail.shape, 1)
    step_out[...] = jnp.where(lane < SH, tail, 0.0)


def project(hidden, gain, weight, cosine, sine):
    count = hidden.shape[0]
    span = count // 2
    return call(
        project_kernel,
        (2,),
        [
            row_block(span, D),
            fixed(1, D),
            fixed(D, WIDE),
            fixed(span, 128),
            fixed(span, 128),
        ],
        [
            row_block(span, D),
            row_block(span, MIXW),
            row_block(span, QW),
            row_block(span, 128),
            row_block(span, 128),
        ],
        [
            shape(count, D, dtype=bf16),
            shape(count, MIXW, dtype=bf16),
            shape(count, QW, dtype=bf16),
            shape(count, 128, dtype=bf16),
            shape(count, 128),
        ],
    )(hidden, gain, weight, cosine, sine)


def visible_keys(span, keys, at):
    query = lax.broadcasted_iota(jnp.int32, (span, keys), 0)
    key = lax.broadcasted_iota(jnp.int32, (span, keys), 1)
    return (key < span) & (key <= query) | (key >= span) & (key < (at + 1) * span)


def attend_kernel(at, query, key_value, attended_out, total_out):
    span, keys = query.shape[0], key_value.shape[1]
    visible = visible_keys(span, keys, at[0])
    pair = key_value[0]
    for h in range(QW // HD):
        part = slice(h * HD, (h + 1) * HD)
        scores = product(query[:, part], pair[:, :HD], 1, 1) * HD ** (-0.5)
        scores = jnp.where(visible, scores, NEGATIVE)
        peak = jnp.max(scores, -1, keepdims=True)
        weights = jnp.exp(scores - peak)
        total = jnp.sum(weights, -1, keepdims=True)
        summed = product(weights.astype(bf16), pair[:, HD:])
        attended_out[:, part] = (summed / total).astype(bf16)
        total_out[:, part] = jnp.broadcast_to(peak + jnp.log(total), (span, HD))


def attend(at, query, key_values):
    count = query.shape[0]
    span = count // 2
    return call(
        attend_kernel,
        (2,),
        [SCALAR, row_block(span, QW), seq_block(*key_values.shape[1:])],
        [row_block(span, QW), row_block(span, QW)],
        [shape(count, QW, dtype=bf16), shape(count, QW)],
    )(at, query, key_values)


def attend_back_kernel(
    at, query, key_value, attended, log_total, back, cosine, sine, query_out, own_out, other_out
):
    span, keys = query.shape[0], key_value.shape[1]
    scale = HD ** (-0.5)
    visible = visible_keys(span, keys, at[0])
    pair = key_value[0]
    back_pair = jnp.zeros((keys, 2 * HD), f32)
    turned = []
    for h in range(QW // HD):
        part = slice(h * HD, (h + 1) * HD)
        head = query[:, part]
        upstream = back[:, part]
        delta = jnp.sum(
            upstream.astype(f32) * attended[:, part].astype(f32), -1, keepdims=True
        )
        scores = product(head, pair[:, :HD], 1, 1) * scale
        chance = jnp.where(visible, jnp.exp(scores - log_total[:, part][:, :1]), 0.0)
        back_chance = product(upstream, pair[:, HD:], 1, 1)
        back_scores = (chance * (back_chance - delta) * scale).astype(bf16)
        turned.append(product(back_scores, pair[:, :HD]))
        back_pair = back_pair + jnp.concatenate(
            [product(back_scores, head, 0, 0), product(chance.astype(bf16), upstream, 0, 0)], 1
        )
    query_out[...] = turn(jnp.concatenate(turned, 1), cosine[...], -sine[...]).astype(bf16)
    own_out[0] = back_pair[:span]
    other_out[0] = back_pair[span:].astype(bf16)


def attend_back(at, query, key_values, attended, log_total, back, cosine, sine):
    count = query.shape[0]
    span = count // 2
    keys = key_values.shape[1]
    return call(
        attend_back_kernel,
        (2,),
        [SCALAR, row_block(span, QW), seq_block(keys, 2 * HD)]
        + [row_block(span, QW)] * 3
        + [fixed(span, 128)] * 2,
        [row_block(span, QW), seq_block(span, 2 * HD), seq_block(keys - span, 2 * HD)],
        [
            shape(count, QW, dtype=bf16),
            shape(2, span, 2 * HD),
            shape(2, keys - span, 2 * HD, dtype=bf16),
        ],
    )(at, query, key_values, attended, log_total, back, cosine, sine)


LEAD = 8


def extend(scratch, rim, mix):
    scratch[0:LEAD] = rim[0].astype(f32)
    scratch[LEAD:] = mix[...].astype(f32)


def prep_kernel(rim, mix, step, taps, heads, conv_out, prep_out, turned_out, message_out, ext):
    rows = mix.shape[0]
    extend(ext, rim, mix)
    conv = taps[KW : KW + 1] + taps[0:1] * ext[pl.ds(LEAD - KW + 1, rows)]
    for tap in range(1, KW):
        conv = conv + taps[tap : tap + 1] * ext[pl.ds(LEAD - KW + 1 + tap, rows)]
    conv = conv / (1.0 + jnp.exp(-conv))
    conv_out[...] = conv
    lane = lax.broadcasted_iota(jnp.int32, step.shape, 1)
    raw = step[...] + heads[0:1]
    steps = jnp.maximum(raw, 0.0) + jnp.log1p(jnp.exp(-jnp.abs(raw)))
    steps = jnp.where(lane < SH, steps, 0.0)
    rate = -jnp.exp(heads[1:2]) * steps
    below = lax.broadcasted_iota(jnp.int32, (rows, rows), 0)
    along = lax.broadcasted_iota(jnp.int32, (rows, rows), 1)
    lower = jnp.where(below >= along, 1.0, 0.0)
    curve = lax.dot_general(
        lower, rate, (((1,), (0,)), ((), ())), precision=HIGHEST, preferred_element_type=f32
    )
    prep_out[:, :128] = steps
    prep_out[:, 128:] = curve
    turned_out[0, :8] = steps.T[:8]
    turned_out[0, 8:] = curve.T[:8]
    last = curve[rows - 1 : rows]
    weights = jnp.exp(last - curve) * steps
    mask = head_mask()
    scaled = spread_heads(weights, mask) * conv[:, :SW]
    state = fine_product(scaled, conv[:, SW : SW + NS], 0, 0)
    message_out[0, :SW] = state.astype(bf16)
    high = last.astype(bf16)
    low = (last - high.astype(f32)).astype(bf16)
    row = lax.broadcasted_iota(jnp.int32, (16, 128), 0)
    tail = jnp.where(row == 0, high.astype(f32), jnp.where(row == 1, low.astype(f32), 0.0))
    message_out[0, SW:] = tail.astype(bf16)


def prep(rim, mix, step, taps, heads):
    count = mix.shape[0]
    rows = count // 2
    return call(
        prep_kernel,
        (2,),
        [
            seq_block(LEAD, MIXW),
            row_block(rows, MIXW),
            row_block(rows, 128),
            fixed(8, MIXW),
            fixed(8, 128),
        ],
        [
            row_block(rows, MIXW),
            row_block(rows, 256),
            seq_block(16, rows),
            seq_block(SW + 16, NS),
        ],
        [
            shape(count, MIXW),
            shape(count, 256),
            shape(2, 16, rows),
            shape(2, SW + 16, NS, dtype=bf16),
        ],
        [pltpu.VMEM((LEAD + rows, MIXW), f32)],
    )(rim, mix, step, taps, heads)


def head_column(tail):
    row = lax.broadcasted_iota(jnp.int32, (SW, 128), 0)
    lane = lax.broadcasted_iota(jnp.int32, (SW, 128), 1)
    return jnp.sum(jnp.where(row // MP == lane, tail, 0.0), 1, keepdims=True)


def decay_of(message, at):
    return message[0, at : at + 1].astype(f32) + message[0, at + 1 : at + 2].astype(f32)


def scan_kernel(
    parts, normed, gate_weight, conv, prep, turned, skip, *refs
):
    messages = refs[:parts]
    gate_out, mixed_out, state_out, square_out = refs[parts:]
    rows = conv.shape[0]
    gate = product(normed[...], gate_weight[...])
    gate_out[...] = gate
    between = jnp.zeros((1, 128), f32)
    state = jnp.zeros((SW, NS), f32)
    for message in messages:
        state = state + jnp.exp(head_column(between)) * message[0, :SW].astype(f32)
        between = between + decay_of(message, SW)
    state_out[0] = state
    entry = conv[:, SW : SW + NS]
    readout = conv[:, SW + NS :]
    meeting = fine_product(readout, entry, 1, 1)
    below = lax.broadcasted_iota(jnp.int32, (rows, rows), 0)
    along = lax.broadcasted_iota(jnp.int32, (rows, rows), 1)
    causal = below >= along
    meeting = jnp.where(causal, meeting, 0.0)
    parts_out = []
    for h in range(SH):
        spread = prep[:, 128 + h : 129 + h] - turned[0, 8 + h : 9 + h]
        mixing = jnp.exp(jnp.where(causal, spread, 0.0)) * meeting * turned[0, h : h + 1]
        signal = conv[:, MP * h : MP * (h + 1)].astype(bf16)
        parts_out.append(product(mixing.astype(bf16), signal))
    signal = conv[:, :SW]
    carried = fine_product(readout, state, 1, 1)
    grown = spread_heads(jnp.exp(prep[:, 128:]), head_mask())
    mixed = jnp.concatenate(parts_out, 1) + carried * grown + skip[...] * signal
    mixed_out[...] = mixed
    gated = mixed * gate / (1.0 + jnp.exp(-gate))
    square_out[...] = jnp.broadcast_to(jnp.sum(gated * gated, 1, keepdims=True), (rows, 128))


def scan(normed, feed, conv, prepared, turned, skip, messages):
    count = conv.shape[0]
    rows = count // 2
    return call(
        lambda *refs: scan_kernel(len(messages), *refs),
        (2,),
        [
            row_block(rows, D),
            fixed(D, SW),
            row_block(rows, MIXW),
            row_block(rows, 256),
            seq_block(16, rows),
            fixed(1, SW),
        ]
        + [seq_block(SW + 16, NS)] * len(messages),
        [
            row_block(rows, SW),
            row_block(rows, SW),
            seq_block(SW, NS),
            row_block(rows, 128),
        ],
        [shape(count, SW), shape(count, SW), shape(2, SW, NS), shape(count, 128)],
    )(normed, feed, conv, prepared, turned, skip, *messages)


def scan_back_kernel(parts, back, conv, prep, turned, skip, state, *refs):
    tails = refs[:parts]
    conv_out, prep_out, skip_out = refs[parts : parts + 3]
    sent_out = refs[parts + 3 :]
    rows = conv.shape[0]
    mask = head_mask()
    entry = conv[:, SW : SW + NS]
    readout = conv[:, SW + NS :]
    signal = conv[:, :SW]
    upstream = back[...]
    meeting = fine_product(readout, entry, 1, 1)
    below = lax.broadcasted_iota(jnp.int32, (rows, rows), 0)
    along = lax.broadcasted_iota(jnp.int32, (rows, rows), 1)
    causal = below >= along
    back_meeting = jnp.zeros((rows, rows), f32)
    lane = lax.broadcasted_iota(jnp.int32, (rows, 128), 1)
    place = lax.broadcasted_iota(jnp.int32, (8, rows), 0)
    back_steps = jnp.zeros((8, rows), f32)
    curve_along = jnp.zeros((8, rows), f32)
    back_curve = jnp.zeros((rows, 128), f32)
    back_signal = []
    for h in range(SH):
        part = slice(MP * h, MP * (h + 1))
        spread = prep[:, 128 + h : 129 + h] - turned[0, 8 + h : 9 + h]
        decay = jnp.where(causal, jnp.exp(jnp.where(causal, spread, 0.0)), 0.0)
        step = turned[0, h : h + 1]
        head_back = upstream[:, part].astype(bf16)
        back_mixing = product(head_back, signal[:, part].astype(bf16), 1, 1) * decay
        back_meeting = back_meeting + back_mixing * step
        scaled = back_mixing * meeting
        down = jnp.sum(scaled, 0, keepdims=True)
        across = jnp.sum(scaled * step, 1, keepdims=True)
        back_steps = jnp.where(place == h, down, back_steps)
        curve_along = jnp.where(place == h, -down * step, curve_along)
        back_curve = jnp.where(lane == h, across, back_curve)
        mixing = (decay * meeting * step).astype(bf16)
        back_signal.append(product(mixing, head_back, 0, 0))
    fold = jnp.concatenate([back_steps, curve_along, jnp.zeros((112, rows), f32)], 0).T
    grown = spread_heads(jnp.exp(prep[:, 128:]), mask)
    back_carried = upstream * grown
    carried = fine_product(readout, state[0], 1, 1)
    back_curve = back_curve + sum_heads(back_carried * carried, mask)
    back_curve = back_curve + jnp.where(lane < SH, pltpu.roll(fold, 120, 1), 0.0)
    conv_out[:, :SW] = jnp.concatenate(back_signal, 1) + skip[...] * upstream
    conv_out[:, SW : SW + NS] = fine_product(back_meeting, readout, 0, 0)
    conv_out[:, SW + NS :] = fine_product(back_meeting, entry) + fine_product(
        back_carried, state[0]
    )
    prep_out[:, :128] = jnp.where(lane < SH, fold, 0.0)
    prep_out[:, 128:] = back_curve
    back_skip = jnp.sum(upstream * signal, 0, keepdims=True)
    skip_out[0] = jnp.broadcast_to(sum_heads(jnp.broadcast_to(back_skip, (8, SW)), mask), (8, 128))
    back_state = fine_product(back_carried, readout, 0, 0)
    between = jnp.zeros((1, 128), f32)
    for tail, sent in zip(tails, sent_out):
        sent[0] = (jnp.exp(head_column(between)) * back_state).astype(bf16)
        between = between + decay_of(tail, 0)


def scan_back(back, conv, prepared, turned, skip, state, messages):
    count = conv.shape[0]
    rows = count // 2
    tail = pl.BlockSpec((1, 16, NS), lambda b: (b, SW // 16, 0))
    return call(
        lambda *refs: scan_back_kernel(len(messages), *refs),
        (2,),
        [
            row_block(rows, SW),
            row_block(rows, MIXW),
            row_block(rows, 256),
            seq_block(16, rows),
            fixed(1, SW),
            seq_block(SW, NS),
        ]
        + [tail] * len(messages),
        [row_block(rows, MIXW), row_block(rows, 256), seq_block(8, 128)]
        + [seq_block(SW, NS)] * len(messages),
        [shape(count, MIXW), shape(count, 256), shape(2, 8, 128)]
        + [shape(2, SW, NS, dtype=bf16)] * len(messages),
    )(back, conv, prepared, turned, skip, state, *messages)


def prep_back_kernel(
    parts,
    rim,
    mix,
    step,
    taps,
    heads,
    conv,
    prep,
    state,
    back_conv,
    back_prep,
    back_skip,
    *refs,
):
    received = refs[:parts]
    mix_out, step_out, rim_out, tap_out, head_out, ext, padded = refs[parts:]
    rows = mix.shape[0]
    mask = head_mask()
    next_back = jnp.zeros((SW, NS), f32)
    for piece in received:
        next_back = next_back + piece[0].astype(f32)
    steps, curve = prep[:, :128], prep[:, 128:]
    last = curve[rows - 1 : rows]
    decay = jnp.exp(last - curve)
    wide = spread_heads(decay * steps, mask)
    signal = conv[:, :SW]
    entry = conv[:, SW : SW + NS]
    back_scaled = fine_product(entry, next_back, 1, 1)
    back_weights = sum_heads(back_scaled * signal, mask)
    both = back_weights * decay
    back_steps = back_prep[:, :128] + both
    weighed = both * steps
    whole = jnp.sum(next_back * state[0], 1, keepdims=True)
    row = lax.broadcasted_iota(jnp.int32, (SW, 128), 0)
    lane = lax.broadcasted_iota(jnp.int32, (SW, 128), 1)
    whole = jnp.sum(jnp.where(row // MP == lane, whole, 0.0), 0, keepdims=True) * jnp.exp(last)
    at_last = lax.broadcasted_iota(jnp.int32, (rows, 128), 0) == rows - 1
    back_curve = back_prep[:, 128:] - weighed
    back_curve = back_curve + jnp.where(
        at_last, jnp.sum(weighed, 0, keepdims=True) + whole, 0.0
    )
    below = lax.broadcasted_iota(jnp.int32, (rows, rows), 0)
    along = lax.broadcasted_iota(jnp.int32, (rows, rows), 1)
    upper = jnp.where(below <= along, 1.0, 0.0)
    back_rate = lax.dot_general(
        upper, back_curve, (((1,), (0,)), ((), ())), precision=HIGHEST, preferred_element_type=f32
    )
    pace = -jnp.exp(heads[1:2])
    back_decay = jnp.sum(back_rate * pace * steps, 0, keepdims=True)
    raw = step[...] + heads[0:1]
    back_steps = (back_steps + back_rate * pace) / (1.0 + jnp.exp(-raw))
    wide_lane = lax.broadcasted_iota(jnp.int32, (rows, 128), 1)
    back_steps = jnp.where(wide_lane < SH, back_steps, 0.0)
    step_out[...] = back_steps
    place = lax.broadcasted_iota(jnp.int32, (8, 128), 0)
    total = jnp.where(place == 0, jnp.sum(back_steps, 0, keepdims=True), 0.0)
    total = jnp.where(place == 1, back_decay, total)
    head_out[0] = jnp.where(place == 2, back_skip[0], total)

    extend(ext, rim, mix)
    before = taps[KW : KW + 1] + taps[0:1] * ext[pl.ds(LEAD - KW + 1, rows)]
    for tap in range(1, KW):
        before = before + taps[tap : tap + 1] * ext[pl.ds(LEAD - KW + 1 + tap, rows)]
    sigmoid = 1.0 / (1.0 + jnp.exp(-before))
    slope = sigmoid * (1.0 + before * (1.0 - sigmoid))
    scaled = wide * signal
    upstream = jnp.concatenate(
        [
            back_conv[:, :SW] + back_scaled * wide,
            back_conv[:, SW : SW + NS] + fine_product(scaled, next_back),
            back_conv[:, SW + NS :],
        ],
        1,
    )
    back = upstream * slope
    place = lax.broadcasted_iota(jnp.int32, (8, MIXW), 0)
    sums = jnp.where(place == KW, jnp.sum(back, 0, keepdims=True), 0.0)
    for tap in range(KW):
        moved = jnp.sum(back * ext[pl.ds(LEAD - KW + 1 + tap, rows)], 0, keepdims=True)
        sums = jnp.where(place == tap, moved, sums)
    tap_out[0] = sums
    padded[0:LEAD] = jnp.zeros((LEAD, MIXW), f32)
    padded[LEAD : LEAD + rows] = back
    padded[LEAD + rows :] = jnp.zeros((LEAD, MIXW), f32)
    result = taps[KW - 1 : KW] * back
    first = jnp.zeros((LEAD, MIXW), f32)
    for tap in range(KW):
        if tap < KW - 1:
            result = result + taps[tap : tap + 1] * padded[pl.ds(LEAD + KW - 1 - tap, rows)]
        first = first + taps[tap : tap + 1] * padded[pl.ds(LEAD - tap, LEAD)]
    mix_out[...] = result
    rim_out[0] = jnp.where(place < KW - 1, first, 0.0)


def prep_back(rim, mix, step, taps, heads, conv, prepared, state, back_conv, back_prep, back_skip, received):
    count = mix.shape[0]
    rows = count // 2
    return call(
        lambda *refs: prep_back_kernel(len(received), *refs),
        (2,),
        [
            seq_block(LEAD, MIXW),
            row_block(rows, MIXW),
            row_block(rows, 128),
            fixed(8, MIXW),
            fixed(8, 128),
            row_block(rows, MIXW),
            row_block(rows, 256),
            seq_block(SW, NS),
            row_block(rows, MIXW),
            row_block(rows, 256),
            seq_block(8, 128),
        ]
        + [seq_block(SW, NS)] * len(received),
        [
            row_block(rows, MIXW),
            row_block(rows, 128),
            seq_block(LEAD, MIXW),
            seq_block(8, MIXW),
            seq_block(8, 128),
        ],
        [
            shape(count, MIXW),
            shape(count, 128),
            shape(2, LEAD, MIXW),
            shape(2, 8, MIXW),
            shape(2, 8, 128),
        ],
        [
            pltpu.VMEM((LEAD + rows, MIXW), f32),
            pltpu.VMEM((rows + 2 * LEAD, MIXW), f32),
        ],
    )(
        rim,
        mix,
        step,
        taps,
        heads,
        conv,
        prepared,
        state,
        back_conv,
        back_prep,
        back_skip,
        *received,
    )


def assemble_kernel(parts, gate, mix, rim, step, query, own, cosine, sine, *refs):
    received, out = refs[:parts], refs[parts]
    rows = mix.shape[0]
    out[:, :SW] = gate[...]
    mixed = slice(SW, SW + MIXW)
    out[:, mixed] = mix[...].astype(bf16)
    tail = mix[rows - 16 :]
    returned = jnp.concatenate([jnp.zeros((16 - LEAD, MIXW), f32), rim[0]], 0)
    tail = tail + pltpu.roll(returned, LEAD - KW + 1, 0)
    out[rows - 16 :, mixed] = tail.astype(bf16)
    at = SW + MIXW
    out[:, at : at + QW] = query[...]
    pair = own[0]
    for piece in received:
        pair = pair + piece[0].astype(f32)
    at += QW
    out[:, at : at + 2 * HD] = turn_first(pair, cosine[...], -sine[...]).astype(bf16)
    out[:, SW + STEP_AT :] = step[...].astype(bf16)


def assemble(gate, mix, rim, step, query, own, received, cosine, sine):
    count = mix.shape[0]
    rows = count // 2
    return call(
        lambda *refs: assemble_kernel(len(received), *refs),
        (2,),
        [
            row_block(rows, SW),
            row_block(rows, MIXW),
            seq_block(LEAD, MIXW),
            row_block(rows, 128),
            row_block(rows, QW),
            seq_block(rows, 2 * HD),
            fixed(rows, 128),
            fixed(rows, 128),
        ]
        + [seq_block(rows, 2 * HD)] * len(received),
        row_block(rows, SW + WIDE),
        shape(count, SW + WIDE, dtype=bf16),
    )(gate, mix, rim, step, query, own, cosine, sine, *received)


def sums_kernel(first_left, first_right, second_left, second_right, out):
    width = first_right.shape[1]
    out[:, :width] = product(first_left[...], first_right[...], 0, 0).astype(bf16)
    out[:, width:] = product(second_left[...], second_right[...], 0, 0).astype(bf16)


def weight_sums(first_left, first_right, second_left, second_right):
    count = first_left.shape[0]
    wide, more = first_right.shape[1], second_right.shape[1]
    rows = 256
    left = pl.BlockSpec((count, rows), lambda b: (0, b))
    return call(
        sums_kernel,
        (D // rows,),
        [left, fixed(count, wide), left, fixed(count, more)],
        row_block(rows, wide + more),
        shape(D, wide + more, dtype=bf16),
    )(first_left, first_right, second_left, second_right)


def local(
    tokens,
    out_cotangent,
    input_gain,
    mamba_gate_weight,
    mamba_mix_weight,
    mamba_step_weight,
    conv_kernel,
    conv_offset,
    step_offset,
    decay_log,
    skip_scale,
    mamba_norm_gain,
    mamba_out_weight,
    query_weight,
    key_weight,
    value_weight,
    attention_out_weight,
    ffn_gain,
    feed_gate_weight,
    feed_up_weight,
    feed_down_weight,
):
    rows = tokens.shape[1]
    span = 2 * rows
    count = 2 * span
    pairs, spans = lax.axis_size("dp") // 2, lax.axis_size("ctx") // 2
    devices = 4 * pairs * spans
    dp_at, ctx_at = lax.axis_index("dp"), lax.axis_index("ctx")
    side, span_at = ctx_at % 2, ctx_at // 2
    rank = (dp_at % 2) * 2 + side
    part = D // devices
    conv_part = CONV // devices
    gain_part = DSSM // devices
    groups = [
        [(y * 2 + c) * 2 * spans + z * 2 + x for y in range(pairs) for z in range(spans)]
        for c in range(2)
        for x in range(2)
    ]

    def order(value):
        lead = value.shape[:-1]
        value = value.reshape(*lead, pairs, 2, spans, 2 * part)
        return jnp.swapaxes(value, -3, -2).reshape(*lead, D)

    def disorder(value):
        lead = value.shape[:-1]
        value = value.reshape(*lead, pairs, spans, 2, 2 * part)
        return jnp.swapaxes(value, -3, -2).reshape(*lead, D)

    def gather(value):
        return lax.all_gather(value, BOTH, axis=0, tiled=True, axis_index_groups=groups)

    def scatter(value):
        return lax.psum_scatter(
            value, BOTH, scatter_dimension=0, tiled=True, axis_index_groups=groups
        )

    vector = jnp.concatenate(
        [
            input_gain,
            ffn_gain,
            conv_kernel.reshape(-1),
            conv_offset,
            mamba_norm_gain,
        ]
    )
    vector = jnp.pad(vector, (0, part * VEC - vector.shape[0])).reshape(part, VEC)

    def mixer_part(s):
        kv = s // 2
        return jnp.concatenate(
            [
                mamba_mix_weight[:, SW * s : SW * (s + 1)],
                mamba_mix_weight[:, DSSM:],
                query_weight[:, QW * s : QW * (s + 1)],
                key_weight[:, HD * kv : HD * (kv + 1)],
                value_weight[:, HD * kv : HD * (kv + 1)],
                mamba_step_weight[:, SH * s : SH * (s + 1)],
                vector,
                jnp.zeros((part, WIDE - STEP_AT - SH - VEC), bf16),
            ],
            1,
        )

    mamba_out_turned = mamba_out_weight.T
    attention_out_turned = attention_out_weight.T
    feed_down_turned = feed_down_weight.T

    def feed_part(s):
        return jnp.concatenate(
            [
                mamba_gate_weight[:, SW * s : SW * (s + 1)],
                mamba_out_turned[:, SW * s : SW * (s + 1)],
                attention_out_turned[:, QW * s : QW * (s + 1)],
                feed_gate_weight[:, FW * s : FW * (s + 1)],
                feed_up_weight[:, FW * s : FW * (s + 1)],
                feed_down_turned[:, FW * s : FW * (s + 1)],
            ],
            1,
        )

    mixer_own = group_swap(jnp.stack([mixer_part(s) for s in range(TP)]), rank)
    mixer = gather(mixer_own.reshape(TP * part, WIDE))
    feed_own = group_swap(jnp.stack([feed_part(s) for s in range(TP)]), rank)
    own_low = order(tokens[0])
    own_hidden = own_low.astype(f32)
    own_scale_one = lax.rsqrt(jnp.mean(own_hidden * own_hidden, -1, keepdims=True) + EPSILON)
    hidden = group_gather(own_low, side)
    own_cotangent = order(out_cotangent[0])
    upstream = group_gather(own_cotangent, side)
    cosine, sine = rope_tables(span_at * span + jnp.arange(span, dtype=jnp.int32))
    feed_own, mixer, hidden, upstream, cosine, sine = lax.optimization_barrier(
        (feed_own, mixer, hidden, upstream, cosine, sine)
    )
    feed_own = feed_own.reshape(TP * part, feed_own.shape[-1])
    branch = gather(feed_own[:, : 2 * SW + QW])
    feed = gather(feed_own[:, 2 * SW + QW :])
    full_gate = branch[:, :SW]
    full_out = branch[:, SW:]
    full_gate_up = feed[:, : 2 * FW]
    full_down = feed[:, 2 * FW :]

    vectors = mixer[:, STEP_AT + SH : STEP_AT + SH + VEC].reshape(devices, part * VEC)
    full_gain = vectors[:, :part].reshape(D).astype(f32)
    full_gain_two = vectors[:, part : 2 * part].reshape(D).astype(f32)
    natural = vectors.reshape(pairs, spans, 2, 2, part * VEC)
    natural = natural.transpose(0, 2, 1, 3, 4).reshape(devices, part * VEC)
    at = 2 * part
    all_kernel = natural[:, at : at + KW * conv_part].reshape(devices, KW, conv_part)
    all_kernel = all_kernel.transpose(1, 0, 2).reshape(KW, CONV)
    at += KW * conv_part
    all_offset = natural[:, at : at + conv_part].reshape(1, CONV)
    at += conv_part
    all_mamba_gain = natural[:, at : at + gain_part].reshape(DSSM)
    taps = jnp.concatenate([all_kernel, all_offset], 0)
    taps = jnp.concatenate(
        [lax.dynamic_slice_in_dim(taps, rank * SW, SW, 1), taps[:, DSSM:]], 1
    ).astype(f32)
    kernel, offset = taps[:KW], taps[KW]
    mamba_gain = lax.dynamic_slice_in_dim(all_mamba_gain, rank * SW, SW, 0).astype(f32)
    own_step_offset = lax.dynamic_slice_in_dim(step_offset, rank * SH, SH, 0)
    own_decay_log = lax.dynamic_slice_in_dim(decay_log, rank * SH, SH, 0)
    own_skip = lax.dynamic_slice_in_dim(skip_scale, rank * SH, SH, 0)

    at = jnp.reshape(span_at, (1,)).astype(jnp.int32)
    taps = jnp.pad(taps, ((0, 8 - taps.shape[0]), (0, 0)))
    heads = jnp.stack([own_step_offset, own_decay_log])
    heads = jnp.pad(heads, ((0, 6), (0, 128 - SH)))
    skip = jnp.repeat(own_skip, MP)[None]

    low_normed, mix_rows, query, key_value, step_rows = project(
        hidden, full_gain[None], mixer, cosine, sine
    )
    rim = mix_rows.reshape(2, span, MIXW)[:, span - LEAD :]
    rim = move_spans(rim, 1)
    key_value = key_value.reshape(2, span, 2 * HD)
    reached = [key_value] + [move_spans(key_value, s) for s in range(1, spans)]
    key_values = jnp.concatenate(reached, 1)
    conv, prepared, turned, message = prep(rim, mix_rows, step_rows, taps, heads)
    messages = [move_spans(message, s) for s in range(1, spans)]
    attended, log_total = attend(at, query, key_values)
    gate_rows, mixed, state_in, square = scan(
        low_normed, branch, conv, prepared, turned, skip, messages
    )
    square = group_sum(square[:, 0])
    mamba_scale = lax.rsqrt(square / DSSM + EPSILON)[:, None]
    gate_sigmoid = jax.nn.sigmoid(gate_rows)
    gate_silu = gate_rows * gate_sigmoid
    gated = mixed * gate_silu
    mamba_rows = (gated * mamba_scale * mamba_gain).astype(bf16)
    branches = jnp.concatenate([mamba_rows, attended], 1)
    middle = own_hidden + group_scatter(input_product(branches, full_out), side)

    scale_two = lax.rsqrt(jnp.mean(middle * middle, -1, keepdims=True) + EPSILON)
    low_two = group_gather((middle * scale_two * full_gain_two).astype(bf16), side)
    pre = forward_product(low_two, full_gate_up)
    gate_pre, up_pre = pre[:, :FW], pre[:, FW:]
    sigmoid = jax.nn.sigmoid(gate_pre)
    silu = gate_pre * sigmoid
    activation = (silu * up_pre).astype(bf16)

    back_activation = forward_product(upstream, full_down)
    back_gate = (back_activation * up_pre * sigmoid * (1.0 + gate_pre * (1.0 - sigmoid))).astype(
        bf16
    )
    back_up = (back_activation * silu).astype(bf16)
    back_feed = jnp.concatenate([back_gate, back_up], 1)
    feed_sums = weight_sums(low_two, back_feed, upstream, activation)
    back_feed, feed_sums = lax.optimization_barrier((back_feed, feed_sums))
    gradient_feed = scatter(feed_sums)
    back_normed_two = group_scatter(input_product(back_feed, full_gate_up), side)
    weighted = back_normed_two * full_gain_two
    gradient_gain_two = jnp.sum(back_normed_two * middle * scale_two, 0)
    back_middle = (
        own_cotangent.astype(f32)
        + scale_two * weighted
        - middle * scale_two**3 * jnp.mean(weighted * middle, -1, keepdims=True)
    )
    low_middle = group_gather(back_middle.astype(bf16), side)

    layer_out = middle + group_scatter(input_product(activation, full_down), side)

    back_branches = forward_product(low_middle, full_out)
    back_attended = back_branches[:, SW:].astype(bf16)
    back_rows = back_branches[:, :SW]
    weighted = back_rows * mamba_gain
    gradient_mamba_gain = jnp.sum(back_rows * gated * mamba_scale, 0)
    mean = group_sum(jnp.sum(weighted * gated, -1))[:, None] / DSSM
    back_gated = mamba_scale * weighted - gated * mamba_scale**3 * mean
    back_mixed = back_gated * gate_silu
    low_gate = (
        back_gated * mixed * gate_sigmoid * (1.0 + gate_rows * (1.0 - gate_sigmoid))
    ).astype(bf16)
    back_conv, back_prep, back_skip, *sent = scan_back(
        back_mixed, conv, prepared, turned, skip, state_in, messages
    )
    received = [move_spans(piece, -s) for s, piece in zip(range(1, spans), sent)]
    back_query, own_back, other_back = attend_back(
        at, query, key_values, attended, log_total, back_attended, cosine, sine
    )
    other_back = other_back.reshape(2, spans - 1, span, 2 * HD)
    pieces = [move_spans(other_back[:, s - 1], -s) for s in range(1, spans)]
    back_mix, back_step, back_rim, tap_sums, head_sums = prep_back(
        rim,
        mix_rows,
        step_rows,
        taps,
        heads,
        conv,
        prepared,
        state_in,
        back_conv,
        back_prep,
        back_skip,
        received,
    )
    back_rim = move_spans(back_rim, -1)
    back_all = assemble(
        low_gate, back_mix, back_rim, back_step, back_query, own_back, pieces, cosine, sine
    )
    back_all, gradient_feed = lax.optimization_barrier((back_all, gradient_feed))
    gradient_mixer = scatter(weight_sums(low_normed, back_all, low_middle, branches))
    back_normed = group_scatter(
        input_product(back_all[:, :SW], full_gate) + input_product(back_all[:, SW:], mixer), side
    )
    weighted = back_normed * full_gain
    gradient_gain_one = jnp.sum(back_normed * own_hidden * own_scale_one, 0)
    input_gradient = (
        back_middle
        + own_scale_one * weighted
        - own_hidden * own_scale_one**3 * jnp.mean(weighted * own_hidden, -1, keepdims=True)
    )

    def placed(value, width):
        wide = jnp.zeros(value.shape[:-1] + (width,), f32)
        return lax.dynamic_update_slice_in_dim(
            wide, value, rank * value.shape[-1], value.ndim - 1
        )

    tap_grads = jnp.sum(tap_sums, 0)[: KW + 1]
    tap_grads = jnp.concatenate([placed(tap_grads[:, :SW], DSSM), tap_grads[:, SW:]], 1)
    head_grads = jnp.sum(head_sums, 0)[:3, :SH]
    gain_grads, tap_grads, mamba_gain_grad, head_grads = lax.psum(
        (
            jnp.stack([gradient_gain_one, gradient_gain_two]),
            tap_grads,
            placed(gradient_mamba_gain, DSSM),
            placed(head_grads, MH),
        ),
        BOTH,
    )
    feature_at = ((dp_at // 2 * spans + span_at) * TP + rank) * part
    own_gains = lax.dynamic_slice_in_dim(gain_grads, feature_at, part, 1)
    device_at = dp_at * 2 * spans + ctx_at
    own_taps = lax.dynamic_slice_in_dim(tap_grads, device_at * conv_part, conv_part, 1)
    own_mamba_gain = lax.dynamic_slice_in_dim(
        mamba_gain_grad, device_at * gain_part, gain_part, 0
    )

    feed_parts = group_swap(gradient_feed.reshape(TP, part, 3 * FW), rank).astype(f32)
    mixer_parts = group_swap(gradient_mixer.reshape(TP, part, -1), rank).astype(f32)

    def columns(parts, start, width):
        piece = parts[:, :, start : start + width]
        return piece.transpose(1, 0, 2).reshape(part, TP * width)

    def shared(start):
        piece = mixer_parts[:, :, start : start + HD].reshape(KVH, TP // KVH, part, HD)
        return jnp.sum(piece, 1).transpose(1, 0, 2).reshape(part, KVH * HD)

    at = SW + MIXW
    step_at = SW + STEP_AT
    mix_gradient = jnp.concatenate(
        [
            columns(mixer_parts, SW, SW),
            jnp.sum(mixer_parts[:, :, 2 * SW : SW + MIXW], 0),
        ],
        1,
    )
    return (
        disorder(layer_out.astype(bf16))[None],
        disorder(input_gradient)[None],
        own_gains[0],
        columns(mixer_parts, 0, SW),
        mix_gradient,
        columns(mixer_parts, step_at, SH),
        own_taps[:KW],
        own_taps[KW],
        head_grads[0],
        head_grads[1],
        head_grads[2],
        own_mamba_gain,
        columns(mixer_parts, SW + WIDE, SW).T,
        columns(mixer_parts, at, QW),
        shared(at + QW),
        shared(at + QW + HD),
        columns(mixer_parts, 2 * SW + WIDE, QW).T,
        own_gains[1],
        columns(feed_parts, 0, FW),
        columns(feed_parts, FW, FW),
        columns(feed_parts, 2 * FW, FW).T,
    )


def solution(mesh):
    both = BOTH
    tokens = P("dp", "ctx", None)
    first = P(both, None)
    second = P(None, both)
    vector = P(both)
    whole = P()
    weights = (
        vector,
        first,
        first,
        first,
        second,
        vector,
        whole,
        whole,
        whole,
        vector,
        second,
        first,
        first,
        first,
        second,
        vector,
        first,
        first,
        second,
    )
    return jax.shard_map(
        local,
        mesh=mesh,
        in_specs=(tokens, tokens) + weights,
        out_specs=(tokens, tokens) + weights,
        check_vma=False,
    )
```

time: 569 us -> 451 us (0.79)
  matrix products: 71.2 us -> 15.5 us
  waiting for transfers between devices: 226 us -> 179 us
  Pallas kernels: 0 us -> 36.7 us
  other arithmetic: 48.9 us -> 19.2 us
  local copies, waits for them, and re-layouts: 91.8 us -> 76.9 us
    reduce_scatter x2, waiting for transfers between devices: 72.2 us -> 3.48 us  [scatter(): lax.psum_scatter(value, BOTH, scatter_dimension=0, tiled=True, axis_index...]
    dot_general x24 -> x0, matrix products: 55.6 us -> none  [the longest x3 15 us: mamba_out(): jnp.einsum('bhts,bshp->bthp', mixing, signal, precision=HIGHEST)]
    pallas_call x0 -> x10, Pallas kernels: none -> 36.7 us  [the longest x2 8.32 us: weight_sums(): call(sums_kernel, (D // rows,), [left, fixed(count, wide), left, fixed(co...]
    reshape x17 -> x0, local copies, waits for them, and re-layouts: 18.1 us -> none  [the longest x3 5.05 us: split(): value.reshape(2, span, heads, HD).transpose(0, 2, 1, 3)]
    all_gather x2 -> x3, waiting for transfers between devices: 42.1 us -> 58.8 us  [gather(): lax.all_gather(value, BOTH, axis=0, tiled=True, axis_index_groups=groups)]
    reduce_sum x10 -> x2, other arithmetic: 15.9 us -> 0.01 us  [the longest x1 0.01 us: local(): tap_grads = jnp.sum(tap_sums, 0)[:KW + 1]]
    dynamic_update_slice x12 -> x14, local copies, waits for them, and re-layouts: 0.18 us -> 12.1 us  [group_swap(): result = lax.dynamic_update_slice_in_dim(result, piece, index, 0)]
    unnamed x312 -> x208, local copies, waits for them, and re-layouts: 19.9 us -> 31.3 us
  transfers between devices with their start and end apart: 52 -> 51, of which waited for: 31 -> 28; matrix products, arithmetic and copies ran while one was open for 25% -> 14% of each run, Pallas kernels for 0% -> 6%
where the time goes in v2:
time: 451 us; the launch traced here: 442 us
  waiting for transfers between devices  179 us (40%)
  local copies, waits for them, and re-layouts  76.9 us (17%)
  starting transfers between devices  59.1 us (13%)
  blocking collectives  39.9 us (9%)
  Pallas kernels  36.7 us (8%)
  other arithmetic  19.2 us (4%)
  between operations  16.1 us (4%)
  matrix products  15.5 us (3%)
    ppermute x14, waiting for transfers between devices, swap_side(): return lax.ppermute(value, 'ctx', pairs)  58.9 us
    all_gather x3, waiting for transfers between devices, gather(): lax.all_gather(value, BOTH, axis=0, tiled=True, axis_index_groups=groups)  58.8 us
    psum x1, blocking collectives, local(): lax.psum((jnp.stack([gradient_gain_one, gradient_gain_two]), tap_grads, p...  39.9 us
    ppermute x14, waiting for transfers between devices, move_spans(): return lax.ppermute(value, 'ctx', pairs)  37.6 us
    ppermute x14, starting transfers between devices, move_spans(): return lax.ppermute(value, 'ctx', pairs)  36.7 us
    unnamed x208, local copies, waits for them, and re-layouts  31.3 us
    ppermute x14, starting transfers between devices, swap_side(): return lax.ppermute(value, 'ctx', pairs)  16.5 us
    dynamic_update_slice x14, local copies, waits for them, and re-layouts, group_swap(): result = lax.dynamic_update_slice_in_dim(result, piece, index, 0)  12.1 us
  transfers between devices with their start and end apart: 51, of which 28 were waited for; matrix products, arithmetic and copies ran while one was open for 14% of the time, Pallas kernels for 6%

profile of v2, /device:TPU:0, one launch (start us, length us, event | category | flops | bytes accessed | tf_op | source)
XLA Modules:
  0.0 442.1 jit_solution(7637890806688353590)
XLA Ops:
  12.2 2.8 concatenate.93
  16.7 3.0 collective-permute-start.3
  20.0 2.0 collective-permute-done.3
  31.5 8.9 %collective-permute-done.8 = bf16[128,1024]{1,0:T(8,128)(2,1)S(1)} collective-permute-done((bf16[128,1024]{1,0:T(8,128)(2,1)S(1)}, bf16[128,1024]{1,0:T(8,128)(2,1)S(1)}, u32[]{:S(2)}, u32[]{:S(2)}) %collective-permute-start.8) | collective-permute-done | bytes 262176 | tf_op jit(solution)/shard_map/ppermute | solution.py:56
  40.4 5.2 %collective-permute-done.6 = bf16[128,1024]{1,0:T(8,128)(2,1)S(1)} collective-permute-done((bf16[128,1024]{1,0:T(8,128)(2,1)S(1)}, bf16[128,1024]{1,0:T(8,128)(2,1)S(1)}, u32[]{:S(2)}, u32[]{:S(2)}) %collective-permute-start.6) | collective-permute-done | bytes 262176 | tf_op jit(solution)/shard_map/ppermute | solution.py:56
  49.5 25.2 %all-gather.4.cloned.1.call-done.weight = bf16[1024,1024]{1,0:T(8,128)(2,1)} async-done(((bf16[128,1024]{1,0:T(8,128)(2,1)}), bf16[1024,1024]{1,0:T(8,128)(2,1)}) %all-gather.4.cloned.1.call-update) | async-done | bytes 2097168 | tf_op jit(solution)/shard_map/all_gather | solution.py:824
  80.5 1.9 shard_map.364
  84.8 3.4 collective-permute-start.10
  89.7 4.3 shard_map.365
  94.6 4.3 collective-permute-start.11
  98.9 2.8 collective-permute-start.12
  103.3 1.9 collective-permute-start.18
  105.2 1.9 collective-permute-start.17
  110.4 11.7 %collective-permute-start.16 = (bf16[2,256,128]{2,1,0:T(8,128)(2,1)}, bf16[2,256,128]{2,1,0:T(8,128)(2,1)}, u32[]{:S(2)}, u32[]{:S(2)}) collective-permute-start(bf16[2,256,128]{2,1,0:T(8,128)(2,1)} %bitcast.119), channel_id=1, source_target_pairs={{0,2},{1,3},{2,4},{3,5},{4,6},{5,7},{8,10},{9,11},{10,12},{11,13},... | collective-permute-start | bytes 393224 | tf_op jit(solution)/shard_map/ppermute | solution.py:69
  123.5 8.5 %all-gather.6.cloned.1.call-done.refs_1_ = bf16[1024,896]{1,0:T(8,128)(2,1)} async-done(((bf16[128,896]{1,0:T(8,128)(2,1)}), bf16[1024,896]{1,0:T(8,128)(2,1)}) %all-gather.6.cloned.1.call-update) | async-done | bytes 1835024 | tf_op jit(solution)/shard_map/all_gather | solution.py:824
  136.8 4.1 shard_map.366
  143.1 1.9 collective-permute-start.15
  146.1 2.6 shard_map.367
  150.7 2.6 collective-permute-done.19
  156.2 7.7 %collective-permute-done.20 = bf16[128,1024]{1,0:T(8,128)(2,1)} collective-permute-done((bf16[128,1024]{1,0:T(8,128)(2,1)}, bf16[128,1024]{1,0:T(8,128)(2,1)}, u32[]{:S(2)}, u32[]{:S(2)}) %collective-permute-start.20) | collective-permute-done | bytes 262176 | tf_op jit(solution)/shard_map/ppermute | solution.py:56
  166.5 7.2 %collective-permute-done.21 = bf16[128,1024]{1,0:T(8,128)(2,1)S(1)} collective-permute-done((bf16[128,1024]{1,0:T(8,128)(2,1)S(1)}, bf16[128,1024]{1,0:T(8,128)(2,1)S(1)}, u32[]{:S(2)}, u32[]{:S(2)}) %collective-permute-start.21) | collective-permute-done | bytes 262176 | tf_op jit(solution)/shard_map/ppermute | solution.py:56
  177.8 25.1 %all-gather.8.cloned.1.call-done = bf16[1024,1536]{1,0:T(8,128)(2,1)} async-done(((bf16[128,1536]{1,0:T(8,128)(2,1)}), bf16[1024,1536]{1,0:T(8,128)(2,1)}) %all-gather.8.cloned.1.call-update) | async-done | bytes 3145744 | tf_op jit(solution)/shard_map/all_gather | solution.py:824
  202.9 3.2 fusion.2
  206.2 2.3 multiply_convert_fusion.1
  209.9 3.9 shard_map.368
  215.0 3.2 fusion
  219.3 2.0 fusion.8
  225.9 5.0 %collective-permute-done.26 = bf16[128,1024]{1,0:T(8,128)(2,1)S(1)} collective-permute-done((bf16[128,1024]{1,0:T(8,128)(2,1)S(1)}, bf16[128,1024]{1,0:T(8,128)(2,1)S(1)}, u32[]{:S(2)}, u32[]{:S(2)}) %collective-permute-start.26) | collective-permute-done | bytes 262176 | tf_op jit(solution)/shard_map/ppermute | solution.py:56
  231.7 4.4 collective-permute-done.24
  238.8 6.6 %collective-permute-done.27 = bf16[128,1024]{1,0:T(8,128)(2,1)S(1)} collective-permute-done((bf16[128,1024]{1,0:T(8,128)(2,1)S(1)}, bf16[128,1024]{1,0:T(8,128)(2,1)S(1)}, u32[]{:S(2)}, u32[]{:S(2)}) %collective-permute-start.27) | collective-permute-done | bytes 262176 | tf_op jit(solution)/shard_map/ppermute | solution.py:56
  245.5 1.9 collective-permute-done.28
  252.8 4.3 shard_map.371
  258.5 4.4 shard_map.369
  270.4 2.7 collective-permute-done.31.refs_11_
  274.6 29.4 %collective-permute-done.32.refs_12_ = bf16[2,384,128]{2,1,0:T(8,128)(2,1)S(1)} collective-permute-done((bf16[2,384,128]{2,1,0:T(8,128)(2,1)S(1)}, bf16[2,384,128]{2,1,0:T(8,128)(2,1)S(1)}, u32[]{:S(2)}, u32[]{:S(2)}) %collective-permute-start.32) | collective-permute-done | bytes 196640 | tf_op jit(solution)/shard_map/ppermute | solution.py:69
  304.0 6.3 %shard_map.370 = (f32[512,640]{1,0:T(8,128)S(1)}, f32[512,128]{1,0:T(8,128)S(1)}, f32[2,8,640]{2,1,0:T(8,128)S(1)}, f32[2,8,640]{2,1,0:T(8,128)S(1)}, f32[2,8,128]{2,1,0:T(8,128)S(1)}) custom-call(bf16[2,8,640]{2,1,0:T(8,128)(2,1)S(1)} %copy-done.48, bf16[512,640]{1,0:T(8,128)(2,1)S(1)} %copy-done.9, f32[512,128]{1,0:T(8,128)S(1)} %copy-done.25, ...), custom_call_target="tpu_custom_call" | custom-call | tf_op jit(solution)/shard_map/pallas_call | solution.py:660
  311.9 4.5 %collective-permute-done.34.refs_2_ = f32[2,8,640]{2,1,0:T(8,128)S(1)} collective-permute-done((f32[2,8,640]{2,1,0:T(8,128)S(1)}, f32[2,8,640]{2,1,0:T(8,128)S(1)}, u32[]{:S(2)}, u32[]{:S(2)}) %collective-permute-start.34) | collective-permute-done | bytes 40992 | tf_op jit(solution)/shard_map/ppermute | solution.py:69
  318.7 4.4 shard_map.373
  323.1 2.0 fusion.14
  334.4 2.1 collective-permute-start.45
  338.6 2.9 dynamic_update_slice.72
  342.6 2.9 dynamic_update_slice.73
  346.6 2.9 dynamic_update_slice.74
  350.6 2.9 dynamic_update_slice.75
  357.9 39.9 %all-reduce.3 = (f32[2,1024]{1,0:T(2,128)S(1)}, f32[5,1792]{1,0:T(8,128)S(1)}, f32[3,24]{1,0:T(4,128)S(1)}, f32[1536]{0:T(1024)S(1)}) all-reduce(f32[2,1024]{1,0:T(2,128)S(1)} %pad_maximum_fusion.17, f32[5,1792]{1,0:T(8,128)S(1)} %pad_maximum_fusion.16, ...), channel_id=1, replica_groups=mesh['dp'=4,'ctx'=8] {'dp','ctx'}, use_global_device_ids=true, to_apply=%region_8.9 | all-reduce | flops 12616 | bytes 100928 | tf_op jit(solution)/shard_map/psum | solution.py:1036
  400.7 3.5 reduce-scatter.5.cloned.1.call-done
  409.0 10.9 %collective-permute-done.40 = bf16[1,32,1920]{1,2,0:T(8,128)(2,1)S(1)} collective-permute-done((bf16[1,32,1920]{1,2,0:T(8,128)(2,1)S(1)}, bf16[1,32,1920]{1,2,0:T(8,128)(2,1)S(1)}, u32[]{:S(2)}, u32[]{:S(2)}) %collective-permute-start.40) | collective-permute-done | bytes 122912 | tf_op jit(solution)/shard_map/ppermute | solution.py:56
  420.1 8.2 %collective-permute-done.42 = bf16[1,32,1920]{1,2,0:T(8,128)(2,1)S(1)} collective-permute-done((bf16[1,32,1920]{1,2,0:T(8,128)(2,1)S(1)}, bf16[1,32,1920]{1,2,0:T(8,128)(2,1)S(1)}, u32[]{:S(2)}, u32[]{:S(2)}) %collective-permute-start.42) | collective-permute-done | bytes 122912 | tf_op jit(solution)/shard_map/ppermute | solution.py:63
  (458 shorter events, 120.1 us)
Async XLA Ops:
  7.2 67.5 %all-gather.4.cloned.1.call-start = ((), (), s32[]{:S(2)}) async-start(), calls=%async_computation.2 | async-start | bytes 2359296 | tf_op jit(solution)/shard_map/all_gather | solution.py:824
  16.7 5.3 %collective-permute-start.3 = (bf16[1,32,1024]{2,1,0:T(8,128)(2,1)S(1)}, bf16[1,32,1024]{2,1,0:T(8,128)(2,1)S(1)}, u32[]{:S(2)}, u32[]{:S(2)}) collective-permute-start(bf16[1,32,1024]{2,1,0:T(8,128)(2,1)S(1)} %get-tuple-element.242), channel_id=1, source_target_pairs={{0,1},{1,0},{2,3},{3,2},{4,5},{5,4},{6,7},{7,6},{8,9},{9,8},{10,11... | collective-permute-start | bytes 196616 | tf_op jit(solution)/shard_map/ppermute | solution.py:56
  19.7 2.3 collective-permute-start.4
  19.7 3.7 collective-permute-start.5
  24.2 107.8 %all-gather.6.cloned.1.call-start = ((), (), s32[]{:S(2)}) async-start(), calls=%async_computation.3 | async-start | bytes 2064384 | tf_op jit(solution)/shard_map/all_gather | solution.py:824
  24.6 6.9 %collective-permute-start = (bf16[1,32,2432]{2,1,0:T(8,128)(2,1)S(1)}, bf16[1,32,2432]{2,1,0:T(8,128)(2,1)S(1)}, u32[]{:S(2)}, u32[]{:S(2)}) collective-permute-start(bf16[1,32,2432]{2,1,0:T(8,128)(2,1)S(1)} %get-tuple-element.215), channel_id=1, source_target_pairs={{0,1},{1,0},{2,3},{3,2},{4,5},{5,4},{6,7},{7,6},{8,9},{9,8},{10,11... | collective-permute-start | bytes 466952 | tf_op jit(solution)/shard_map/ppermute | solution.py:56
  25.8 20.7 %collective-permute-start.1 = (bf16[1,32,2432]{2,1,0:T(8,128)(2,1)S(1)}, bf16[1,32,2432]{2,1,0:T(8,128)(2,1)S(1)}, u32[]{:S(2)}, u32[]{:S(2)}) collective-permute-start(bf16[1,32,2432]{2,1,0:T(8,128)(2,1)S(1)} %get-tuple-element.214), channel_id=1, source_target_pairs={{0,8},{8,0},{16,24},{24,16},{1,9},{9,1},{17,25},{25,17},{2,10},{10... | collective-permute-start | bytes 466952 | tf_op jit(solution)/shard_map/ppermute | solution.py:51
  25.9 20.5 %collective-permute-start.2 = (bf16[1,32,2432]{2,1,0:T(8,128)(2,1)S(1)}, bf16[1,32,2432]{2,1,0:T(8,128)(2,1)S(1)}, u32[]{:S(2)}, u32[]{:S(2)}) collective-permute-start(bf16[1,32,2432]{2,1,0:T(8,128)(2,1)S(1)} %get-tuple-element.213), channel_id=1, source_target_pairs={{0,9},{1,8},{2,11},{3,10},{4,13},{5,12},{6,15},{7,14},{8,1},{9,0},... | collective-permute-start | bytes 466952 | tf_op jit(solution)/shard_map/ppermute | solution.py:63
  27.2 13.3 %collective-permute-start.8 = (bf16[128,1024]{1,0:T(8,128)(2,1)S(1)}, bf16[128,1024]{1,0:T(8,128)(2,1)S(1)}, u32[]{:S(2)}, u32[]{:S(2)}) collective-permute-start(bf16[128,1024]{1,0:T(8,128)(2,1)S(1)} %copy.204), channel_id=1, source_target_pairs={{0,1},{1,0},{2,3},{3,2},{4,5},{5,4},{6,7},{7,6},{8,9},{9,8},{10,11... | collective-permute-start | bytes 786440 | tf_op jit(solution)/shard_map/ppermute | solution.py:56
  28.7 16.9 %collective-permute-start.6 = (bf16[128,1024]{1,0:T(8,128)(2,1)S(1)}, bf16[128,1024]{1,0:T(8,128)(2,1)S(1)}, u32[]{:S(2)}, u32[]{:S(2)}) collective-permute-start(bf16[128,1024]{1,0:T(8,128)(2,1)S(1)} %copy.193), channel_id=1, source_target_pairs={{0,1},{1,0},{2,3},{3,2},{4,5},{5,4},{6,7},{7,6},{8,9},{9,8},{10,11... | collective-permute-start | bytes 786440 | tf_op jit(solution)/shard_map/ppermute | solution.py:56
  45.8 2.0 collective-permute-start.7
  45.9 2.6 collective-permute-start.9
  75.5 127.4 %all-gather.8.cloned.1.call-start = ((), (), s32[]{:S(2)}) async-start(), calls=%async_computation.4 | async-start | bytes 3538944 | tf_op jit(solution)/shard_map/all_gather | solution.py:824
  84.8 4.8 %collective-permute-start.10 = (bf16[2,8,640]{2,1,0:T(8,128)(2,1)S(1)}, bf16[2,8,640]{2,1,0:T(8,128)(2,1)S(1)}, u32[]{:S(2)}, u32[]{:S(2)}) collective-permute-start(bf16[2,8,640]{2,1,0:T(8,128)(2,1)S(1)} %slice.462), channel_id=1, source_target_pairs={{0,2},{1,3},{2,4},{3,5},{4,6},{5,7},{8,10},{9,11},{10,12},{11,13},... | collective-permute-start | bytes 61448 | tf_op jit(solution)/shard_map/ppermute | solution.py:69
  94.6 15.2 %collective-permute-start.11 = (bf16[2,400,128]{2,1,0:T(8,128)(2,1)}, bf16[2,400,128]{2,1,0:T(8,128)(2,1)S(1)}, u32[]{:S(2)}, u32[]{:S(2)}) collective-permute-start(bf16[2,400,128]{2,1,0:T(8,128)(2,1)} %get-tuple-element.71), channel_id=1, source_target_pairs={{0,2},{1,3},{2,4},{3,5},{4,6},{5,7},{8,10},{9,11},{10,12},{11,13},... | collective-permute-start | bytes 614408 | tf_op jit(solution)/shard_map/ppermute | solution.py:69
  98.9 23.2 %collective-permute-start.12 = (bf16[2,400,128]{2,1,0:T(8,128)(2,1)}, bf16[2,400,128]{2,1,0:T(8,128)(2,1)S(1)}, u32[]{:S(2)}, u32[]{:S(2)}) collective-permute-start(bf16[2,400,128]{2,1,0:T(8,128)(2,1)} %get-tuple-element.71), channel_id=1, source_target_pairs={{0,4},{1,5},{2,6},{3,7},{8,12},{9,13},{10,14},{11,15},{16,20},{17,... | collective-permute-start | bytes 614408 | tf_op jit(solution)/shard_map/ppermute | solution.py:69
  101.7 21.1 %collective-permute-start.13 = (bf16[2,400,128]{2,1,0:T(8,128)(2,1)}, bf16[2,400,128]{2,1,0:T(8,128)(2,1)S(1)}, u32[]{:S(2)}, u32[]{:S(2)}) collective-permute-start(bf16[2,400,128]{2,1,0:T(8,128)(2,1)} %get-tuple-element.71), channel_id=1, source_target_pairs={{0,6},{1,7},{8,14},{9,15},{16,22},{17,23},{24,30},{25,31}} | collective-permute-start | bytes 614408 | tf_op jit(solution)/shard_map/ppermute | solution.py:69
  103.3 41.7 %collective-permute-start.18 = (bf16[2,256,128]{2,1,0:T(8,128)(2,1)}, bf16[2,256,128]{2,1,0:T(8,128)(2,1)}, u32[]{:S(2)}, u32[]{:S(2)}) collective-permute-start(bf16[2,256,128]{2,1,0:T(8,128)(2,1)} %bitcast.117), channel_id=1, source_target_pairs={{0,6},{1,7},{8,14},{9,15},{16,22},{17,23},{24,30},{25,31}} | collective-permute-start | bytes 393224 | tf_op jit(solution)/shard_map/ppermute | solution.py:69
  105.2 39.8 %collective-permute-start.17 = (bf16[2,256,128]{2,1,0:T(8,128)(2,1)}, bf16[2,256,128]{2,1,0:T(8,128)(2,1)}, u32[]{:S(2)}, u32[]{:S(2)}) collective-permute-start(bf16[2,256,128]{2,1,0:T(8,128)(2,1)} %bitcast.118), channel_id=1, source_target_pairs={{0,4},{1,5},{2,6},{3,7},{8,12},{9,13},{10,14},{11,15},{16,20},{17,... | collective-permute-start | bytes 393224 | tf_op jit(solution)/shard_map/ppermute | solution.py:69
  109.7 207.2 %reduce-scatter.3.cloned.1.call-start = ((), (), s32[]{:S(2)}) async-start(), calls=%async_computation.5 | async-start | bytes 3538944 | tf_op jit(solution)/shard_map/reduce_scatter | solution.py:827
  110.4 34.6 %collective-permute-start.16 = (bf16[2,256,128]{2,1,0:T(8,128)(2,1)}, bf16[2,256,128]{2,1,0:T(8,128)(2,1)}, u32[]{:S(2)}, u32[]{:S(2)}) collective-permute-start(bf16[2,256,128]{2,1,0:T(8,128)(2,1)} %bitcast.119), channel_id=1, source_target_pairs={{0,2},{1,3},{2,4},{3,5},{4,6},{5,7},{8,10},{9,11},{10,12},{11,13},... | collective-permute-start | bytes 393224 | tf_op jit(solution)/shard_map/ppermute | solution.py:69
  143.1 5.6 %collective-permute-start.15 = (f32[512]{0:T(512)S(1)}, f32[512]{0:T(512)S(1)}, u32[]{:S(2)}, u32[]{:S(2)}) collective-permute-start(f32[512]{0:T(512)S(1)} %maximum_add_fusion), channel_id=1, source_target_pairs={{0,1},{1,0},{2,3},{3,2},{4,5},{5,4},{6,7},{7,6},{8,9},{9,8},{10,11... | collective-permute-start | bytes 6152 | tf_op jit(solution)/shard_map/ppermute | solution.py:56
  150.6 2.7 collective-permute-start.19
  155.3 8.7 %collective-permute-start.20 = (bf16[128,1024]{1,0:T(8,128)(2,1)}, bf16[128,1024]{1,0:T(8,128)(2,1)}, u32[]{:S(2)}, u32[]{:S(2)}) collective-permute-start(bf16[128,1024]{1,0:T(8,128)(2,1)} %select_convert_fusion.3), channel_id=1, source_target_pairs={{0,1},{1,0},{2,3},{3,2},{4,5},{5,4},{6,7},{7,6},{8,9},{9,8},{10,11... | collective-permute-start | bytes 786440 | tf_op jit(solution)/shard_map/ppermute | solution.py:56
  166.2 7.6 %collective-permute-start.21 = (bf16[128,1024]{1,0:T(8,128)(2,1)S(1)}, bf16[128,1024]{1,0:T(8,128)(2,1)S(1)}, u32[]{:S(2)}, u32[]{:S(2)}) collective-permute-start(bf16[128,1024]{1,0:T(8,128)(2,1)S(1)} %multiply_convert_fusion.5), channel_id=1, source_target_pairs={{0,1},{1,0},{2,3},{3,2},{4,5},{5,4},{6,7},{7,6},{8,9},{9,8},{10,11... | collective-permute-start | bytes 786440 | tf_op jit(solution)/shard_map/ppermute | solution.py:56
  174.0 2.0 collective-permute-start.22
  214.8 189.3 %reduce-scatter.5.cloned.1.call-start = ((), (), s32[]{:S(2)}) async-start(), calls=%async_computation.6 | async-start | bytes 4423680 | tf_op jit(solution)/shard_map/reduce_scatter | solution.py:827
  218.4 3.1 collective-permute-start.25
  221.4 2.7 collective-permute-start.23
  221.7 9.2 %collective-permute-start.26 = (bf16[128,1024]{1,0:T(8,128)(2,1)S(1)}, bf16[128,1024]{1,0:T(8,128)(2,1)S(1)}, u32[]{:S(2)}, u32[]{:S(2)}) collective-permute-start(bf16[128,1024]{1,0:T(8,128)(2,1)S(1)} %select_convert_fusion.1), channel_id=1, source_target_pairs={{0,1},{1,0},{2,3},{3,2},{4,5},{5,4},{6,7},{7,6},{8,9},{9,8},{10,11... | collective-permute-start | bytes 786440 | tf_op jit(solution)/shard_map/ppermute | solution.py:56
  224.4 11.7 %collective-permute-start.24 = (bf16[128,1024]{1,0:T(8,128)(2,1)S(1)}, bf16[128,1024]{1,0:T(8,128)(2,1)S(1)}, u32[]{:S(2)}, u32[]{:S(2)}) collective-permute-start(bf16[128,1024]{1,0:T(8,128)(2,1)S(1)} %select_convert_fusion.2), channel_id=1, source_target_pairs={{0,1},{1,0},{2,3},{3,2},{4,5},{5,4},{6,7},{7,6},{8,9},{9,8},{10,11... | collective-permute-start | bytes 786440 | tf_op jit(solution)/shard_map/ppermute | solution.py:56
  237.3 8.0 %collective-permute-start.27 = (bf16[128,1024]{1,0:T(8,128)(2,1)S(1)}, bf16[128,1024]{1,0:T(8,128)(2,1)S(1)}, u32[]{:S(2)}, u32[]{:S(2)}) collective-permute-start(bf16[128,1024]{1,0:T(8,128)(2,1)S(1)} %get-tuple-element.198), channel_id=1, source_target_pairs={{0,1},{1,0},{2,3},{3,2},{4,5},{5,4},{6,7},{7,6},{8,9},{9,8},{10,11... | collective-permute-start | bytes 786440 | tf_op jit(solution)/shard_map/ppermute | solution.py:56
  250.4 6.9 %collective-permute-start.30 = (f32[512]{0:T(512)S(1)}, f32[512]{0:T(512)S(1)}, u32[]{:S(2)}, u32[]{:S(2)}) collective-permute-start(f32[512]{0:T(512)S(1)} %maximum_add_fusion.1), channel_id=1, source_target_pairs={{0,1},{1,0},{2,3},{3,2},{4,5},{5,4},{6,7},{7,6},{8,9},{9,8},{10,11... | collective-permute-start | bytes 6152 | tf_op jit(solution)/shard_map/ppermute | solution.py:56
  263.9 9.2 %collective-permute-start.31 = (bf16[2,384,128]{2,1,0:T(8,128)(2,1)S(1)}, bf16[2,384,128]{2,1,0:T(8,128)(2,1)S(1)}, u32[]{:S(2)}, u32[]{:S(2)}) collective-permute-start(bf16[2,384,128]{2,1,0:T(8,128)(2,1)S(1)} %get-tuple-element.84), channel_id=1, source_target_pairs={{2,0},{3,1},{4,2},{5,3},{6,4},{7,5},{10,8},{11,9},{12,10},{13,11},... | collective-permute-start | bytes 589832 | tf_op jit(solution)/shard_map/ppermute | solution.py:69
  265.2 38.8 %collective-permute-start.32 = (bf16[2,384,128]{2,1,0:T(8,128)(2,1)S(1)}, bf16[2,384,128]{2,1,0:T(8,128)(2,1)S(1)}, u32[]{:S(2)}, u32[]{:S(2)}) collective-permute-start(bf16[2,384,128]{2,1,0:T(8,128)(2,1)S(1)} %get-tuple-element.85), channel_id=1, source_target_pairs={{4,0},{5,1},{6,2},{7,3},{12,8},{13,9},{14,10},{15,11},{20,16},{21,... | collective-permute-start | bytes 589832 | tf_op jit(solution)/shard_map/ppermute | solution.py:69
  266.5 37.5 %collective-permute-start.33 = (bf16[2,384,128]{2,1,0:T(8,128)(2,1)S(1)}, bf16[2,384,128]{2,1,0:T(8,128)(2,1)S(1)}, u32[]{:S(2)}, u32[]{:S(2)}) collective-permute-start(bf16[2,384,128]{2,1,0:T(8,128)(2,1)S(1)} %get-tuple-element.86), channel_id=1, source_target_pairs={{6,0},{7,1},{14,8},{15,9},{22,16},{23,17},{30,24},{31,25}} | collective-permute-start | bytes 589832 | tf_op jit(solution)/shard_map/ppermute | solution.py:69
  267.8 44.0 %collective-permute-start.35 = (bf16[2,256,128]{2,1,0:T(8,128)(2,1)S(1)}, bf16[2,256,128]{2,1,0:T(8,128)(2,1)S(1)}, u32[]{:S(2)}, u32[]{:S(2)}) collective-permute-start(bf16[2,256,128]{2,1,0:T(8,128)(2,1)S(1)} %get-tuple-element.239), channel_id=1, source_target_pairs={{2,0},{3,1},{4,2},{5,3},{6,4},{7,5},{10,8},{11,9},{12,10},{13,11},... | collective-permute-start | bytes 393224 | tf_op jit(solution)/shard_map/ppermute | solution.py:69
  269.1 42.8 %collective-permute-start.36 = (bf16[2,256,128]{2,1,0:T(8,128)(2,1)S(1)}, bf16[2,256,128]{2,1,0:T(8,128)(2,1)S(1)}, u32[]{:S(2)}, u32[]{:S(2)}) collective-permute-start(bf16[2,256,128]{2,1,0:T(8,128)(2,1)S(1)} %get-tuple-element.238), channel_id=1, source_target_pairs={{4,0},{5,1},{6,2},{7,3},{12,8},{13,9},{14,10},{15,11},{20,16},{21,... | collective-permute-start | bytes 393224 | tf_op jit(solution)/shard_map/ppermute | solution.py:69
  273.1 38.8 %collective-permute-start.37 = (bf16[2,256,128]{2,1,0:T(8,128)(2,1)S(1)}, bf16[2,256,128]{2,1,0:T(8,128)(2,1)S(1)}, u32[]{:S(2)}, u32[]{:S(2)}) collective-permute-start(bf16[2,256,128]{2,1,0:T(8,128)(2,1)S(1)} %get-tuple-element.237), channel_id=1, source_target_pairs={{6,0},{7,1},{14,8},{15,9},{22,16},{23,17},{30,24},{31,25}} | collective-permute-start | bytes 393224 | tf_op jit(solution)/shard_map/ppermute | solution.py:69
  310.4 6.0 %collective-permute-start.34 = (f32[2,8,640]{2,1,0:T(8,128)S(1)}, f32[2,8,640]{2,1,0:T(8,128)S(1)}, u32[]{:S(2)}, u32[]{:S(2)}) collective-permute-start(f32[2,8,640]{2,1,0:T(8,128)S(1)} %get-tuple-element.88), channel_id=1, source_target_pairs={{2,0},{3,1},{4,2},{5,3},{6,4},{7,5},{10,8},{11,9},{12,10},{13,11},... | collective-permute-start | bytes 122888 | tf_op jit(solution)/shard_map/ppermute | solution.py:69
  326.6 10.0 %collective-permute-start.38 = (f32[256,1024]{1,0:T(8,128)S(1)}, f32[256,1024]{1,0:T(8,128)}, u32[]{:S(2)}, u32[]{:S(2)}) collective-permute-start(f32[256,1024]{1,0:T(8,128)S(1)} %slice.492), channel_id=1, source_target_pairs={{0,8},{8,0},{16,24},{24,16},{1,9},{9,1},{17,25},{25,17},{2,10},{10... | collective-permute-start | bytes 3145736 | tf_op jit(solution)/shard_map/ppermute | solution.py:51
  334.4 7.2 %collective-permute-start.43 = (bf16[1,32,1536]{2,1,0:T(8,128)(2,1)}, bf16[1,32,1536]{2,1,0:T(8,128)(2,1)}, u32[]{:S(2)}, u32[]{:S(2)}) collective-permute-start(bf16[1,32,1536]{2,1,0:T(8,128)(2,1)} %get-tuple-element.235), channel_id=1, source_target_pairs={{0,1},{1,0},{2,3},{3,2},{4,5},{5,4},{6,7},{7,6},{8,9},{9,8},{10,11... | collective-permute-start | bytes 294920 | tf_op jit(solution)/shard_map/ppermute | solution.py:56
  334.4 11.2 %collective-permute-start.44 = (bf16[1,32,1536]{2,1,0:T(8,128)(2,1)}, bf16[1,32,1536]{2,1,0:T(8,128)(2,1)}, u32[]{:S(2)}, u32[]{:S(2)}) collective-permute-start(bf16[1,32,1536]{2,1,0:T(8,128)(2,1)} %get-tuple-element.234), channel_id=1, source_target_pairs={{0,8},{8,0},{16,24},{24,16},{1,9},{9,1},{17,25},{25,17},{2,10},{10... | collective-permute-start | bytes 294920 | tf_op jit(solution)/shard_map/ppermute | solution.py:51
  334.4 15.2 %collective-permute-start.45 = (bf16[1,32,1536]{2,1,0:T(8,128)(2,1)}, bf16[1,32,1536]{2,1,0:T(8,128)(2,1)}, u32[]{:S(2)}, u32[]{:S(2)}) collective-permute-start(bf16[1,32,1536]{2,1,0:T(8,128)(2,1)} %get-tuple-element.233), channel_id=1, source_target_pairs={{0,9},{1,8},{2,11},{3,10},{4,13},{5,12},{6,15},{7,14},{8,1},{9,0},... | collective-permute-start | bytes 294920 | tf_op jit(solution)/shard_map/ppermute | solution.py:63
  338.0 18.1 %collective-permute-start.39 = (bf16[128,1024]{1,0:T(8,128)(2,1)S(1)}, bf16[128,1024]{1,0:T(8,128)(2,1)S(1)}, u32[]{:S(2)}, u32[]{:S(2)}) collective-permute-start(bf16[128,1024]{1,0:T(8,128)(2,1)S(1)} %select_convert_fusion), channel_id=1, source_target_pairs={{0,1},{1,0},{2,3},{3,2},{4,5},{5,4},{6,7},{7,6},{8,9},{9,8},{10,11... | collective-permute-start | bytes 786440 | tf_op jit(solution)/shard_map/ppermute | solution.py:56
  405.8 14.2 %collective-permute-start.40 = (bf16[1,32,1920]{1,2,0:T(8,128)(2,1)S(1)}, bf16[1,32,1920]{1,2,0:T(8,128)(2,1)S(1)}, u32[]{:S(2)}, u32[]{:S(2)}) collective-permute-start(bf16[1,32,1920]{1,2,0:T(8,128)(2,1)S(1)} %copy.247), channel_id=1, source_target_pairs={{0,1},{1,0},{2,3},{3,2},{4,5},{5,4},{6,7},{7,6},{8,9},{9,8},{10,11... | collective-permute-start | bytes 368648 | tf_op jit(solution)/shard_map/ppermute | solution.py:56
  407.6 12.4 %collective-permute-start.41 = (bf16[1,32,1920]{1,2,0:T(8,128)(2,1)S(1)}, bf16[1,32,1920]{1,2,0:T(8,128)(2,1)S(1)}, u32[]{:S(2)}, u32[]{:S(2)}) collective-permute-start(bf16[1,32,1920]{1,2,0:T(8,128)(2,1)S(1)} %copy.248), channel_id=1, source_target_pairs={{0,8},{8,0},{16,24},{24,16},{1,9},{9,1},{17,25},{25,17},{2,10},{10... | collective-permute-start | bytes 368648 | tf_op jit(solution)/shard_map/ppermute | solution.py:51
  408.0 20.4 %collective-permute-start.42 = (bf16[1,32,1920]{1,2,0:T(8,128)(2,1)S(1)}, bf16[1,32,1920]{1,2,0:T(8,128)(2,1)S(1)}, u32[]{:S(2)}, u32[]{:S(2)}) collective-permute-start(bf16[1,32,1920]{1,2,0:T(8,128)(2,1)S(1)} %copy.249), channel_id=1, source_target_pairs={{0,9},{1,8},{2,11},{3,10},{4,13},{5,12},{6,15},{7,14},{8,1},{9,0},... | collective-permute-start | bytes 368648 | tf_op jit(solution)/shard_map/ppermute | solution.py:63
  (98 other events, 1040.3 us)
Sparse Core Ops, SparseCore 0:
  24.3 50.3 all-gather.3
  77.4 54.5 all-gather.5
  134.1 68.7 all-gather.7
  214.9 92.4 reduce-scatter.2
  323.2 80.8 reduce-scatter.4

commit v3 on v2

--- a/solution.py
+++ b/solution.py
@@ -21,11 +21,13 @@
 SW = DSSM // TP
 SH = MH // TP
 QW = AH * HD // TP
-FW = FF // TP
+FEED = 8
+FW = FF // FEED
 MIXW = SW + 2 * NS
 STEP_AT = MIXW + QW + 2 * HD
 VEC = 16
 WIDE = 1024
+FULL = WIDE + SW
 
 EPSILON = 1e-05
 ROPE_BASE = 100000000000.0
@@ -56,11 +58,9 @@
     return lax.ppermute(value, "ctx", pairs)
 
 
-def swap_both(value):
-    blocks = lax.axis_size("ctx")
-    count = lax.axis_size("dp") * blocks
-    pairs = [(i, ((i // blocks) ^ 1) * blocks + ((i % blocks) ^ 1)) for i in range(count)]
-    return lax.ppermute(value, BOTH, pairs)
+def swap_pair(value):
+    pairs = [(i, i ^ 2) for i in range(lax.axis_size("dp"))]
+    return lax.ppermute(value, "dp", pairs)
 
 
 def move_spans(value, by):
@@ -93,20 +93,68 @@
     return value + swap_side(value)
 
 
-def group_swap(parts, rank):
-    def at(index):
-        return lax.dynamic_index_in_dim(parts, index, 0, keepdims=True)
-
-    pieces = (
-        (rank, at(rank)),
-        (rank ^ 1, swap_side(at(rank ^ 1))),
-        (rank ^ 2, swap_core(at(rank ^ 2))),
-        (rank ^ 3, swap_both(at(rank ^ 3))),
-    )
-    result = jnp.zeros_like(parts)
-    for index, piece in pieces:
-        result = lax.dynamic_update_slice_in_dim(result, piece, index, 0)
-    return result
+def exchange(parts, axis, bit, swap):
+    first = lax.index_in_dim(parts, 0, axis, keepdims=False)
+    second = lax.index_in_dim(parts, 1, axis, keepdims=False)
+    low = bit == 0
+    keep = jnp.where(low, first, second)
+    other = swap(jnp.where(low, second, first))
+    return jnp.stack([jnp.where(low, keep, other), jnp.where(low, other, keep)], axis)
+
+
+def group_swap(parts, core, side):
+    split = parts.reshape(2, 2, *parts.shape[1:])
+    split = exchange(exchange(split, 0, core, swap_core), 1, side, swap_side)
+    return split.reshape(parts.shape)
+
+
+def feed_swap(parts, pair, core, side):
+    split = parts.reshape(2, 2, 2, *parts.shape[1:])
+    split = exchange(exchange(split, 1, core, swap_core), 2, side, swap_side)
+    return exchange(split, 0, pair, swap_pair).reshape(parts.shape)
+
+
+def both(first, second):
+    return lax.optimization_barrier((first, second))
+
+
+def feed_gather(value):
+    half = value.shape[0] // 2
+    first, second = value[:half], value[half:]
+    first_other, second_other = both(swap_side(first), swap_pair(second))
+    first_pair = jnp.concatenate([first, first_other], 0)
+    second_pair = jnp.concatenate([second, second_other], 0)
+    first_other, second_other = both(swap_pair(first_pair), swap_side(second_pair))
+    mine = jnp.concatenate([first_pair, first_other, second_pair, second_other], 0)
+    return jnp.concatenate([mine, swap_core(mine)], 0)
+
+
+def feed_gather_slow(value):
+    half = value.shape[0] // 2
+    row = jnp.stack([value, swap_side(value)])
+    square = jnp.stack([row, swap_pair(row)])
+    first = square[:, :, :half].reshape(4 * half, -1)
+    second = square[:, :, half:].swapaxes(0, 1).reshape(4 * half, -1)
+    mine = jnp.concatenate([first, second], 0)
+    return jnp.concatenate([mine, swap_core(mine)], 0)
+
+
+def feed_scatter(own, other):
+    part = own.shape[0] // 4
+
+    def meet(first, second, first_swap, second_swap):
+        rows = first.shape[0] // 2
+        first_other, second_other = both(
+            first_swap(first[rows:].astype(bf16)), second_swap(second[rows:].astype(bf16))
+        )
+        return (
+            first[:rows] + first_other.astype(f32),
+            second[:rows] + second_other.astype(f32),
+        )
+
+    mine = own.astype(f32) + swap_core(other).astype(f32)
+    first, second = meet(mine[: 2 * part], mine[2 * part :], swap_pair, swap_side)
+    return jnp.concatenate(meet(first, second, swap_side, swap_pair), 0)
 
 
 def call(body, grid, in_specs, out_specs, out_shape, scratch=()):
@@ -203,11 +251,23 @@
 
 
 def project_kernel(
-    hidden, gain, weight, cosine, sine, normed_out, mix_out, query_out, key_value_out, step_out
+    hidden,
+    weight,
+    cosine,
+    sine,
+    normed_out,
+    mix_out,
+    query_out,
+    key_value_out,
+    step_out,
+    gate_out,
+    gain_out,
 ):
     wide = hidden[...].astype(f32)
     scale = lax.rsqrt(jnp.mean(wide * wide, -1, keepdims=True) + EPSILON)
-    normed = (wide * scale * gain[...]).astype(bf16)
+    gains = weight[:, STEP_AT:WIDE].astype(f32).T
+    gain_out[...] = gains[SH : SH + 2]
+    normed = (wide * scale * gains[SH : SH + 1]).astype(bf16)
     normed_out[...] = normed
     rows = product(normed, weight[...])
     mix_out[...] = rows[:, :MIXW].astype(bf16)
@@ -216,30 +276,27 @@
     at += QW
     pair = turn_first(rows[:, at : at + 2 * HD], cosine[...], sine[...])
     key_value_out[...] = pair.astype(bf16)
-    tail = rows[:, STEP_AT:]
+    tail = rows[:, STEP_AT:WIDE]
     lane = lax.broadcasted_iota(jnp.int32, tail.shape, 1)
     step_out[...] = jnp.where(lane < SH, tail, 0.0)
-
-
-def project(hidden, gain, weight, cosine, sine):
+    gate_out[...] = rows[:, WIDE:]
+
+
+def project(hidden, weight, cosine, sine):
     count = hidden.shape[0]
     span = count // 2
     return call(
         project_kernel,
         (2,),
-        [
-            row_block(span, D),
-            fixed(1, D),
-            fixed(D, WIDE),
-            fixed(span, 128),
-            fixed(span, 128),
-        ],
+        [row_block(span, D), fixed(*weight.shape), fixed(span, 128), fixed(span, 128)],
         [
             row_block(span, D),
             row_block(span, MIXW),
             row_block(span, QW),
             row_block(span, 128),
             row_block(span, 128),
+            row_block(span, SW),
+            fixed(2, D),
         ],
         [
             shape(count, D, dtype=bf16),
@@ -247,8 +304,66 @@
             shape(count, QW, dtype=bf16),
             shape(count, 128, dtype=bf16),
             shape(count, 128),
-        ],
-    )(hidden, gain, weight, cosine, sine)
+            shape(count, SW),
+            shape(2, D),
+        ],
+    )(hidden, weight, cosine, sine)
+
+
+def feed_kernel(
+    normed, upstream, gate_up, down, back_out, activation_out, own_out, other_out, layer_out
+):
+    pre = product(normed[...], gate_up[...])
+    gate, up = pre[:, :FW], pre[:, FW:]
+    sigmoid = 1.0 / (1.0 + jnp.exp(-gate))
+    silu = gate * sigmoid
+    activation = (silu * up).astype(bf16)
+    activation_out[...] = activation
+    back = product(upstream[...], down[...])
+    back_gate = back * up * sigmoid * (1.0 + gate * (1.0 - sigmoid))
+    back_feed = jnp.concatenate([back_gate.astype(bf16), (back * silu).astype(bf16)], 1)
+    back_out[...] = back_feed
+    partial = product(back_feed, gate_up[...], 1, 1)
+    mine = pl.program_id(0) < pl.num_programs(0) // 2
+
+    @pl.when(mine)
+    def _():
+        own_out[...] = partial
+
+    @pl.when(jnp.logical_not(mine))
+    def _():
+        other_out[...] = partial.astype(bf16)
+
+    layer_out[...] = product(activation, down[...], 1, 1).astype(bf16)
+
+
+def feed_pass(normed, upstream, feed):
+    count = normed.shape[0]
+    rows = count // 4
+    return call(
+        feed_kernel,
+        (4,),
+        [
+            row_block(rows, D),
+            row_block(rows, D),
+            fixed(D, 2 * FW),
+            pl.BlockSpec((D, FW), lambda b: (0, 2)),
+        ],
+        [
+            row_block(rows, 2 * FW),
+            row_block(rows, FW),
+            pl.BlockSpec((rows, D), lambda b: (jnp.minimum(b, 1), 0)),
+            pl.BlockSpec((rows, D), lambda b: (jnp.maximum(b - 2, 0), 0)),
+            row_block(rows, D),
+        ],
+        [
+            shape(count, 2 * FW, dtype=bf16),
+            shape(count, FW, dtype=bf16),
+            shape(count // 2, D),
+            shape(count // 2, D, dtype=bf16),
+            shape(count, D, dtype=bf16),
+        ],
+    )(normed, upstream, feed, feed)
 
 
 def visible_keys(span, keys, at):
@@ -417,13 +532,11 @@
 
 
 def scan_kernel(
-    parts, normed, gate_weight, conv, prep, turned, skip, *refs
+    parts, gate, conv, prep, turned, skip, *refs
 ):
     messages = refs[:parts]
-    gate_out, mixed_out, state_out, square_out = refs[parts:]
+    mixed_out, state_out, square_out = refs[parts:]
     rows = conv.shape[0]
-    gate = product(normed[...], gate_weight[...])
-    gate_out[...] = gate
     between = jnp.zeros((1, 128), f32)
     state = jnp.zeros((SW, NS), f32)
     for message in messages:
@@ -448,19 +561,18 @@
     grown = spread_heads(jnp.exp(prep[:, 128:]), head_mask())
     mixed = jnp.concatenate(parts_out, 1) + carried * grown + skip[...] * signal
     mixed_out[...] = mixed
-    gated = mixed * gate / (1.0 + jnp.exp(-gate))
+    gated = mixed * gate[...] / (1.0 + jnp.exp(-gate[...]))
     square_out[...] = jnp.broadcast_to(jnp.sum(gated * gated, 1, keepdims=True), (rows, 128))
 
 
-def scan(normed, feed, conv, prepared, turned, skip, messages):
+def scan(gate, conv, prepared, turned, skip, messages):
     count = conv.shape[0]
     rows = count // 2
     return call(
         lambda *refs: scan_kernel(len(messages), *refs),
         (2,),
         [
-            row_block(rows, D),
-            fixed(D, SW),
+            row_block(rows, SW),
             row_block(rows, MIXW),
             row_block(rows, 256),
             seq_block(16, rows),
@@ -469,12 +581,11 @@
         + [seq_block(SW + 16, NS)] * len(messages),
         [
             row_block(rows, SW),
-            row_block(rows, SW),
             seq_block(SW, NS),
             row_block(rows, 128),
         ],
-        [shape(count, SW), shape(count, SW), shape(2, SW, NS), shape(count, 128)],
-    )(normed, feed, conv, prepared, turned, skip, *messages)
+        [shape(count, SW), shape(2, SW, NS), shape(count, 128)],
+    )(gate, conv, prepared, turned, skip, *messages)
 
 
 def scan_back_kernel(parts, back, conv, prep, turned, skip, state, *refs):
@@ -708,33 +819,36 @@
     )
 
 
-def assemble_kernel(parts, gate, mix, rim, step, query, own, cosine, sine, *refs):
+def assemble_kernel(parts, side, gate, mix, rim, step, query, own, cosine, sine, *refs):
     received, out = refs[:parts], refs[parts]
     rows = mix.shape[0]
-    out[:, :SW] = gate[...]
-    mixed = slice(SW, SW + MIXW)
+    out[:, WIDE:] = gate[...]
+    mixed = slice(0, MIXW)
     out[:, mixed] = mix[...].astype(bf16)
     tail = mix[rows - 16 :]
     returned = jnp.concatenate([jnp.zeros((16 - LEAD, MIXW), f32), rim[0]], 0)
     tail = tail + pltpu.roll(returned, LEAD - KW + 1, 0)
     out[rows - 16 :, mixed] = tail.astype(bf16)
-    at = SW + MIXW
+    at = MIXW
     out[:, at : at + QW] = query[...]
-    pair = own[0]
+    half = jnp.zeros((rows // 2, 2 * HD), f32)
     for piece in received:
-        pair = pair + piece[0].astype(f32)
+        half = half + piece[0].astype(f32)
+    row = lax.broadcasted_iota(jnp.int32, (rows, 2 * HD), 0)
+    pair = own[0] + jnp.where(row // (rows // 2) == side[0], jnp.concatenate([half, half], 0), 0.0)
     at += QW
     out[:, at : at + 2 * HD] = turn_first(pair, cosine[...], -sine[...]).astype(bf16)
-    out[:, SW + STEP_AT :] = step[...].astype(bf16)
-
-
-def assemble(gate, mix, rim, step, query, own, received, cosine, sine):
+    out[:, STEP_AT:WIDE] = step[...].astype(bf16)
+
+
+def assemble(side, gate, mix, rim, step, query, own, received, cosine, sine):
     count = mix.shape[0]
     rows = count // 2
     return call(
         lambda *refs: assemble_kernel(len(received), *refs),
         (2,),
         [
+            SCALAR,
             row_block(rows, SW),
             row_block(rows, MIXW),
             seq_block(LEAD, MIXW),
@@ -744,10 +858,10 @@
             fixed(rows, 128),
             fixed(rows, 128),
         ]
-        + [seq_block(rows, 2 * HD)] * len(received),
-        row_block(rows, SW + WIDE),
-        shape(count, SW + WIDE, dtype=bf16),
-    )(gate, mix, rim, step, query, own, cosine, sine, *received)
+        + [seq_block(rows // 2, 2 * HD)] * len(received),
+        row_block(rows, FULL),
+        shape(count, FULL, dtype=bf16),
+    )(side, gate, mix, rim, step, query, own, cosine, sine, *received)
 
 
 def sums_kernel(first_left, first_right, second_left, second_right, out):
@@ -796,49 +910,60 @@
     rows = tokens.shape[1]
     span = 2 * rows
     count = 2 * span
-    pairs, spans = lax.axis_size("dp") // 2, lax.axis_size("ctx") // 2
-    devices = 4 * pairs * spans
+    quads, spans = lax.axis_size("dp") // 4, lax.axis_size("ctx") // 2
+    devices = 8 * quads * spans
     dp_at, ctx_at = lax.axis_index("dp"), lax.axis_index("ctx")
     side, span_at = ctx_at % 2, ctx_at // 2
-    rank = (dp_at % 2) * 2 + side
+    core, pair = dp_at % 2, dp_at // 2 % 2
+    rank = core * 2 + side
     part = D // devices
     conv_part = CONV // devices
     gain_part = DSSM // devices
     groups = [
-        [(y * 2 + c) * 2 * spans + z * 2 + x for y in range(pairs) for z in range(spans)]
+        [
+            ((quad * 2 + y) * 2 + c) * 2 * spans + z * 2 + x
+            for quad in range(quads)
+            for z in range(spans)
+            for y in range(2)
+        ]
         for c in range(2)
         for x in range(2)
     ]
+    feed_groups = [
+        [(quad * 4 + d) * 2 * spans + z * 2 + x for quad in range(quads) for z in range(spans)]
+        for d in range(4)
+        for x in range(2)
+    ]
 
     def order(value):
         lead = value.shape[:-1]
-        value = value.reshape(*lead, pairs, 2, spans, 2 * part)
+        value = value.reshape(*lead, quads, 4, spans, 2 * part)
         return jnp.swapaxes(value, -3, -2).reshape(*lead, D)
 
     def disorder(value):
         lead = value.shape[:-1]
-        value = value.reshape(*lead, pairs, spans, 2, 2 * part)
+        value = value.reshape(*lead, quads, spans, 4, 2 * part)
         return jnp.swapaxes(value, -3, -2).reshape(*lead, D)
 
-    def gather(value):
+    def gather(value, groups):
         return lax.all_gather(value, BOTH, axis=0, tiled=True, axis_index_groups=groups)
 
-    def scatter(value):
+    def scatter(value, groups):
         return lax.psum_scatter(
             value, BOTH, scatter_dimension=0, tiled=True, axis_index_groups=groups
         )
 
-    vector = jnp.concatenate(
-        [
-            input_gain,
-            ffn_gain,
-            conv_kernel.reshape(-1),
-            conv_offset,
-            mamba_norm_gain,
-        ]
-    )
-    vector = jnp.pad(vector, (0, part * VEC - vector.shape[0])).reshape(part, VEC)
-
+    vector = jnp.concatenate([conv_kernel.reshape(-1), conv_offset, mamba_norm_gain])
+    vector = jnp.pad(vector, (0, part * (VEC - 2) - vector.shape[0])).reshape(part, VEC - 2)
+    tail = jnp.concatenate(
+        [
+            input_gain[:, None],
+            ffn_gain[:, None],
+            vector,
+            jnp.zeros((part, WIDE - STEP_AT - SH - VEC), bf16),
+        ],
+        1,
+    )
     def mixer_part(s):
         kv = s // 2
         return jnp.concatenate(
@@ -849,22 +974,44 @@
                 key_weight[:, HD * kv : HD * (kv + 1)],
                 value_weight[:, HD * kv : HD * (kv + 1)],
                 mamba_step_weight[:, SH * s : SH * (s + 1)],
-                vector,
-                jnp.zeros((part, WIDE - STEP_AT - SH - VEC), bf16),
+                tail,
+                mamba_gate_weight[:, SW * s : SW * (s + 1)],
             ],
             1,
         )
 
+    mixer_own = group_swap(jnp.stack([mixer_part(s) for s in range(TP)]), core, side)
+    later = (
+        mamba_out_weight,
+        attention_out_weight,
+        feed_gate_weight,
+        feed_up_weight,
+        feed_down_weight,
+        tokens,
+        out_cotangent,
+    )
+    mixer_own, later = lax.optimization_barrier((mixer_own, later))
+    mamba_out_weight, attention_out_weight = later[:2]
+    feed_gate_weight, feed_up_weight, feed_down_weight, tokens, out_cotangent = later[2:]
+    mixer = gather(mixer_own.reshape(TP * part, -1), groups)
     mamba_out_turned = mamba_out_weight.T
     attention_out_turned = attention_out_weight.T
     feed_down_turned = feed_down_weight.T
 
+    def branch_part(s):
+        return jnp.concatenate(
+            [
+                mamba_out_turned[:, SW * s : SW * (s + 1)],
+                attention_out_turned[:, QW * s : QW * (s + 1)],
+            ],
+            1,
+        )
+
+    branch_own = group_swap(jnp.stack([branch_part(s) for s in range(TP)]), core, side)
+    branch_own = branch_own.reshape(TP * part, -1)
     def feed_part(s):
         return jnp.concatenate(
             [
-                mamba_gate_weight[:, SW * s : SW * (s + 1)],
-                mamba_out_turned[:, SW * s : SW * (s + 1)],
-                attention_out_turned[:, QW * s : QW * (s + 1)],
                 feed_gate_weight[:, FW * s : FW * (s + 1)],
                 feed_up_weight[:, FW * s : FW * (s + 1)],
                 feed_down_turned[:, FW * s : FW * (s + 1)],
@@ -872,33 +1019,26 @@
             1,
         )
 
-    mixer_own = group_swap(jnp.stack([mixer_part(s) for s in range(TP)]), rank)
-    mixer = gather(mixer_own.reshape(TP * part, WIDE))
-    feed_own = group_swap(jnp.stack([feed_part(s) for s in range(TP)]), rank)
+    feed_own = feed_swap(jnp.stack([feed_part(s) for s in range(FEED)]), pair, core, side)
+    feed_own = feed_own.reshape(FEED * part, -1)
     own_low = order(tokens[0])
     own_hidden = own_low.astype(f32)
     own_scale_one = lax.rsqrt(jnp.mean(own_hidden * own_hidden, -1, keepdims=True) + EPSILON)
     hidden = group_gather(own_low, side)
     own_cotangent = order(out_cotangent[0])
-    upstream = group_gather(own_cotangent, side)
     cosine, sine = rope_tables(span_at * span + jnp.arange(span, dtype=jnp.int32))
-    feed_own, mixer, hidden, upstream, cosine, sine = lax.optimization_barrier(
-        (feed_own, mixer, hidden, upstream, cosine, sine)
-    )
-    feed_own = feed_own.reshape(TP * part, feed_own.shape[-1])
-    branch = gather(feed_own[:, : 2 * SW + QW])
-    feed = gather(feed_own[:, 2 * SW + QW :])
-    full_gate = branch[:, :SW]
-    full_out = branch[:, SW:]
-    full_gate_up = feed[:, : 2 * FW]
-    full_down = feed[:, 2 * FW :]
-
-    vectors = mixer[:, STEP_AT + SH : STEP_AT + SH + VEC].reshape(devices, part * VEC)
-    full_gain = vectors[:, :part].reshape(D).astype(f32)
-    full_gain_two = vectors[:, part : 2 * part].reshape(D).astype(f32)
-    natural = vectors.reshape(pairs, spans, 2, 2, part * VEC)
-    natural = natural.transpose(0, 2, 1, 3, 4).reshape(devices, part * VEC)
-    at = 2 * part
+    upstream = feed_gather_slow(own_cotangent)
+    branch_own, feed_own, mixer, hidden, upstream, cosine, sine = lax.optimization_barrier(
+        (branch_own, feed_own, mixer, hidden, upstream, cosine, sine)
+    )
+    full_out = gather(branch_own, groups)
+    feed = gather(feed_own, feed_groups)
+
+    at = STEP_AT + SH + 2
+    vectors = mixer[:, at : at + VEC - 2]
+    natural = vectors.reshape(quads, spans, 4, 2, part * (VEC - 2))
+    natural = natural.transpose(0, 2, 1, 3, 4).reshape(devices, part * (VEC - 2))
+    at = 0
     all_kernel = natural[:, at : at + KW * conv_part].reshape(devices, KW, conv_part)
     all_kernel = all_kernel.transpose(1, 0, 2).reshape(KW, CONV)
     at += KW * conv_part
@@ -921,9 +1061,10 @@
     heads = jnp.pad(heads, ((0, 6), (0, 128 - SH)))
     skip = jnp.repeat(own_skip, MP)[None]
 
-    low_normed, mix_rows, query, key_value, step_rows = project(
-        hidden, full_gain[None], mixer, cosine, sine
-    )
+    low_normed, mix_rows, query, key_value, step_rows, gate_rows, gains = project(
+        hidden, mixer, cosine, sine
+    )
+    full_gain, full_gain_two = gains[0], gains[1]
     rim = mix_rows.reshape(2, span, MIXW)[:, span - LEAD :]
     rim = move_spans(rim, 1)
     key_value = key_value.reshape(2, span, 2 * HD)
@@ -932,9 +1073,7 @@
     conv, prepared, turned, message = prep(rim, mix_rows, step_rows, taps, heads)
     messages = [move_spans(message, s) for s in range(1, spans)]
     attended, log_total = attend(at, query, key_values)
-    gate_rows, mixed, state_in, square = scan(
-        low_normed, branch, conv, prepared, turned, skip, messages
-    )
+    mixed, state_in, square = scan(gate_rows, conv, prepared, turned, skip, messages)
     square = group_sum(square[:, 0])
     mamba_scale = lax.rsqrt(square / DSSM + EPSILON)[:, None]
     gate_sigmoid = jax.nn.sigmoid(gate_rows)
@@ -943,25 +1082,15 @@
     mamba_rows = (gated * mamba_scale * mamba_gain).astype(bf16)
     branches = jnp.concatenate([mamba_rows, attended], 1)
     middle = own_hidden + group_scatter(input_product(branches, full_out), side)
+    middle, feed = lax.optimization_barrier((middle, feed))
 
     scale_two = lax.rsqrt(jnp.mean(middle * middle, -1, keepdims=True) + EPSILON)
-    low_two = group_gather((middle * scale_two * full_gain_two).astype(bf16), side)
-    pre = forward_product(low_two, full_gate_up)
-    gate_pre, up_pre = pre[:, :FW], pre[:, FW:]
-    sigmoid = jax.nn.sigmoid(gate_pre)
-    silu = gate_pre * sigmoid
-    activation = (silu * up_pre).astype(bf16)
-
-    back_activation = forward_product(upstream, full_down)
-    back_gate = (back_activation * up_pre * sigmoid * (1.0 + gate_pre * (1.0 - sigmoid))).astype(
-        bf16
-    )
-    back_up = (back_activation * silu).astype(bf16)
-    back_feed = jnp.concatenate([back_gate, back_up], 1)
-    feed_sums = weight_sums(low_two, back_feed, upstream, activation)
-    back_feed, feed_sums = lax.optimization_barrier((back_feed, feed_sums))
-    gradient_feed = scatter(feed_sums)
-    back_normed_two = group_scatter(input_product(back_feed, full_gate_up), side)
+    low_two = feed_gather((middle * scale_two * full_gain_two).astype(bf16))
+    back_feed, activation, own_partial, other_partial, layer_partial = feed_pass(
+        low_two, upstream, feed
+    )
+    gradient_feed = scatter(weight_sums(low_two, back_feed, upstream, activation), feed_groups)
+    back_normed_two = feed_scatter(own_partial, other_partial)
     weighted = back_normed_two * full_gain_two
     gradient_gain_two = jnp.sum(back_normed_two * middle * scale_two, 0)
     back_middle = (
@@ -970,8 +1099,6 @@
         - middle * scale_two**3 * jnp.mean(weighted * middle, -1, keepdims=True)
     )
     low_middle = group_gather(back_middle.astype(bf16), side)
-
-    layer_out = middle + group_scatter(input_product(activation, full_down), side)
 
     back_branches = forward_product(low_middle, full_out)
     back_attended = back_branches[:, SW:].astype(bf16)
@@ -984,15 +1111,20 @@
     low_gate = (
         back_gated * mixed * gate_sigmoid * (1.0 + gate_rows * (1.0 - gate_sigmoid))
     ).astype(bf16)
+    back_attended, gradient_feed = lax.optimization_barrier((back_attended, gradient_feed))
+    back_query, own_back, other_back = attend_back(
+        at, query, key_values, attended, log_total, back_attended, cosine, sine
+    )
+    other_back = other_back.reshape(2, spans - 1, 2, rows, 2 * HD)
+    low_half, high_half = other_back[:, :, 0], other_back[:, :, 1]
+    half_back = jnp.where(side == 0, low_half, high_half).astype(f32)
+    half_back = half_back + swap_side(jnp.where(side == 0, high_half, low_half)).astype(f32)
+    half_back = half_back.astype(bf16)
     back_conv, back_prep, back_skip, *sent = scan_back(
         back_mixed, conv, prepared, turned, skip, state_in, messages
     )
     received = [move_spans(piece, -s) for s, piece in zip(range(1, spans), sent)]
-    back_query, own_back, other_back = attend_back(
-        at, query, key_values, attended, log_total, back_attended, cosine, sine
-    )
-    other_back = other_back.reshape(2, spans - 1, span, 2 * HD)
-    pieces = [move_spans(other_back[:, s - 1], -s) for s in range(1, spans)]
+    pieces = [move_spans(half_back[:, s - 1], -s) for s in range(1, spans)]
     back_mix, back_step, back_rim, tap_sums, head_sums = prep_back(
         rim,
         mix_rows,
@@ -1009,13 +1141,24 @@
     )
     back_rim = move_spans(back_rim, -1)
     back_all = assemble(
-        low_gate, back_mix, back_rim, back_step, back_query, own_back, pieces, cosine, sine
-    )
-    back_all, gradient_feed = lax.optimization_barrier((back_all, gradient_feed))
-    gradient_mixer = scatter(weight_sums(low_normed, back_all, low_middle, branches))
-    back_normed = group_scatter(
-        input_product(back_all[:, :SW], full_gate) + input_product(back_all[:, SW:], mixer), side
-    )
+        jnp.reshape(side, (1,)).astype(jnp.int32),
+        low_gate,
+        back_mix,
+        back_rim,
+        back_step,
+        back_query,
+        own_back,
+        pieces,
+        cosine,
+        sine,
+    )
+    back_all, layer_partial = lax.optimization_barrier((back_all, layer_partial))
+    layer_half = layer_partial.shape[0] // 2
+    layer_out = middle + feed_scatter(layer_partial[:layer_half], layer_partial[layer_half:])
+    gradient_mixer = scatter(
+        weight_sums(low_normed, back_all, low_middle, branches), groups
+    )
+    back_normed = group_scatter(input_product(back_all, mixer), side)
     weighted = back_normed * full_gain
     gradient_gain_one = jnp.sum(back_normed * own_hidden * own_scale_one, 0)
     input_gradient = (
@@ -1042,7 +1185,7 @@
         ),
         BOTH,
     )
-    feature_at = ((dp_at // 2 * spans + span_at) * TP + rank) * part
+    feature_at = (((dp_at // 4 * spans + span_at) * 2 + pair) * TP + rank) * part
     own_gains = lax.dynamic_slice_in_dim(gain_grads, feature_at, part, 1)
     device_at = dp_at * 2 * spans + ctx_at
     own_taps = lax.dynamic_slice_in_dim(tap_grads, device_at * conv_part, conv_part, 1)
@@ -1050,23 +1193,22 @@
         mamba_gain_grad, device_at * gain_part, gain_part, 0
     )
 
-    feed_parts = group_swap(gradient_feed.reshape(TP, part, 3 * FW), rank).astype(f32)
-    mixer_parts = group_swap(gradient_mixer.reshape(TP, part, -1), rank).astype(f32)
+    feed_parts = feed_swap(gradient_feed.reshape(FEED, part, -1), pair, core, side).astype(f32)
+    mixer_parts = group_swap(gradient_mixer.reshape(TP, part, -1), core, side).astype(f32)
 
     def columns(parts, start, width):
         piece = parts[:, :, start : start + width]
-        return piece.transpose(1, 0, 2).reshape(part, TP * width)
+        return piece.transpose(1, 0, 2).reshape(part, parts.shape[0] * width)
 
     def shared(start):
         piece = mixer_parts[:, :, start : start + HD].reshape(KVH, TP // KVH, part, HD)
         return jnp.sum(piece, 1).transpose(1, 0, 2).reshape(part, KVH * HD)
 
-    at = SW + MIXW
-    step_at = SW + STEP_AT
+    at = MIXW
     mix_gradient = jnp.concatenate(
         [
-            columns(mixer_parts, SW, SW),
-            jnp.sum(mixer_parts[:, :, 2 * SW : SW + MIXW], 0),
+            columns(mixer_parts, 0, SW),
+            jnp.sum(mixer_parts[:, :, SW:MIXW], 0),
         ],
         1,
     )
@@ -1074,20 +1216,20 @@
         disorder(layer_out.astype(bf16))[None],
         disorder(input_gradient)[None],
         own_gains[0],
-        columns(mixer_parts, 0, SW),
+        columns(mixer_parts, WIDE, SW),
         mix_gradient,
-        columns(mixer_parts, step_at, SH),
+        columns(mixer_parts, STEP_AT, SH),
         own_taps[:KW],
         own_taps[KW],
         head_grads[0],
         head_grads[1],
         head_grads[2],
         own_mamba_gain,
-        columns(mixer_parts, SW + WIDE, SW).T,
+        columns(mixer_parts, FULL, SW).T,
         columns(mixer_parts, at, QW),
         shared(at + QW),
         shared(at + QW + HD),
-        columns(mixer_parts, 2 * SW + WIDE, QW).T,
+        columns(mixer_parts, FULL + SW, QW).T,
         own_gains[1],
         columns(feed_parts, 0, FW),
         columns(feed_parts, FW, FW),

time: 451 us -> 438 us (0.971)
  local copies, waits for them, and re-layouts: 76.9 us -> 53.5 us
  waiting for transfers between devices: 179 us -> 162 us
  other arithmetic: 19.2 us -> 35.8 us
  Pallas kernels: 36.7 us -> 49.2 us
  matrix products: 15.5 us -> 4.69 us
  starting transfers between devices: 59.1 us -> 65.3 us
    all_gather x3, waiting for transfers between devices: 58.8 us -> 29.8 us  [gather(): lax.all_gather(value, BOTH, axis=0, tiled=True, axis_index_groups=groups)]
    ppermute x4 -> x9, waiting for transfers between devices: 9.61 us -> 27.7 us  [swap_pair(): return lax.ppermute(value, 'dp', pairs)]
    dynamic_update_slice x14 -> x0, local copies, waits for them, and re-layouts: 12.1 us -> none  [group_swap(): result = lax.dynamic_update_slice_in_dim(result, piece, index, 0)]
    pallas_call x2 -> x3, Pallas kernels: 2.4 us -> 13.7 us  [the longest x1 8.54 us: feed_pass(): call(feed_kernel, (4,), [row_block(rows, D), row_block(rows, D), fixed(D,...]
    ppermute x14, waiting for transfers between devices: 37.6 us -> 28.4 us  [move_spans(): return lax.ppermute(value, 'ctx', pairs)]
    ppermute x14, starting transfers between devices: 36.7 us -> 28 us  [move_spans(): return lax.ppermute(value, 'ctx', pairs)]
    ppermute x14 -> x19, starting transfers between devices: 16.5 us -> 24.8 us  [swap_side(): return lax.ppermute(value, 'ctx', pairs)]
    unnamed x208 -> x197, local copies, waits for them, and re-layouts: 31.3 us -> 23.9 us
  transfers between devices with their start and end apart: 51 -> 62, of which waited for: 28 -> 39; matrix products, arithmetic and copies ran while one was open for 14% -> 12% of each run, Pallas kernels for 6% -> 8%
where the time goes in v3:
time: 438 us; the launch traced here: 429 us
  waiting for transfers between devices  162 us (37%)
  starting transfers between devices  65.3 us (15%)
  local copies, waits for them, and re-layouts  53.5 us (12%)
  Pallas kernels  49.2 us (11%)
  blocking collectives  42.4 us (10%)
  other arithmetic  35.8 us (8%)
  between operations  16.2 us (4%)
  matrix products  4.69 us (1%)
    ppermute x19, waiting for transfers between devices, swap_side(): return lax.ppermute(value, 'ctx', pairs)  52.8 us
    psum x1, blocking collectives, local(): lax.psum((jnp.stack([gradient_gain_one, gradient_gain_two]), tap_grads, p...  42.4 us
    all_gather x3, waiting for transfers between devices, gather(): lax.all_gather(value, BOTH, axis=0, tiled=True, axis_index_groups=groups)  29.8 us
    ppermute x14, waiting for transfers between devices, move_spans(): return lax.ppermute(value, 'ctx', pairs)  28.4 us
    ppermute x14, starting transfers between devices, move_spans(): return lax.ppermute(value, 'ctx', pairs)  28 us
    ppermute x9, waiting for transfers between devices, swap_pair(): return lax.ppermute(value, 'dp', pairs)  27.7 us
    ppermute x19, starting transfers between devices, swap_side(): return lax.ppermute(value, 'ctx', pairs)  24.8 us
    unnamed x197, local copies, waits for them, and re-layouts  23.9 us
  transfers between devices with their start and end apart: 62, of which 39 were waited for; matrix products, arithmetic and copies ran while one was open for 12% of the time, Pallas kernels for 8%

profile of v3, /device:TPU:0, one launch (start us, length us, event | category | flops | bytes accessed | tf_op | source)
XLA Modules:
  0.0 428.9 jit_solution(15165748389551993967)
XLA Ops:
  17.7 2.9 collective-permute-start.1
  21.5 4.0 collective-permute-done.1
  33.7 3.5 collective-permute-done.9
  39.1 3.7 collective-permute-done.7
  43.6 4.3 %collective-permute-done.5 = bf16[2,2,32,768]{3,2,0,1:T(8,128)(2,1)S(1)} collective-permute-done((bf16[2,2,32,768]{3,2,0,1:T(8,128)(2,1)S(1)}, bf16[2,2,32,768]{3,2,0,1:T(8,128)(2,1)S(1)}, u32[]{:S(2)}, u32[]{:S(2)}) %collective-permute-start.5) | collective-permute-done | bytes 196640 | tf_op jit(solution)/shard_map/ppermute | solution.py:58
  49.4 4.5 %collective-permute-done.10 = bf16[2,128,1024]{1,2,0:T(8,128)(2,1)S(1)} collective-permute-done((bf16[2,128,1024]{1,2,0:T(8,128)(2,1)S(1)}, bf16[2,128,1024]{1,2,0:T(8,128)(2,1)S(1)}, u32[]{:S(2)}, u32[]{:S(2)}) %collective-permute-start.10) | collective-permute-done | bytes 524320 | tf_op jit(solution)/shard_map/ppermute | solution.py:63
  57.6 7.8 %collective-permute-done.6 = bf16[2,2,32,768]{3,2,0,1:T(8,128)(2,1)S(1)} collective-permute-done((bf16[2,2,32,768]{3,2,0,1:T(8,128)(2,1)S(1)}, bf16[2,2,32,768]{3,2,0,1:T(8,128)(2,1)S(1)}, u32[]{:S(2)}, u32[]{:S(2)}) %collective-permute-start.6) | collective-permute-done | bytes 196640 | tf_op jit(solution)/shard_map/ppermute | solution.py:63
  69.1 20.6 %all-gather.4.cloned.1.call-done.weight = bf16[1024,1408]{1,0:T(8,128)(2,1)} async-done(((bf16[128,1408]{1,0:T(8,128)(2,1)}), bf16[1024,1408]{1,0:T(8,128)(2,1)}) %all-gather.4.cloned.1.call-update) | async-done | bytes 2883600 | tf_op jit(solution)/shard_map/all_gather | solution.py:949
  91.8 4.7 %shard_map.364 = (bf16[512,1024]{1,0:T(8,128)(2,1)S(1)}, bf16[512,640]{1,0:T(8,128)(2,1)S(1)}, bf16[512,128]{1,0:T(8,128)(2,1)S(1)}, bf16[512,128]{1,0:T(8,128)(...) custom-call(bf16[512,1024]{1,0:T(8,128)(2,1)S(1)} %pad_maximum_fusion.2.hidden, ...), custom_call_target="tpu_custom_call" | custom-call | tf_op jit(solution)/shard_map/pallas_call | solution.py:288
  98.1 3.1 collective-permute-start.12
  102.7 4.3 shard_map.365
  108.3 5.6 %collective-permute-start.15 = (bf16[2,400,128]{2,1,0:T(8,128)(2,1)}, bf16[2,400,128]{2,1,0:T(8,128)(2,1)}, u32[]{:S(2)}, u32[]{:S(2)}) collective-permute-start(bf16[2,400,128]{2,1,0:T(8,128)(2,1)} %get-tuple-element.107), channel_id=1, source_target_pairs={{0,6},{1,7},{8,14},{9,15},{16,22},{17,23},{24,30},{25,31}} | collective-permute-start | bytes 614408 | tf_op jit(solution)/shard_map/ppermute | solution.py:69
  113.9 2.0 collective-permute-start.14
  115.9 2.5 collective-permute-start.13
  118.7 1.9 collective-permute-start.20
  120.6 1.9 collective-permute-start.19
  124.8 6.4 %collective-permute-done.14.refs_6_.refs_7_ = bf16[2,400,128]{2,1,0:T(8,128)(2,1)} collective-permute-done((bf16[2,400,128]{2,1,0:T(8,128)(2,1)}, bf16[2,400,128]{2,1,0:T(8,128)(2,1)}, u32[]{:S(2)}, u32[]{:S(2)}) %collective-permute-start.14) | collective-permute-done | bytes 204832 | tf_op jit(solution)/shard_map/ppermute | solution.py:69
  131.2 5.1 %collective-permute-done.13.refs_5_.refs_6_ = bf16[2,400,128]{2,1,0:T(8,128)(2,1)} collective-permute-done((bf16[2,400,128]{2,1,0:T(8,128)(2,1)}, bf16[2,400,128]{2,1,0:T(8,128)(2,1)}, u32[]{:S(2)}, u32[]{:S(2)}) %collective-permute-start.13) | collective-permute-done | bytes 204832 | tf_op jit(solution)/shard_map/ppermute | solution.py:69
  137.0 3.5 shard_map.366
  145.4 2.6 shard_map.367
  152.3 2.2 fusion.57
  154.7 2.6 collective-permute-done.21
  158.8 7.1 %collective-permute-done.22 = bf16[128,1024]{1,0:T(8,128)(2,1)S(1)} collective-permute-done((bf16[128,1024]{1,0:T(8,128)(2,1)S(1)}, bf16[128,1024]{1,0:T(8,128)(2,1)S(1)}, u32[]{:S(2)}, u32[]{:S(2)}) %collective-permute-start.22) | collective-permute-done | bytes 262176 | tf_op jit(solution)/shard_map/ppermute | solution.py:58
  166.9 9.2 %all-gather.8.cloned.1.call-done.gate_up.down = bf16[1024,768]{1,0:T(8,128)(2,1)} async-done(((bf16[256,768]{1,0:T(8,128)(2,1)}), bf16[1024,768]{1,0:T(8,128)(2,1)}) %all-gather.8.cloned.1.call-update) | async-done | bytes 1572880 | tf_op jit(solution)/shard_map/all_gather | solution.py:949
  178.9 2.2 collective-permute-start.24
  188.3 4.7 %collective-permute-done.25 = bf16[128,1024]{1,0:T(8,128)(2,1)S(1)} collective-permute-done((bf16[128,1024]{1,0:T(8,128)(2,1)S(1)}, bf16[128,1024]{1,0:T(8,128)(2,1)S(1)}, u32[]{:S(2)}, u32[]{:S(2)}) %collective-permute-start.25) | collective-permute-done | bytes 262176 | tf_op jit(solution)/shard_map/ppermute | solution.py:63
  193.5 2.6 collective-permute-done.27
  197.7 8.5 %shard_map.368 = (bf16[1024,512]{1,0:T(8,128)(2,1)S(1)}, bf16[1024,256]{1,0:T(8,128)(2,1)S(1)}, f32[512,1024]{1,0:T(8,128)}, bf16[512,1024]{1,0:T(8,128)(2,1)S(1)}, bf16[1024,1024]{1,0:T(8,128)(2,1)}) custom-call(bf16[1024,1024]{1,0:T(8,128)(2,1)} %copy-done, bf16[1024,1024]{1,0:T(8,128)(2,1)} %pad_maximum_fusion.upstream.second_left, ...), custom_call_target="tpu_custom_call" | custom-call | tf_op jit(solution)/shard_map/pallas_call | solution.py:343
  206.4 2.5 collective-permute-done.28
  209.0 2.1 fusion.62
  214.2 5.3 %collective-permute-done.30 = bf16[128,1024]{1,0:T(8,128)(2,1)S(1)} collective-permute-done((bf16[128,1024]{1,0:T(8,128)(2,1)S(1)}, bf16[128,1024]{1,0:T(8,128)(2,1)S(1)}, u32[]{:S(2)}, u32[]{:S(2)}) %collective-permute-start.30) | collective-permute-done | bytes 262176 | tf_op jit(solution)/shard_map/ppermute | solution.py:58
  230.8 4.2 shard_map.371
  243.7 5.2 %collective-permute-done.33 = bf16[128,1024]{1,0:T(8,128)(2,1)S(1)} collective-permute-done((bf16[128,1024]{1,0:T(8,128)(2,1)S(1)}, bf16[128,1024]{1,0:T(8,128)(2,1)S(1)}, u32[]{:S(2)}, u32[]{:S(2)}) %collective-permute-start.33) | collective-permute-done | bytes 262176 | tf_op jit(solution)/shard_map/ppermute | solution.py:58
  259.0 5.8 %shard_map.369 = (f32[512,640]{1,0:T(8,128)S(1)}, f32[512,256]{1,0:T(8,128)S(1)}, f32[2,8,128]{2,1,0:T(8,128)S(1)}, bf16[2,384,128]{2,1,0:T(8,128)(2,1)}, bf16[2...) custom-call(f32[512,384]{1,0:T(8,128)S(1)} %get-tuple-element.290.refs_0_, ...), custom_call_target="tpu_custom_call" | custom-call | tf_op jit(solution)/shard_map/pallas_call | solution.py:654
  270.7 5.7 %reduce-scatter.3.cloned.1.call-done = bf16[256,768]{1,0:T(8,128)(2,1)} async-done(((bf16[1024,768]{1,0:T(8,128)(2,1)}), bf16[256,768]{1,0:T(8,128)(2,1)}) %reduce-scatter.3.cloned.1.call-update) | async-done | bytes 393232 | tf_op jit(solution)/shard_map/reduce_scatter | solution.py:952
  278.4 4.3 %shard_map.372 = (bf16[512,128]{1,0:T(8,128)(2,1)S(1)}, f32[2,256,128]{2,1,0:T(8,128)S(1)}, bf16[2,768,128]{2,1,0:T(8,128)(2,1)S(1)}) custom-call(s32[1]{0:T(128)} %bitcast.76.at, bf16[512,128]{1,0:T(8,128)(2,1)S(1)} %copy-done.30, bf16[2,1024,128]{2,1,0:T(8,128)(2,1)S(1)} %copy-done.5, bf16[512,128]{1,0:T(8,128)(2,1)S(1)} %copy-done.16, ...), custom_call_target="tpu_custom_call" | custom-call | tf_op jit(solution)/shard_map/pallas_call | solution.py:436
  284.4 9.7 %collective-permute-done.38.refs_12_ = bf16[2,384,128]{2,1,0:T(8,128)(2,1)} collective-permute-done((bf16[2,384,128]{2,1,0:T(8,128)(2,1)}, bf16[2,384,128]{2,1,0:T(8,128)(2,1)}, u32[]{:S(2)}, u32[]{:S(2)}) %collective-permute-start.38) | collective-permute-done | bytes 196640 | tf_op jit(solution)/shard_map/ppermute | solution.py:69
  294.2 6.5 %shard_map.370 = (f32[512,640]{1,0:T(8,128)S(1)}, f32[512,128]{1,0:T(8,128)S(1)}, f32[2,8,640]{2,1,0:T(8,128)S(1)}, f32[2,8,640]{2,1,0:T(8,128)S(1)}, f32[2,8,128]{2,1,0:T(8,128)S(1)}) custom-call(bf16[2,8,640]{2,1,0:T(8,128)(2,1)S(1)} %copy-done.39, bf16[512,640]{1,0:T(8,128)(2,1)S(1)} %copy-done.7, f32[512,128]{1,0:T(8,128)S(1)} %copy-done.22, ...), custom_call_target="tpu_custom_call" | custom-call | tf_op jit(solution)/shard_map/pallas_call | solution.py:771
  306.7 3.7 collective-permute-done.44.refs_11_
  310.3 2.0 collective-permute-done.43.refs_10_
  313.6 4.4 %shard_map.374 = bf16[1024,1920]{1,0:T(8,128)(2,1)} custom-call(bf16[512,1024]{1,0:T(8,128)(2,1)S(1)} %copy-done.18, bf16[512,1408]{1,0:T(8,128)(2,1)S(1)} %shard_map.373.first_right, bf16[512,1024]{1,0:T(8,128)(2,1)S(1)} %pad_maximum_fusion.4.second_left, bf16[512,512]{1,0:T(8,128)(2,1)S(1)} %pad_maximum_fusion.8.second_right), custom_call_target="tpu_custom_call" | custom-call | tf_op jit(solution)/shard_map/pallas_call | solution.py:878
  323.0 5.7 %collective-permute-done.55 = bf16[2,2,32,768]{3,2,1,0:T(8,128)(2,1)S(1)} collective-permute-done((bf16[2,2,32,768]{3,2,1,0:T(8,128)(2,1)S(1)}, bf16[2,2,32,768]{3,2,1,0:T(8,128)(2,1)S(1)}, u32[]{:S(2)}, u32[]{:S(2)}) %collective-permute-start.55) | collective-permute-done | bytes 196640 | tf_op jit(solution)/shard_map/ppermute | solution.py:58
  332.4 3.3 collective-permute-done.56
  342.0 6.0 %collective-permute-done.47 = bf16[128,1024]{1,0:T(8,128)(2,1)S(1)} collective-permute-done((bf16[128,1024]{1,0:T(8,128)(2,1)S(1)}, bf16[128,1024]{1,0:T(8,128)(2,1)S(1)}, u32[]{:S(2)}, u32[]{:S(2)}) %collective-permute-start.47) | collective-permute-done | bytes 262176 | tf_op jit(solution)/shard_map/ppermute | solution.py:58
  347.9 4.4 %collective-permute-done.46 = bf16[128,1024]{1,0:T(8,128)(2,1)S(1)} collective-permute-done((bf16[128,1024]{1,0:T(8,128)(2,1)S(1)}, bf16[128,1024]{1,0:T(8,128)(2,1)S(1)}, u32[]{:S(2)}, u32[]{:S(2)}) %collective-permute-start.46) | collective-permute-done | bytes 262176 | tf_op jit(solution)/shard_map/ppermute | solution.py:63
  354.9 42.4 %all-reduce.3 = (f32[2,1024]{1,0:T(2,128)S(1)}, f32[5,1792]{1,0:T(8,128)S(1)}, f32[3,24]{1,0:T(4,128)S(1)}, f32[1536]{0:T(1024)S(1)}) all-reduce(f32[2,1024]{1,0:T(2,128)S(1)} %pad_maximum_fusion.32, f32[5,1792]{1,0:T(8,128)S(1)} %copy-done.71, f32[3,24]{1,0:T(4,128)S(1)} %dynamic_update_slice.10, ...), channel_id=1, replica_groups=mesh['dp'=4,'ctx'=8] {'dp','ctx'}, use_global_device_ids=true, to_apply=%region_8.9 | all-reduce | flops 12616 | bytes 100928 | tf_op jit(solution)/shard_map/psum | solution.py:1179
  398.7 3.7 reduce-scatter.5.cloned.1.call-done
  411.3 4.7 %collective-permute-done.53 = bf16[2,32,1920]{2,1,0:T(8,128)(2,1)S(1)} collective-permute-done((bf16[2,32,1920]{2,1,0:T(8,128)(2,1)S(1)}, bf16[2,32,1920]{2,1,0:T(8,128)(2,1)S(1)}, u32[]{:S(2)}, u32[]{:S(2)}) %collective-permute-start.53) | collective-permute-done | bytes 245792 | tf_op jit(solution)/shard_map/ppermute | solution.py:58
  (502 shorter events, 147.1 us)
Async XLA Ops:
  7.2 82.5 %all-gather.4.cloned.1.call-start = ((), (), s32[]{:S(2)}) async-start(), calls=%async_computation.2 | async-start | bytes 3244032 | tf_op jit(solution)/shard_map/all_gather | solution.py:949
  17.7 7.8 %collective-permute-start.1 = (bf16[2,32,1408]{2,1,0:T(8,128)(2,1)S(1)}, bf16[2,32,1408]{2,1,0:T(8,128)(2,1)S(1)}, u32[]{:S(2)}, u32[]{:S(2)}) collective-permute-start(bf16[2,32,1408]{2,1,0:T(8,128)(2,1)S(1)} %select_bitcast_fusion.11), channel_id=1, source_target_pairs={{0,1},{1,0},{2,3},{3,2},{4,5},{5,4},{6,7},{7,6},{8,9},{9,8},{10,11... | collective-permute-start | bytes 540680 | tf_op jit(solution)/shard_map/ppermute | solution.py:58
  26.4 125.9 %all-gather.6.cloned.1.call-start = ((), (), s32[]{:S(2)}) async-start(), calls=%async_computation.3 | async-start | bytes 1179648 | tf_op jit(solution)/shard_map/all_gather | solution.py:949
  28.0 9.2 %collective-permute-start.9 = (bf16[128,1024]{0,1:T(8,128)(2,1)S(1)}, bf16[128,1024]{0,1:T(8,128)(2,1)S(1)}, u32[]{:S(2)}, u32[]{:S(2)}) collective-permute-start(bf16[128,1024]{0,1:T(8,128)(2,1)S(1)} %bitcast.348), channel_id=1, source_target_pairs={{0,1},{1,0},{2,3},{3,2},{4,5},{5,4},{6,7},{7,6},{8,9},{9,8},{10,11... | collective-permute-start | bytes 786440 | tf_op jit(solution)/shard_map/ppermute | solution.py:58
  29.8 13.0 %collective-permute-start.7 = (bf16[128,1024]{1,0:T(8,128)(2,1)S(1)}, bf16[128,1024]{1,0:T(8,128)(2,1)S(1)}, u32[]{:S(2)}, u32[]{:S(2)}) collective-permute-start(bf16[128,1024]{1,0:T(8,128)(2,1)S(1)} %copy.402), channel_id=1, source_target_pairs={{0,1},{1,0},{2,3},{3,2},{4,5},{5,4},{6,7},{7,6},{8,9},{9,8},{10,11... | collective-permute-start | bytes 786440 | tf_op jit(solution)/shard_map/ppermute | solution.py:58
  31.0 25.0 %collective-permute-start.3 = (bf16[2,32,512]{2,1,0:T(8,128)(2,1)}, bf16[2,32,512]{2,1,0:T(8,128)(2,1)}, u32[]{:S(2)}, u32[]{:S(2)}) collective-permute-start(bf16[2,32,512]{2,1,0:T(8,128)(2,1)} %select_bitcast_fusion.14), channel_id=1, source_target_pairs={{0,1},{1,0},{2,3},{3,2},{4,5},{5,4},{6,7},{7,6},{8,9},{9,8},{10,11... | collective-permute-start | bytes 196616 | tf_op jit(solution)/shard_map/ppermute | solution.py:58
  32.9 15.0 %collective-permute-start.5 = (bf16[2,2,32,768]{3,2,0,1:T(8,128)(2,1)S(1)}, bf16[2,2,32,768]{3,2,0,1:T(8,128)(2,1)S(1)}, u32[]{:S(2)}, u32[]{:S(2)}) collective-permute-start(bf16[2,2,32,768]{3,2,0,1:T(8,128)(2,1)S(1)} %get-tuple-element.283), channel_id=1, source_target_pairs={{0,1},{1,0},{2,3},{3,2},{4,5},{5,4},{6,7},{7,6},{8,9},{9,8},{10,11... | collective-permute-start | bytes 589832 | tf_op jit(solution)/shard_map/ppermute | solution.py:58
  37.2 16.6 %collective-permute-start.10 = (bf16[2,128,1024]{1,2,0:T(8,128)(2,1)S(1)}, bf16[2,128,1024]{1,2,0:T(8,128)(2,1)S(1)}, u32[]{:S(2)}, u32[]{:S(2)}) collective-permute-start(bf16[2,128,1024]{1,2,0:T(8,128)(2,1)S(1)} %get-tuple-element.327), channel_id=1, source_target_pairs={{0,16},{8,24},{16,0},{24,8},{1,17},{9,25},{17,1},{25,9},{2,18},{10... | collective-permute-start | bytes 1572872 | tf_op jit(solution)/shard_map/ppermute | solution.py:63
  43.6 22.6 %collective-permute-start.8 = (bf16[256,1024]{1,0:T(8,128)(2,1)}, bf16[256,1024]{1,0:T(8,128)(2,1)}, u32[]{:S(2)}, u32[]{:S(2)}) collective-permute-start(bf16[256,1024]{1,0:T(8,128)(2,1)} %pad_maximum_fusion.5), channel_id=1, source_target_pairs={{0,8},{8,0},{16,24},{24,16},{1,9},{9,1},{17,25},{25,17},{2,10},{10... | collective-permute-start | bytes 1572872 | tf_op jit(solution)/shard_map/ppermute | solution.py:53
  55.0 12.4 %collective-permute-start.11 = (bf16[512,1024]{1,0:T(8,128)(2,1)S(1)}, bf16[512,1024]{1,0:T(8,128)(2,1)S(1)}, u32[]{:S(2)}, u32[]{:S(2)}) collective-permute-start(bf16[512,1024]{1,0:T(8,128)(2,1)S(1)} %pad_maximum_fusion.3), channel_id=1, source_target_pairs={{0,8},{8,0},{16,24},{24,16},{1,9},{9,1},{17,25},{25,17},{2,10},{10... | collective-permute-start | bytes 3145736 | tf_op jit(solution)/shard_map/ppermute | solution.py:53
  55.6 9.7 %collective-permute-start.6 = (bf16[2,2,32,768]{3,2,0,1:T(8,128)(2,1)S(1)}, bf16[2,2,32,768]{3,2,0,1:T(8,128)(2,1)S(1)}, u32[]{:S(2)}, u32[]{:S(2)}) collective-permute-start(bf16[2,2,32,768]{3,2,0,1:T(8,128)(2,1)S(1)} %fusion.13), channel_id=1, source_target_pairs={{0,16},{8,24},{16,0},{24,8},{1,17},{9,25},{17,1},{25,9},{2,18},{10... | collective-permute-start | bytes 589832 | tf_op jit(solution)/shard_map/ppermute | solution.py:63
  89.7 86.3 %all-gather.8.cloned.1.call-start = ((), (), s32[]{:S(2)}) async-start(), calls=%async_computation.4 | async-start | bytes 1966080 | tf_op jit(solution)/shard_map/all_gather | solution.py:949
  108.3 15.0 %collective-permute-start.15 = (bf16[2,400,128]{2,1,0:T(8,128)(2,1)}, bf16[2,400,128]{2,1,0:T(8,128)(2,1)}, u32[]{:S(2)}, u32[]{:S(2)}) collective-permute-start(bf16[2,400,128]{2,1,0:T(8,128)(2,1)} %get-tuple-element.107), channel_id=1, source_target_pairs={{0,6},{1,7},{8,14},{9,15},{16,22},{17,23},{24,30},{25,31}} | collective-permute-start | bytes 614408 | tf_op jit(solution)/shard_map/ppermute | solution.py:69
  113.9 17.2 %collective-permute-start.14 = (bf16[2,400,128]{2,1,0:T(8,128)(2,1)}, bf16[2,400,128]{2,1,0:T(8,128)(2,1)}, u32[]{:S(2)}, u32[]{:S(2)}) collective-permute-start(bf16[2,400,128]{2,1,0:T(8,128)(2,1)} %get-tuple-element.107), channel_id=1, source_target_pairs={{0,4},{1,5},{2,6},{3,7},{8,12},{9,13},{10,14},{11,15},{16,20},{17,... | collective-permute-start | bytes 614408 | tf_op jit(solution)/shard_map/ppermute | solution.py:69
  115.9 20.4 %collective-permute-start.13 = (bf16[2,400,128]{2,1,0:T(8,128)(2,1)}, bf16[2,400,128]{2,1,0:T(8,128)(2,1)}, u32[]{:S(2)}, u32[]{:S(2)}) collective-permute-start(bf16[2,400,128]{2,1,0:T(8,128)(2,1)} %get-tuple-element.107), channel_id=1, source_target_pairs={{0,2},{1,3},{2,4},{3,5},{4,6},{5,7},{8,10},{9,11},{10,12},{11,13},... | collective-permute-start | bytes 614408 | tf_op jit(solution)/shard_map/ppermute | solution.py:69
  118.7 25.6 %collective-permute-start.20 = (bf16[2,256,128]{2,1,0:T(8,128)(2,1)}, bf16[2,256,128]{2,1,0:T(8,128)(2,1)}, u32[]{:S(2)}, u32[]{:S(2)}) collective-permute-start(bf16[2,256,128]{2,1,0:T(8,128)(2,1)} %bitcast.77), channel_id=1, source_target_pairs={{0,6},{1,7},{8,14},{9,15},{16,22},{17,23},{24,30},{25,31}} | collective-permute-start | bytes 393224 | tf_op jit(solution)/shard_map/ppermute | solution.py:69
  120.6 23.7 %collective-permute-start.19 = (bf16[2,256,128]{2,1,0:T(8,128)(2,1)}, bf16[2,256,128]{2,1,0:T(8,128)(2,1)}, u32[]{:S(2)}, u32[]{:S(2)}) collective-permute-start(bf16[2,256,128]{2,1,0:T(8,128)(2,1)} %bitcast.77), channel_id=1, source_target_pairs={{0,4},{1,5},{2,6},{3,7},{8,12},{9,13},{10,14},{11,15},{16,20},{17,... | collective-permute-start | bytes 393224 | tf_op jit(solution)/shard_map/ppermute | solution.py:69
  123.3 153.2 %reduce-scatter.3.cloned.1.call-start = ((), (), s32[]{:S(2)}) async-start(), calls=%async_computation.5 | async-start | bytes 1966080 | tf_op jit(solution)/shard_map/reduce_scatter | solution.py:952
  123.3 20.9 %collective-permute-start.18 = (bf16[2,256,128]{2,1,0:T(8,128)(2,1)}, bf16[2,256,128]{2,1,0:T(8,128)(2,1)S(1)}, u32[]{:S(2)}, u32[]{:S(2)}) collective-permute-start(bf16[2,256,128]{2,1,0:T(8,128)(2,1)} %bitcast.77), channel_id=1, source_target_pairs={{0,2},{1,3},{2,4},{3,5},{4,6},{5,7},{8,10},{9,11},{10,12},{11,13},... | collective-permute-start | bytes 393224 | tf_op jit(solution)/shard_map/ppermute | solution.py:69
  142.7 7.4 %collective-permute-start.17 = (f32[512]{0:T(512)S(1)}, f32[512]{0:T(512)S(1)}, u32[]{:S(2)}, u32[]{:S(2)}) collective-permute-start(f32[512]{0:T(512)S(1)} %maximum_add_fusion.1), channel_id=1, source_target_pairs={{0,1},{1,0},{2,3},{3,2},{4,5},{5,4},{6,7},{7,6},{8,9},{9,8},{10,11... | collective-permute-start | bytes 6152 | tf_op jit(solution)/shard_map/ppermute | solution.py:58
  157.5 8.4 %collective-permute-start.22 = (bf16[128,1024]{1,0:T(8,128)(2,1)S(1)}, bf16[128,1024]{1,0:T(8,128)(2,1)S(1)}, u32[]{:S(2)}, u32[]{:S(2)}) collective-permute-start(bf16[128,1024]{1,0:T(8,128)(2,1)S(1)} %select_convert_fusion.1), channel_id=1, source_target_pairs={{0,1},{1,0},{2,3},{3,2},{4,5},{5,4},{6,7},{7,6},{8,9},{9,8},{10,11... | collective-permute-start | bytes 786440 | tf_op jit(solution)/shard_map/ppermute | solution.py:58
  178.9 5.6 %collective-permute-start.24 = (bf16[64,1024]{1,0:T(8,128)(2,1)S(1)}, bf16[64,1024]{1,0:T(8,128)(2,1)S(1)}, u32[]{:S(2)}, u32[]{:S(2)}) collective-permute-start(bf16[64,1024]{1,0:T(8,128)(2,1)S(1)} %get-tuple-element.346), channel_id=1, source_target_pairs={{0,16},{8,24},{16,0},{24,8},{1,17},{9,25},{17,1},{25,9},{2,18},{10... | collective-permute-start | bytes 393224 | tf_op jit(solution)/shard_map/ppermute | solution.py:63
  186.2 6.8 %collective-permute-start.25 = (bf16[128,1024]{1,0:T(8,128)(2,1)S(1)}, bf16[128,1024]{1,0:T(8,128)(2,1)S(1)}, u32[]{:S(2)}, u32[]{:S(2)}) collective-permute-start(bf16[128,1024]{1,0:T(8,128)(2,1)S(1)} %pad_maximum_fusion.14), channel_id=1, source_target_pairs={{0,16},{8,24},{16,0},{24,8},{1,17},{9,25},{17,1},{25,9},{2,18},{10... | collective-permute-start | bytes 786440 | tf_op jit(solution)/shard_map/ppermute | solution.py:63
  186.5 6.8 %collective-permute-start.26 = (bf16[128,1024]{1,0:T(8,128)(2,1)S(1)}, bf16[128,1024]{1,0:T(8,128)(2,1)S(1)}, u32[]{:S(2)}, u32[]{:S(2)}) collective-permute-start(bf16[128,1024]{1,0:T(8,128)(2,1)S(1)} %pad_maximum_fusion.15), channel_id=1, source_target_pairs={{0,1},{1,0},{2,3},{3,2},{4,5},{5,4},{6,7},{7,6},{8,9},{9,8},{10,11... | collective-permute-start | bytes 786440 | tf_op jit(solution)/shard_map/ppermute | solution.py:58
  211.2 8.4 %collective-permute-start.30 = (bf16[128,1024]{1,0:T(8,128)(2,1)S(1)}, bf16[128,1024]{1,0:T(8,128)(2,1)S(1)}, u32[]{:S(2)}, u32[]{:S(2)}) collective-permute-start(bf16[128,1024]{1,0:T(8,128)(2,1)S(1)} %get-tuple-element.298), channel_id=1, source_target_pairs={{0,1},{1,0},{2,3},{3,2},{4,5},{5,4},{6,7},{7,6},{8,9},{9,8},{10,11... | collective-permute-start | bytes 786440 | tf_op jit(solution)/shard_map/ppermute | solution.py:58
  212.6 8.1 %collective-permute-start.29 = (bf16[128,1024]{1,0:T(8,128)(2,1)S(1)}, bf16[128,1024]{1,0:T(8,128)(2,1)S(1)}, u32[]{:S(2)}, u32[]{:S(2)}) collective-permute-start(bf16[128,1024]{1,0:T(8,128)(2,1)S(1)} %get-tuple-element.299), channel_id=1, source_target_pairs={{0,16},{8,24},{16,0},{24,8},{1,17},{9,25},{17,1},{25,9},{2,18},{10... | collective-permute-start | bytes 786440 | tf_op jit(solution)/shard_map/ppermute | solution.py:63
  223.0 13.5 %collective-permute-start.32 = (bf16[64,1024]{1,0:T(8,128)(2,1)}, bf16[64,1024]{1,0:T(8,128)(2,1)}, u32[]{:S(2)}, u32[]{:S(2)}) collective-permute-start(bf16[64,1024]{1,0:T(8,128)(2,1)} %slice.907), channel_id=1, source_target_pairs={{0,16},{8,24},{16,0},{24,8},{1,17},{9,25},{17,1},{25,9},{2,18},{10... | collective-permute-start | bytes 393224 | tf_op jit(solution)/shard_map/ppermute | solution.py:63
  224.7 11.9 %collective-permute-start.31 = (bf16[64,1024]{1,0:T(8,128)(2,1)}, bf16[64,1024]{1,0:T(8,128)(2,1)}, u32[]{:S(2)}, u32[]{:S(2)}) collective-permute-start(bf16[64,1024]{1,0:T(8,128)(2,1)} %slice.908), channel_id=1, source_target_pairs={{0,1},{1,0},{2,3},{3,2},{4,5},{5,4},{6,7},{7,6},{8,9},{9,8},{10,11... | collective-permute-start | bytes 393224 | tf_op jit(solution)/shard_map/ppermute | solution.py:58
  236.2 166.2 %reduce-scatter.5.cloned.1.call-start = ((), (), s32[]{:S(2)}) async-start(), calls=%async_computation.6 | async-start | bytes 4423680 | tf_op jit(solution)/shard_map/reduce_scatter | solution.py:952
  242.2 6.7 %collective-permute-start.33 = (bf16[128,1024]{1,0:T(8,128)(2,1)S(1)}, bf16[128,1024]{1,0:T(8,128)(2,1)S(1)}, u32[]{:S(2)}, u32[]{:S(2)}) collective-permute-start(bf16[128,1024]{1,0:T(8,128)(2,1)S(1)} %get-tuple-element.277), channel_id=1, source_target_pairs={{0,1},{1,0},{2,3},{3,2},{4,5},{5,4},{6,7},{7,6},{8,9},{9,8},{10,11... | collective-permute-start | bytes 786440 | tf_op jit(solution)/shard_map/ppermute | solution.py:58
  266.7 17.7 %collective-permute-start.37 = (bf16[2,384,128]{2,1,0:T(8,128)(2,1)}, bf16[2,384,128]{2,1,0:T(8,128)(2,1)}, u32[]{:S(2)}, u32[]{:S(2)}) collective-permute-start(bf16[2,384,128]{2,1,0:T(8,128)(2,1)} %get-tuple-element.133), channel_id=1, source_target_pairs={{2,0},{3,1},{4,2},{5,3},{6,4},{7,5},{10,8},{11,9},{12,10},{13,11},... | collective-permute-start | bytes 589832 | tf_op jit(solution)/shard_map/ppermute | solution.py:69
  268.1 26.0 %collective-permute-start.38 = (bf16[2,384,128]{2,1,0:T(8,128)(2,1)}, bf16[2,384,128]{2,1,0:T(8,128)(2,1)}, u32[]{:S(2)}, u32[]{:S(2)}) collective-permute-start(bf16[2,384,128]{2,1,0:T(8,128)(2,1)} %get-tuple-element.134), channel_id=1, source_target_pairs={{4,0},{5,1},{6,2},{7,3},{12,8},{13,9},{14,10},{15,11},{20,16},{21,... | collective-permute-start | bytes 589832 | tf_op jit(solution)/shard_map/ppermute | solution.py:69
  269.4 24.7 %collective-permute-start.39 = (bf16[2,384,128]{2,1,0:T(8,128)(2,1)}, bf16[2,384,128]{2,1,0:T(8,128)(2,1)}, u32[]{:S(2)}, u32[]{:S(2)}) collective-permute-start(bf16[2,384,128]{2,1,0:T(8,128)(2,1)} %get-tuple-element.135), channel_id=1, source_target_pairs={{6,0},{7,1},{14,8},{15,9},{22,16},{23,17},{30,24},{31,25}} | collective-permute-start | bytes 589832 | tf_op jit(solution)/shard_map/ppermute | solution.py:69
  282.8 19.3 %collective-permute-start.41 = (bf16[2,3,128,128]{3,2,0,1:T(8,128)(2,1)S(1)}, bf16[2,3,128,128]{3,2,0,1:T(8,128)(2,1)S(1)}, u32[]{:S(2)}, u32[]{:S(2)}) collective-permute-start(bf16[2,3,128,128]{3,2,0,1:T(8,128)(2,1)S(1)} %select_bitcast_fusion.6), channel_id=1, source_target_pairs={{0,1},{1,0},{2,3},{3,2},{4,5},{5,4},{6,7},{7,6},{8,9},{9,8},{10,11... | collective-permute-start | bytes 589832 | tf_op jit(solution)/shard_map/ppermute | solution.py:58
  300.6 6.0 %collective-permute-start.40 = (f32[2,8,640]{2,1,0:T(8,128)S(1)}, f32[2,8,640]{2,1,0:T(8,128)S(1)}, u32[]{:S(2)}, u32[]{:S(2)}) collective-permute-start(f32[2,8,640]{2,1,0:T(8,128)S(1)} %get-tuple-element.137), channel_id=1, source_target_pairs={{2,0},{3,1},{4,2},{5,3},{6,4},{7,5},{10,8},{11,9},{12,10},{13,11},... | collective-permute-start | bytes 122888 | tf_op jit(solution)/shard_map/ppermute | solution.py:69
  302.2 8.1 %collective-permute-start.44 = (bf16[2,128,128]{2,1,0:T(8,128)(2,1)S(1)}, bf16[2,128,128]{2,1,0:T(8,128)(2,1)S(1)}, u32[]{:S(2)}, u32[]{:S(2)}) collective-permute-start(bf16[2,128,128]{2,1,0:T(8,128)(2,1)S(1)} %get-tuple-element.348), channel_id=1, source_target_pairs={{6,0},{7,1},{14,8},{15,9},{22,16},{23,17},{30,24},{31,25}} | collective-permute-start | bytes 196616 | tf_op jit(solution)/shard_map/ppermute | solution.py:69
  303.5 8.9 %collective-permute-start.43 = (bf16[2,128,128]{2,1,0:T(8,128)(2,1)S(1)}, bf16[2,128,128]{2,1,0:T(8,128)(2,1)S(1)}, u32[]{:S(2)}, u32[]{:S(2)}) collective-permute-start(bf16[2,128,128]{2,1,0:T(8,128)(2,1)S(1)} %get-tuple-element.349), channel_id=1, source_target_pairs={{4,0},{5,1},{6,2},{7,3},{12,8},{13,9},{14,10},{15,11},{20,16},{21,... | collective-permute-start | bytes 196616 | tf_op jit(solution)/shard_map/ppermute | solution.py:69
  304.8 7.6 %collective-permute-start.42 = (bf16[2,128,128]{2,1,0:T(8,128)(2,1)S(1)}, bf16[2,128,128]{2,1,0:T(8,128)(2,1)S(1)}, u32[]{:S(2)}, u32[]{:S(2)}) collective-permute-start(bf16[2,128,128]{2,1,0:T(8,128)(2,1)S(1)} %get-tuple-element.350), channel_id=1, source_target_pairs={{2,0},{3,1},{4,2},{5,3},{6,4},{7,5},{10,8},{11,9},{12,10},{13,11},... | collective-permute-start | bytes 196616 | tf_op jit(solution)/shard_map/ppermute | solution.py:69
  321.7 7.0 %collective-permute-start.55 = (bf16[2,2,32,768]{3,2,1,0:T(8,128)(2,1)S(1)}, bf16[2,2,32,768]{3,2,1,0:T(8,128)(2,1)S(1)}, u32[]{:S(2)}, u32[]{:S(2)}) collective-permute-start(bf16[2,2,32,768]{3,2,1,0:T(8,128)(2,1)S(1)} %select_bitcast_fusion.4), channel_id=1, source_target_pairs={{0,1},{1,0},{2,3},{3,2},{4,5},{5,4},{6,7},{7,6},{8,9},{9,8},{10,11... | collective-permute-start | bytes 589832 | tf_op jit(solution)/shard_map/ppermute | solution.py:58
  322.9 15.1 %collective-permute-start.45 = (bf16[512,1024]{1,0:T(8,128)(2,1)S(1)}, bf16[512,1024]{1,0:T(8,128)(2,1)S(1)}, u32[]{:S(2)}, u32[]{:S(2)}) collective-permute-start(bf16[512,1024]{1,0:T(8,128)(2,1)S(1)} %slice.584), channel_id=1, source_target_pairs={{0,8},{8,0},{16,24},{24,16},{1,9},{9,1},{17,25},{25,17},{2,10},{10... | collective-permute-start | bytes 3145736 | tf_op jit(solution)/shard_map/ppermute | solution.py:53
  328.8 6.8 %collective-permute-start.56 = (bf16[2,2,32,768]{3,2,0,1:T(8,128)(2,1)S(1)}, bf16[2,2,32,768]{3,2,0,1:T(8,128)(2,1)S(1)}, u32[]{:S(2)}, u32[]{:S(2)}) collective-permute-start(bf16[2,2,32,768]{3,2,0,1:T(8,128)(2,1)S(1)} %select_bitcast_fusion.3), channel_id=1, source_target_pairs={{0,16},{8,24},{16,0},{24,8},{1,17},{9,25},{17,1},{25,9},{2,18},{10... | collective-permute-start | bytes 589832 | tf_op jit(solution)/shard_map/ppermute | solution.py:63
  332.3 8.4 %collective-permute-start.50 = (f32[256,1024]{1,0:T(8,128)S(1)}, f32[256,1024]{1,0:T(8,128)S(1)}, u32[]{:S(2)}, u32[]{:S(2)}) collective-permute-start(f32[256,1024]{1,0:T(8,128)S(1)} %slice.692), channel_id=1, source_target_pairs={{0,8},{8,0},{16,24},{24,16},{1,9},{9,1},{17,25},{25,17},{2,10},{10... | collective-permute-start | bytes 3145736 | tf_op jit(solution)/shard_map/ppermute | solution.py:53
  338.6 9.3 %collective-permute-start.47 = (bf16[128,1024]{1,0:T(8,128)(2,1)S(1)}, bf16[128,1024]{1,0:T(8,128)(2,1)S(1)}, u32[]{:S(2)}, u32[]{:S(2)}) collective-permute-start(bf16[128,1024]{1,0:T(8,128)(2,1)S(1)} %get-tuple-element.296), channel_id=1, source_target_pairs={{0,1},{1,0},{2,3},{3,2},{4,5},{5,4},{6,7},{7,6},{8,9},{9,8},{10,11... | collective-permute-start | bytes 786440 | tf_op jit(solution)/shard_map/ppermute | solution.py:58
  340.1 12.2 %collective-permute-start.46 = (bf16[128,1024]{1,0:T(8,128)(2,1)S(1)}, bf16[128,1024]{1,0:T(8,128)(2,1)S(1)}, u32[]{:S(2)}, u32[]{:S(2)}) collective-permute-start(bf16[128,1024]{1,0:T(8,128)(2,1)S(1)} %get-tuple-element.297), channel_id=1, source_target_pairs={{0,16},{8,24},{16,0},{24,8},{1,17},{9,25},{17,1},{25,9},{2,18},{10... | collective-permute-start | bytes 786440 | tf_op jit(solution)/shard_map/ppermute | solution.py:63
  340.9 13.7 %collective-permute-start.51 = (bf16[128,1024]{1,0:T(8,128)(2,1)S(1)}, bf16[128,1024]{1,0:T(8,128)(2,1)S(1)}, u32[]{:S(2)}, u32[]{:S(2)}) collective-permute-start(bf16[128,1024]{1,0:T(8,128)(2,1)S(1)} %select_convert_fusion), channel_id=1, source_target_pairs={{0,1},{1,0},{2,3},{3,2},{4,5},{5,4},{6,7},{7,6},{8,9},{9,8},{10,11... | collective-permute-start | bytes 786440 | tf_op jit(solution)/shard_map/ppermute | solution.py:58
  353.8 52.7 %collective-permute-start.49 = (bf16[64,1024]{1,0:T(8,128)(2,1)}, bf16[64,1024]{1,0:T(8,128)(2,1)}, u32[]{:S(2)}, u32[]{:S(2)}) collective-permute-start(bf16[64,1024]{1,0:T(8,128)(2,1)} %slice.904), channel_id=1, source_target_pairs={{0,16},{8,24},{16,0},{24,8},{1,17},{9,25},{17,1},{25,9},{2,18},{10... | collective-permute-start | bytes 393224 | tf_op jit(solution)/shard_map/ppermute | solution.py:63
  354.1 52.4 %collective-permute-start.48 = (bf16[64,1024]{1,0:T(8,128)(2,1)}, bf16[64,1024]{1,0:T(8,128)(2,1)}, u32[]{:S(2)}, u32[]{:S(2)}) collective-permute-start(bf16[64,1024]{1,0:T(8,128)(2,1)} %slice.905), channel_id=1, source_target_pairs={{0,1},{1,0},{2,3},{3,2},{4,5},{5,4},{6,7},{7,6},{8,9},{9,8},{10,11... | collective-permute-start | bytes 393224 | tf_op jit(solution)/shard_map/ppermute | solution.py:58
  407.6 8.4 %collective-permute-start.53 = (bf16[2,32,1920]{2,1,0:T(8,128)(2,1)S(1)}, bf16[2,32,1920]{2,1,0:T(8,128)(2,1)S(1)}, u32[]{:S(2)}, u32[]{:S(2)}) collective-permute-start(bf16[2,32,1920]{2,1,0:T(8,128)(2,1)S(1)} %select_bitcast_fusion), channel_id=1, source_target_pairs={{0,1},{1,0},{2,3},{3,2},{4,5},{5,4},{6,7},{7,6},{8,9},{9,8},{10,11... | collective-permute-start | bytes 737288 | tf_op jit(solution)/shard_map/ppermute | solution.py:58
  (104 other events, 830.4 us)
Sparse Core Ops, SparseCore 0:
  26.5 63.1 all-gather.3
  92.4 44.1 all-gather.5
  138.1 37.8 all-gather.7
  236.3 40.0 reduce-scatter.2
  318.1 84.1 reduce-scatter.4
